TPU v7x, 128 devices: a whole 4x4x4 slice. The times are simulated.
128 devices in a mesh: outer: 4 (over x), inner: 32 (over z, y, core).
Axes of the slice: x: 4, y: 4, z: 4, core: 2. Of those that a mesh axis runs over, the one named last changes fastest.
Arguments:
- tokens: bfloat16 [16384, 1024], P(('outer', 'inner')), may hold values from -200 to 200
- out_grad: bfloat16 [16384, 1024], P(('outer', 'inner')), may hold values from -30 to 30
- query_weight: bfloat16 [1024, 1024], replicated, may hold values from -0.1875 to 0.1875
- gain: float32 [1024], replicated, may hold values from 0.1 to 1.9
- shift: float32 [1024], replicated, may hold values from -3 to 3
- first_keys: bfloat16 [2, 512, 256], replicated, may hold values from -0.65 to 0.65
- second_keys: bfloat16 [2, 512, 256], replicated, may hold values from -0.65 to 0.65
- values: bfloat16 [2, 262144, 1024], P(None, ('outer', 'inner')), may hold values from -6 to 6
- pick_shard: int32 [16384, 2, 16], P(('outer', 'inner')), may hold values from 0 to 127, all different within a row; in each aligned block of 256 rows (0 to 255, 256 to 511, ..., all dimensions but the last counted through in order) at most 40 rows name the same one
- pick_low: int32 [16384, 2, 16], P(('outer', 'inner')), may hold values from 0 to 3
- pick_second: int32 [16384, 2, 16], P(('outer', 'inner')), may hold values from 0 to 511
Outputs:
- token_grad: bfloat16 [16384, 1024], P(('outer', 'inner'))
- query_weight_grad: float32 [1024, 1024], P(('outer', 'inner'))
- gain_grad: float32 [1024], replicated
- shift_grad: float32 [1024], replicated
- first_key_grad: float32 [2, 512, 256], replicated
- second_key_grad: float32 [2, 512, 256], replicated
- value_grad: bfloat16 [2, 262144, 1024], P(None, ('outer', 'inner'))
Inputs may be any that keep to these rules, and one draw needn't show every extreme that they name: `pick_shard`: the 16 picks of one token and head name 16 different shards; among the picks of one device's tokens no shard is named more than 40 times, and in some device's tokens one is named exactly 40 times.
All inputs are finite; a program needn't handle non-finite values.
Results may differ from a plain program's by a relative error of at most 0.01.
The roundings to bfloat16 on the way count: a program that leaves them out, or rounds other values in their place, can miss the bound.
Values may be sent and summed in bfloat16 or wider, within the bound.
No kernel may reach another device: no remote copies, remote signals or barrier semaphores. Data moves between devices by JAX's collectives and lax.ppermute only.
A program may use at most 128 MiB of HBM per device.

v0:
```python
import jax
import jax.numpy as jnp
from jax import lax
from jax.sharding import PartitionSpec as P

epsilon = 1e-05


def place_slots(target, is_live, groups, capacity):
    matches = jnp.logical_and(
        target[:, :, None] == jnp.arange(groups, dtype=jnp.int32), is_live[:, :, None]
    )
    row_hits = jnp.sum(matches.astype(jnp.int32), axis=1)
    earlier = jnp.cumsum(row_hits, axis=0) - row_hits
    position = jnp.take_along_axis(earlier, jnp.clip(target, 0, groups - 1), axis=1)
    return jnp.where(is_live, target * capacity + position, groups * capacity).reshape(-1)


def slot_owners(slot_ids, total_slots, pick_count):
    vacant = jnp.full((total_slots,), pick_count, jnp.int32)
    return vacant.at[slot_ids].set(jnp.arange(pick_count, dtype=jnp.int32), mode="drop")


def build_rows(grad_rows, weight_flat, local_flat, owner_of_slot, per_token):
    token_of = owner_of_slot // per_token
    picked = jnp.take(grad_rows, token_of, axis=0, mode="fill", fill_value=0)
    pick_weight = jnp.take(weight_flat, owner_of_slot, mode="fill", fill_value=0.0)
    row_index = jnp.take(local_flat, owner_of_slot, mode="fill", fill_value=0)
    message = (pick_weight[:, None] * picked.astype(jnp.float32)).astype(jnp.bfloat16)
    return (message, row_index)


def serve_rows(message, row_index, values):
    value_table = values.reshape(-1, values.shape[-1])
    fetched = jnp.take(value_table, row_index, axis=0)
    product = jnp.einsum("nd,nd->n", message, fetched, preferred_element_type=jnp.float32)
    summed = (
        jnp.zeros(value_table.shape, jnp.float32).at[row_index].add(message.astype(jnp.float32))
    )
    return (product, summed.astype(jnp.bfloat16).reshape(values.shape))


def per_device(
    tokens,
    out_grad,
    query_weight,
    gain,
    shift,
    first_keys,
    second_keys,
    values,
    pick_shard,
    pick_low,
    pick_second,
):
    n_outer = lax.axis_size("outer")
    n_inner = lax.axis_size("inner")
    devices = n_outer * n_inner
    tok_rows = tokens.shape[0]
    head_count, rows_dev, model_width = values.shape
    subkey_count = first_keys.shape[1]
    half_width = first_keys.shape[2]
    top_count = pick_shard.shape[2]
    all_tokens = tok_rows * devices
    raw_query = jnp.dot(tokens, query_weight, preferred_element_type=jnp.float32)
    centre = lax.psum(jnp.sum(raw_query, axis=0), ("outer", "inner")) / all_tokens
    shifted = raw_query - centre
    spread = lax.psum(jnp.sum(shifted * shifted, axis=0), ("outer", "inner")) / all_tokens
    inverse = 1.0 / jnp.sqrt(spread + epsilon)
    normed = shifted * inverse
    query = (
        (normed * gain + shift).astype(jnp.bfloat16).reshape(tok_rows, head_count, 2 * half_width)
    )
    first_index = pick_shard * (subkey_count // devices) + pick_low
    score_parts = []
    for head_id in range(head_count):
        near_full = jnp.dot(
            query[:, head_id, :half_width],
            first_keys[head_id].T,
            preferred_element_type=jnp.float32,
        )
        far_full = jnp.dot(
            query[:, head_id, half_width:],
            second_keys[head_id].T,
            preferred_element_type=jnp.float32,
        )
        score_parts.append(
            jnp.take_along_axis(near_full, first_index[:, head_id], axis=1)
            + jnp.take_along_axis(far_full, pick_second[:, head_id], axis=1)
        )
    weight = jax.nn.softmax(jnp.stack(score_parts, axis=1), axis=-1)
    head_base = (jnp.arange(head_count, dtype=jnp.int32) * rows_dev)[None, :, None]
    local_row = pick_low * subkey_count + pick_second + head_base
    pick_count = tok_rows * head_count * top_count
    capacity = min(5 * pick_count // (4 * devices), tok_rows * head_count)
    all_live = jnp.ones((tok_rows * head_count, top_count), jnp.bool_)
    slot_ids = place_slots(pick_shard.reshape(-1, top_count), all_live, devices, capacity)
    owner_of_slot = slot_owners(slot_ids, devices * capacity, pick_count)
    message, row_index = build_rows(
        out_grad, weight.reshape(-1), local_row.reshape(-1), owner_of_slot, head_count * top_count
    )
    arrived, arrived_index = (
        lax.all_to_all(
            message.reshape(devices, capacity, model_width),
            ("outer", "inner"),
            split_axis=0,
            concat_axis=0,
            tiled=True,
        ),
        lax.all_to_all(
            row_index.reshape(devices, capacity),
            ("outer", "inner"),
            split_axis=0,
            concat_axis=0,
            tiled=True,
        ),
    )
    product, value_grad = serve_rows(
        arrived.reshape(-1, model_width), arrived_index.reshape(-1), values
    )
    returned = lax.all_to_all(
        product.reshape(devices, capacity),
        ("outer", "inner"),
        split_axis=0,
        concat_axis=0,
        tiled=True,
    )
    pick_product = jnp.take(returned.reshape(-1), slot_ids, mode="fill", fill_value=0.0).reshape(
        tok_rows, head_count, top_count
    )
    score_grad = pick_product - weight * jnp.sum(pick_product, axis=-1, keepdims=True)
    subkey_ids = jnp.arange(subkey_count, dtype=jnp.int32)
    query_parts = []
    first_parts = []
    second_parts = []
    for head_id in range(head_count):
        near_dense = jnp.sum(
            jnp.where(
                first_index[:, head_id, :, None] == subkey_ids, score_grad[:, head_id, :, None], 0.0
            ),
            axis=1,
        )
        far_dense = jnp.sum(
            jnp.where(
                pick_second[:, head_id, :, None] == subkey_ids, score_grad[:, head_id, :, None], 0.0
            ),
            axis=1,
        )
        near_query = query[:, head_id, :half_width].astype(jnp.float32)
        far_query = query[:, head_id, half_width:].astype(jnp.float32)
        query_parts.append(
            jnp.dot(
                near_dense, first_keys[head_id].astype(jnp.float32), precision=lax.Precision.HIGHEST
            )
        )
        query_parts.append(
            jnp.dot(
                far_dense, second_keys[head_id].astype(jnp.float32), precision=lax.Precision.HIGHEST
            )
        )
        first_parts.append(jnp.dot(near_dense.T, near_query, precision=lax.Precision.HIGHEST))
        second_parts.append(jnp.dot(far_dense.T, far_query, precision=lax.Precision.HIGHEST))
    query_grad = jnp.concatenate(query_parts, axis=1)
    first_key_grad, second_key_grad, shift_grad, gain_grad = lax.psum(
        (
            jnp.stack(first_parts),
            jnp.stack(second_parts),
            jnp.sum(query_grad, axis=0),
            jnp.sum(query_grad * normed, axis=0),
        ),
        ("outer", "inner"),
    )
    raw_grad = (
        gain * inverse * (query_grad - shift_grad / all_tokens - normed * gain_grad / all_tokens)
    ).astype(jnp.bfloat16)
    token_grad = jnp.einsum(
        "tk,dk->td", raw_grad, query_weight, preferred_element_type=jnp.float32
    ).astype(jnp.bfloat16)
    query_weight_grad = lax.psum_scatter(
        jnp.einsum("tk,td->kd", raw_grad, tokens, preferred_element_type=jnp.float32),
        ("outer", "inner"),
        scatter_dimension=0,
        tiled=True,
    )
    return (
        token_grad,
        query_weight_grad,
        gain_grad,
        shift_grad,
        first_key_grad,
        second_key_grad,
        value_grad,
    )


def solution(mesh):
    in_specs = (
        P(("outer", "inner"), None),
        P(("outer", "inner"), None),
        P(),
        P(),
        P(),
        P(),
        P(),
        P(None, ("outer", "inner"), None),
        P(("outer", "inner"), None, None),
        P(("outer", "inner"), None, None),
        P(("outer", "inner"), None, None),
    )
    out_specs = (
        P(("outer", "inner"), None),
        P(("outer", "inner"), None),
        P(),
        P(),
        P(),
        P(),
        P(None, ("outer", "inner"), None),
    )
    return jax.shard_map(
        per_device, mesh=mesh, in_specs=in_specs, out_specs=out_specs, check_vma=False
    )
```

profile of v0, /device:TPU:1, one launch (start us, length us, event | category | flops | bytes accessed | tf_op | source)
XLA Modules:
  0.0 1373.6 jit_solution(9482046198031445677)
XLA Ops:
  10.2 68.7 %psum.42 = f32[1024]{0:T(1024)S(1)} all-reduce(f32[1024]{0:T(1024)S(1)} %get-tuple-element.46), channel_id=1, replica_groups=mesh['outer'=4,'inner'=32] {'outer','inner'}, use_global_device_ids=true, to_apply=%region_1.0 | all-reduce | flops 1024 | bytes 8192 | tf_op jit(solution)/shard_map/psum | solution.py:66
  79.0 62.6 %psum.43 = f32[1024]{0:T(1024)S(1)} all-reduce(f32[1024]{0:T(1024)S(1)} %multiply_reduce_fusion.1), channel_id=1, replica_groups=mesh['outer'=4,'inner'=32] {'outer','inner'}, use_global_device_ids=true, to_apply=%region_3.0 | all-reduce | flops 1024 | bytes 8192 | tf_op jit(solution)/shard_map/psum | solution.py:68
  147.1 16.6 %gather_fusion.7 = f32[2048]{0:T(1024)S(1)} fusion(f32[128,512]{1,0:T(8,128)S(1)} %fusion.16, s32[2048]{0:T(1024)S(1)} %reshape.416), kind=kCustom, calls=%fused_computation.1.clone | custom fusion | bytes 32768 | tf_op jit(solution)/shard_map/jit(take_along_axis)/gather | solution.py:89
  167.3 16.6 %gather_fusion.6 = f32[2048]{0:T(1024)S(1)} fusion(f32[128,512]{1,0:T(8,128)S(1)} %fusion.20, s32[2048]{0:T(1024)S(1)} %reshape.411), kind=kCustom, calls=%fused_computation.clone | custom fusion | bytes 32768 | tf_op jit(solution)/shard_map/jit(take_along_axis)/gather | solution.py:88
  185.2 16.6 %gather_fusion.9 = f32[2048]{0:T(1024)S(1)} fusion(f32[128,512]{1,0:T(8,128)S(1)} %fusion.8, s32[2048]{0:T(1024)S(1)} %reshape.426), kind=kCustom, calls=%fused_computation.3.clone | custom fusion | bytes 32768 | tf_op jit(solution)/shard_map/jit(take_along_axis)/gather | solution.py:89
  202.5 16.6 %gather_fusion.8 = f32[2048]{0:T(1024)S(1)} fusion(f32[128,512]{1,0:T(8,128)S(1)} %fusion.12, s32[2048]{0:T(1024)S(1)} %reshape.421), kind=kCustom, calls=%fused_computation.2.clone | custom fusion | bytes 32768 | tf_op jit(solution)/shard_map/jit(take_along_axis)/gather | solution.py:88
  222.4 25.6 %gather_fusion.5 = s32[4096]{0:T(1024)S(1)} fusion(s32[256,128]{1,0:T(8,128)S(1)} %bitcast_subtract_fusion, s32[4096]{0:T(1024)S(1)} %reshape.363), kind=kCustom, calls=%fused_computation.9 | custom fusion | bytes 65536 | tf_op jit(solution)/shard_map/jit(take_along_axis)/gather | solution.py:15
  248.1 15.5 %scatter_custom_fusion = s32[5120]{0:T(1024)S(1)} fusion(s32[4096]{0:T(1024)S(1)} %bitcast.145, s32[4096]{0:T(1024)S(1)} %iota.16, s32[]{:T(128)} %constant.102.clone.1), kind=kCustom, calls=%fused_computation.122 | custom fusion | bytes 20484 | tf_op jit(solution)/shard_map/scatter | solution.py:21
  263.7 28.7 %gather_fusion = f32[5120]{0:T(1024)S(1)} fusion(f32[4096]{0:T(1024)S(1)} %div.45, s32[5120]{0:T(1024)S(1)} %get-tuple-element.33), kind=kCustom, calls=%fused_computation.4 | custom fusion | bytes 61440 | tf_op jit(solution)/shard_map/jit(_take)/gather | solution.py:27
  292.7 28.7 %gather_fusion.2 = s32[5120]{0:T(1024)S(1)} fusion(s32[4096]{0:T(1024)S(1)} %reshape.290, s32[5120]{0:T(1024)S(1)} %get-tuple-element.33), kind=kCustom, calls=%fused_computation.6 | custom fusion | bytes 61440 | tf_op jit(solution)/shard_map/jit(_take)/gather | solution.py:28
  327.6 22.6 %gather_fusion.1 = bf16[5120,1024]{1,0:T(8,128)(2,1)} fusion(bf16[128,1024]{1,0:T(8,128)(2,1)S(1)} %copy-done.1, s32[5120]{0:T(1024)S(1)} %get-tuple-element.32), kind=kCustom, calls=%fused_computation.5 | custom fusion | bytes 20992000 | tf_op jit(solution)/shard_map/jit(_take)/gather | solution.py:26
  350.2 11.0 multiply_convert_fusion
  361.2 10.2 all-to-all-start
  373.0 30.3 %gather_fusion.3 = bf16[5120,1024]{1,0:T(8,128)(2,1)} fusion(bf16[4096,1024]{1,0:T(8,128)(2,1)} %bitcast.131, s32[5120]{0:T(1024)S(1)} %broadcast_clamp_fusion.2), kind=kCustom, calls=%fused_computation.7 | custom fusion | bytes 20992000 | tf_op jit(solution)/shard_map/jit(_take)/gather | solution.py:35
  403.3 103.2 %all-to-all-done = bf16[128,40,1024]{2,1,0:T(8,128)(2,1)} async-done(((bf16[128,40,1024]{2,1,0:T(8,128)(2,1)}), bf16[128,40,1024]{2,1,0:T(8,128)(2,1)}, u32[]{:S(2)}, u32[]{:S(2)}) %all-to-all-start) | async-done | bytes 10485792 | tf_op jit(solution)/shard_map/all_to_all | solution.py:103
  506.5 9.7 fusion.3
  516.9 8.9 all-to-all-start.2
  529.7 5.6 all-to-all-done.2
  536.8 23.0 %gather_fusion.4 = f32[4096]{0:T(1024)S(1)} fusion(f32[5120]{0:T(1024)S(1)} %reshape.294, s32[4096]{0:T(1024)S(1)} %broadcast_clamp_fusion.3), kind=kCustom, calls=%fused_computation.8 | custom fusion | bytes 49152 | tf_op jit(solution)/shard_map/jit(_take)/gather | solution.py:128
  577.8 64.2 %all-reduce = (f32[1024]{0:T(1024)S(1)}, f32[1024]{0:T(1024)S(1)}) all-reduce(f32[1024]{0:T(1024)S(1)} %get-tuple-element.9, f32[1024]{0:T(1024)S(1)} %get-tuple-element.8), channel_id=1, replica_groups=mesh['outer'=4,'inner'=32] {'outer','inner'}, use_global_device_ids=true, to_apply=%region_18.20 | all-reduce | flops 2048 | bytes 16384 | tf_op jit(solution)/shard_map/psum | solution.py:164
  645.8 50.0 %scatter_custom_fusion.1 = f32[4096,1024]{1,0:T(8,128)} fusion(s32[5120]{0:T(1024)} %bitcast.144, bf16[5120,1024]{1,0:T(8,128)(2,1)} %bitcast.28, f32[]{:T(128)} %constant.85.clone.1), kind=kCustom, calls=%fused_computation.13 | custom fusion | flops 10485760 | bytes 27263488 | tf_op jit(solution)/shard_map/scatter-add | solution.py:38
  695.8 9.3 convert_element_type.41
  706.7 16.7 %all-reduce.4.cloned.1.call-done = (f32[2,512,256]{2,1,0:T(8,128)}, f32[2,512,256]{2,1,0:T(8,128)}) async-done(((f32[2,512,256]{2,1,0:T(8,128)}, f32[2,512,256]{2,1,0:T(8,128)}), (f32[2,512,256]{2,1,0:T(8,128)}, f32[2,512,256]{2,1,0:T(8,128)})) %all-reduce.4.cloned.1.call-update) | async-done | bytes 2097168 | tf_op jit(solution)/shard_map/psum | solution.py:164
  723.4 638.9 %reduce-scatter.2.cloned.1.call-done = f32[8,1024]{1,0:T(8,128)} async-done(((f32[1024,1024]{1,0:T(8,128)}), f32[8,1024]{1,0:T(8,128)}) %reduce-scatter.2.cloned.1.call-update) | async-done | bytes 32784 | tf_op jit(solution)/shard_map/reduce_scatter | solution.py:179
  (177 shorter events, 58.7 us)
Async XLA Ops:
  7.2 139.4 %copy-start.16 = (s32[128,2,16]{0,2,1:T(8,128)S(1)}, s32[128,2,16]{0,2,1:T(8,128)}, u32[]{:S(2)}) copy-start(s32[128,2,16]{0,2,1:T(8,128)} %param.23) | copy-start | bytes 49156
  7.2 139.7 %copy-start.4 = (bf16[2,512,256]{2,1,0:T(8,128)(2,1)S(1)}, bf16[2,512,256]{2,1,0:T(8,128)(2,1)}, u32[]{:S(2)}) copy-start(bf16[2,512,256]{2,1,0:T(8,128)(2,1)} %param.19) | copy-start | bytes 1572868
  10.2 136.5 %copy-start.2 = (f32[128,1024]{1,0:T(8,128)}, f32[128,1024]{1,0:T(8,128)S(1)}, u32[]{:S(2)}) copy-start(f32[128,1024]{1,0:T(8,128)S(1)} %get-tuple-element.47) | copy-start | bytes 1572868
  78.9 65.5 %copy-start.19 = (f32[1024]{0:T(1024)}, f32[1024]{0:T(1024)S(1)}, u32[]{:S(2)}) copy-start(f32[1024]{0:T(1024)S(1)} %broadcast_multiply_fusion.2) | copy-start | bytes 12292
  146.6 17.1 %copy-start.12 = (bf16[128,1,256]{2,1,0:T(2,128)(2,1)}, bf16[128,1,256]{2,1,0:T(2,128)(2,1)S(1)}, u32[]{:S(2)}) copy-start(bf16[128,1,256]{2,1,0:T(2,128)(2,1)S(1)} %get-tuple-element.24) | copy-start | bytes 196612
  147.1 17.5 %copy-start.24 = (s32[128,2,16]{0,2,1:T(8,128)S(1)}, s32[128,2,16]{0,2,1:T(8,128)}, u32[]{:S(2)}) copy-start(s32[128,2,16]{0,2,1:T(8,128)} %param.21) | copy-start | bytes 49156
  147.1 17.6 %copy-start.30 = (s32[128,2,16]{0,2,1:T(8,128)S(1)}, s32[128,2,16]{0,2,1:T(8,128)}, u32[]{:S(2)}) copy-start(s32[128,2,16]{0,2,1:T(8,128)} %param.22) | copy-start | bytes 49156
  147.1 17.6 %copy-start.33 = (s32[2]{0:T(128)S(1)}, s32[2]{0:T(128)}, u32[]{:S(2)}) copy-start(s32[2]{0:T(128)} %iota_multiply_fusion) | copy-start | bytes 28
  147.1 19.0 %copy-start.10 = (bf16[128,1,256]{2,1,0:T(2,128)(2,1)S(1)}, bf16[128,1,256]{2,1,0:T(2,128)(2,1)}, u32[]{:S(2)}) copy-start(bf16[128,1,256]{2,1,0:T(2,128)(2,1)} %get-tuple-element.22) | copy-start | bytes 196612
  165.4 18.6 %copy-start.17 = (s32[128,2,16]{0,2,1:T(8,128)}, s32[128,2,16]{0,2,1:T(8,128)S(1)}, u32[]{:S(2)}) copy-start(s32[128,2,16]{0,2,1:T(8,128)S(1)} %get-tuple-element.39) | copy-start | bytes 49156
  167.3 17.4 %copy-start.14 = (bf16[128,1,256]{2,1,0:T(2,128)(2,1)S(1)}, bf16[128,1,256]{2,1,0:T(2,128)(2,1)}, u32[]{:S(2)}) copy-start(bf16[128,1,256]{2,1,0:T(2,128)(2,1)} %get-tuple-element.25) | copy-start | bytes 196612
  185.2 17.1 %copy-start.28 = (s32[128,16,1]{0,1,2:T(8,128)S(1)}, s32[128,16,1]{0,1,2:T(8,128)}, u32[]{:S(2)}) copy-start(s32[128,16,1]{0,1,2:T(8,128)} %get-tuple-element.41) | copy-start | bytes 24580
  263.6 28.7 %copy-start.25 = (s32[128,2,16]{0,2,1:T(8,128)S(1)}, s32[128,2,16]{0,2,1:T(8,128)}, u32[]{:S(2)}) copy-start(s32[128,2,16]{0,2,1:T(8,128)} %get-tuple-element.38) | copy-start | bytes 49156
  322.1 39.1 %all-to-all-start.1 = ((s32[128,1,40]{2,1,0:T(1,128)}), s32[128,1,40]{2,1,0:T(1,128)S(1)}, u32[]{:S(2)}, u32[]{:S(2)}) async-start(s32[128,1,40]{2,1,0:T(1,128)} %bitcast.29), calls=%async_computation.1 | async-start | bytes 131072 | tf_op jit(solution)/shard_map/all_to_all | solution.py:110
  361.2 145.3 %all-to-all-start = ((bf16[128,40,1024]{2,1,0:T(8,128)(2,1)}), bf16[128,40,1024]{2,1,0:T(8,128)(2,1)}, u32[]{:S(2)}, u32[]{:S(2)}) async-start(bf16[128,40,1024]{2,1,0:T(8,128)(2,1)} %multiply_convert_fusion), calls=%async_computation | async-start | bytes 20971520 | tf_op jit(solution)/shard_map/all_to_all | solution.py:103
  373.0 30.3 %copy-start.21 = (s32[5120,1]{0,1:T(1,128)}, s32[5120,1]{0,1:T(1,128)S(1)}, u32[]{:S(2)}) copy-start(s32[5120,1]{0,1:T(1,128)S(1)} %compare_select_fusion.3) | copy-start | bytes 61444
  516.9 18.4 %all-to-all-start.2 = ((f32[128,1,40]{2,1,0:T(1,128)}), f32[128,1,40]{2,1,0:T(1,128)S(1)}, u32[]{:S(2)}, u32[]{:S(2)}) async-start(f32[128,1,40]{2,1,0:T(1,128)} %bitcast.32), calls=%async_computation.2 | async-start | bytes 131072 | tf_op jit(solution)/shard_map/all_to_all | solution.py:121
  525.9 197.5 %all-reduce.4.cloned.1.call-start = ((), (), s32[]{:S(2)}) async-start(), calls=%async_computation.5 | async-start | bytes 4194304 | tf_op jit(solution)/shard_map/psum | solution.py:164
  536.8 29.0 %copy-start.7 = (bf16[2,512,256]{2,1,0:T(8,128)(2,1)S(1)}, bf16[2,512,256]{2,1,0:T(8,128)(2,1)}, u32[]{:S(2)}) copy-start(bf16[2,512,256]{2,1,0:T(8,128)(2,1)} %param.18) | copy-start | bytes 1572868
  536.8 30.6 %copy-start.5 = (bf16[2,512,256]{2,1,0:T(8,128)(2,1)S(1)}, bf16[2,512,256]{2,1,0:T(8,128)(2,1)}, u32[]{:S(2)}) copy-start(bf16[2,512,256]{2,1,0:T(8,128)(2,1)} %param.19) | copy-start | bytes 1572868
  573.0 69.0 %copy-start.29 = (f32[1024]{0:T(1024)S(1)}, f32[1024]{0:T(1024)}, u32[]{:S(2)}) copy-start(f32[1024]{0:T(1024)} %get-tuple-element.44) | copy-start | bytes 12292
  576.3 786.0 %reduce-scatter.2.cloned.1.call-start = ((), (), s32[]{:S(2)}) async-start(), calls=%async_computation.4 | async-start | bytes 4227072 | tf_op jit(solution)/shard_map/reduce_scatter | solution.py:179
  642.0 53.8 %copy-start.31 = (f32[1024]{0:T(1024)}, f32[1024]{0:T(1024)S(1)}, u32[]{:S(2)}) copy-start(f32[1024]{0:T(1024)S(1)} %get-tuple-element.52) | copy-start | bytes 12292
  642.0 53.8 %copy-start.32 = (f32[1024]{0:T(1024)}, f32[1024]{0:T(1024)S(1)}, u32[]{:S(2)}) copy-start(f32[1024]{0:T(1024)S(1)} %get-tuple-element.53) | copy-start | bytes 12292
  (15 other events, 155.4 us)
Sparse Core Ops, SparseCore 0:
  576.4 146.8 all-reduce.3
  726.3 635.9 reduce-scatter.1
where the time goes:
time: 1380 us; the launch traced here: 1370 us
  waiting for transfers between devices  764 us (55%)
  local copies, waits for them, and re-layouts  260 us (19%)
  blocking collectives  196 us (14%)
  other arithmetic  98.5 us (7%)
  starting transfers between devices  24.5 us (2%)
  matrix products  15.3 us (1%)
  between operations  14.8 us (1%)
    reduce_scatter x1, waiting for transfers between devices, per_device(): lax.psum_scatter(jnp.einsum('tk,td->kd', raw_grad, tokens, preferred_elem...  639 us
    all_to_all x1, waiting for transfers between devices, per_device(): lax.all_to_all(message.reshape(devices, capacity, model_width), ('outer',...  103 us
    psum x1, blocking collectives, per_device(): lax.psum(jnp.sum(raw_query, axis=0), ('outer', 'inner')) / all_tokens  68.7 us
    psum x1, blocking collectives, per_device(): lax.psum((jnp.stack(first_parts), jnp.stack(second_parts), jnp.sum(query_...  64.2 us
    psum x1, blocking collectives, per_device(): lax.psum(jnp.sum(shifted * shifted, axis=0), ('outer', 'inner'))  62.6 us
    scatter-add x1, other arithmetic, serve_rows(): jnp.zeros(value_table.shape, jnp.float32).at[row_index]  50 us
    gather x10, local copies, waits for them, and re-layouts, per_device(): jnp.take_along_axis(far_full, pick_second[:, head_id], axis=1)  34.5 us
    gather x10, local copies, waits for them, and re-layouts, per_device(): jnp.take_along_axis(near_full, first_index[:, head_id], axis=1)  34.5 us
  transfers between devices with their start and end apart: 5, of which 4 were waited for; matrix products, arithmetic and copies ran while one was open for 10% of the time, Pallas kernels for 0%

commit v1 on v0

v1 whole, which is shorter than its diff:
```python
import functools
import jax
import jax.numpy as jnp
from jax import lax
from jax.experimental import pallas as pl
from jax.experimental.pallas import tpu as pltpu
from jax.sharding import Mesh, PartitionSpec as P

epsilon = 1e-05
F32, BF16, I32 = jnp.float32, jnp.bfloat16, jnp.int32
ALL = ("x", "z", "y", "c")
CHIPS = ("x", "z", "y")
CAP = 40
GROUP = 8
LANES = 128
NT = (((1,), (1,)), ((), ()))
TN = (((0,), (0,)), ((), ()))


def iota(shape, axis):
    return lax.broadcasted_iota(I32, shape, axis)


def slot_table(pos, payload):
    lines = []
    for j in range(CAP):
        found = sum(jnp.where(p == j, v, jnp.zeros_like(v)) for p, v in zip(pos, payload))
        lines.append(jnp.sum(found, axis=0, keepdims=True))
    lines.append(jnp.zeros((LANES - CAP, LANES), payload[0].dtype))
    return lines


def slots_kernel(heads, top, shard_ref, code_ref, pos_ref, dense_ref, slot_ref):
    n = shard_ref.shape[0]
    lane = iota((n, LANES), 1)
    row = iota((n, LANES), 0)
    below = (iota((n, n), 1) < iota((n, n), 0)).astype(BF16)
    before = jnp.zeros((1, LANES), F32)
    pos, packed = [], []
    for h in range(heads):
        code = jnp.full((n, LANES), -1, I32)
        for k in range(top):
            at = h * top + k
            code = jnp.where(shard_ref[:, at : at + 1] == lane, code_ref[:, at : at + 1], code)
        hit = code >= 0
        ones = jnp.where(hit, 1.0, 0.0)
        place = jnp.dot(below, ones.astype(BF16), preferred_element_type=F32) + before
        before = before + jnp.sum(ones, axis=0, keepdims=True)
        place = jnp.where(hit, place, -1.0)
        pos.append(place)
        packed.append(((h * 2048 + code) * n + row).astype(F32))
        pos_ref[h * n : (h + 1) * n, :] = place
        dense_ref[h * n : (h + 1) * n, :] = code
    lines = slot_table(pos, packed)
    table = jnp.concatenate(lines[:CAP] + [before, lines[CAP][1:]], axis=0)
    slot_ref[...] = table.T.astype(I32)


def score_kernel(
    heads, half, raw_ref, stat_ref, gain_ref, shift_ref, first_ref, second_ref, pos_ref, dense_ref,
    query_ref, normed_ref, weight_ref, slot_ref,
):
    n = raw_ref.shape[0]
    normed = (raw_ref[...] - stat_ref[0:1, :]) * stat_ref[1:2, :]
    normed_ref[...] = normed
    query = (normed * gain_ref[...] + shift_ref[...]).astype(BF16)
    query_ref[...] = query
    pos, weights = [], []
    for h in range(heads):
        code = dense_ref[h * n : (h + 1) * n, :]
        hit = code >= 0
        low = code >> 9
        second = jnp.maximum(code, 0) & 511
        base = h * 2 * half
        near = query[:, base : base + half]
        far = query[:, base + half : base + 2 * half]
        score = jnp.zeros((n, LANES), F32)
        for part in range(4):
            dense = lax.dot_general(
                near, first_ref[h, part * LANES : (part + 1) * LANES, :], NT, preferred_element_type=F32
            )
            score = jnp.where(low == part, dense, score)
        found = jnp.zeros((n, LANES), F32)
        for part in range(4):
            dense = lax.dot_general(
                far, second_ref[h, part * LANES : (part + 1) * LANES, :], NT, preferred_element_type=F32
            )
            taken = jnp.take_along_axis(dense, second & (LANES - 1), axis=1)
            found = jnp.where((second >> 7) == part, taken, found)
        score = jnp.where(hit, score + found, -jnp.inf)
        most = jnp.max(score, axis=1, keepdims=True)
        power = jnp.where(hit, jnp.exp(score - most), 0.0)
        weight = power / jnp.sum(power, axis=1, keepdims=True)
        weight_ref[h * n : (h + 1) * n, :] = weight
        pos.append(pos_ref[h * n : (h + 1) * n, :])
        weights.append(weight)
    slot_ref[...] = jnp.concatenate(slot_table(pos, weights), axis=0).T


def serve_kernel(tokens, rows, index_ref, weight_ref, grad_ref, value_ref, out_ref, product_ref, total, held):
    step = pl.program_id(0)

    @pl.when(step == 0)
    def _():
        def clear(i, carry):
            at = pl.multiple_of(i * 256, 256)
            total[pl.ds(at, 256), :] = jnp.zeros((256, LANES), F32)
            return carry

        lax.fori_loop(0, rows * 8 // 256, clear, 0)

    eye = iota((CAP, LANES), 0) == iota((CAP, LANES), 1)

    def one_sender(g, carry):
        sender = step * GROUP + g
        count = index_ref[sender, CAP]

        def eight(b, inner):
            for u in range(8):
                j = b * 8 + u
                packed = index_ref[sender, j]
                weight = weight_ref[sender, j]
                row = packed // tokens
                token = packed % tokens
                grad = grad_ref[g * tokens + token].astype(F32)
                message = (grad * weight).astype(BF16).astype(F32)
                value = value_ref[row].astype(F32)
                held[pl.ds(pl.multiple_of(j * 8, 8), 8), :] = message * value
                at = pl.ds(pl.multiple_of(row * 8, 8), 8)
                total[at, :] += message
            return inner

        lax.fori_loop(0, (count + 7) // 8, eight, 0)
        part = held[pl.ds(0, CAP, stride=8), :]
        for c in range(1, 8):
            part = part + held[pl.ds(c, CAP, stride=8), :]
        summed = jnp.sum(part, axis=1, keepdims=True)
        line = jnp.sum(jnp.where(eye, summed, 0.0), axis=0, keepdims=True)
        product_ref[pl.ds(sender, 1), :] = line
        return carry

    lax.fori_loop(0, GROUP, one_sender, 0)

    @pl.when(step == pl.num_programs(0) - 1)
    def _():
        def emit(i, carry):
            at = pl.multiple_of(i * 16, 16)
            for c in range(8):
                out_ref[pl.ds(at, 16), c * LANES : (c + 1) * LANES] = total[
                    pl.ds(at * 8 + c, 16, stride=8), :
                ].astype(BF16)
            return carry

        lax.fori_loop(0, rows // 16, emit, 0)


def split(value):
    high = value.astype(BF16)
    return high, (value - high.astype(F32)).astype(BF16)


def back_kernel(
    heads, top, half, back_ref, shard_ref, second_ids_ref, pos_ref, dense_ref, weight_ref, query_ref,
    normed_ref, first_ref, second_ref, grad_ref, key_ref, sum_ref,
):
    n = query_ref.shape[0]
    table = back_ref[...].T
    wide = iota((n, 4 * LANES), 1)
    for h in range(heads):
        pos = pos_ref[h * n : (h + 1) * n, :]
        product = jnp.zeros((n, LANES), F32)
        for j in range(CAP):
            product = jnp.where(pos == j, table[j : j + 1, :], product)
        weight = weight_ref[h * n : (h + 1) * n, :]
        score = product - weight * jnp.sum(product, axis=1, keepdims=True)
        code = dense_ref[h * n : (h + 1) * n, :]
        low = code >> 9
        near_dense = jnp.concatenate([jnp.where(low == part, score, 0.0) for part in range(4)], axis=1)
        shards = jnp.concatenate(
            [shard_ref[:, h * top : (h + 1) * top], jnp.zeros((n, LANES - top), I32)], axis=1
        )
        picked = jnp.take_along_axis(score, shards, axis=1)
        far_dense = jnp.zeros((n, 4 * LANES), F32)
        for k in range(top):
            at = h * top + k
            far_dense = far_dense + jnp.where(
                second_ids_ref[:, at : at + 1] == wide, picked[:, k : k + 1], 0.0
            )
        base = h * 2 * half
        for side, dense, keys in ((0, near_dense, first_ref), (1, far_dense, second_ref)):
            cols = slice(base + side * half, base + (side + 1) * half)
            high, rest = split(dense)
            table_h = keys[h]
            grad = jnp.dot(high, table_h, preferred_element_type=F32) + jnp.dot(
                rest, table_h, preferred_element_type=F32
            )
            grad_ref[:, cols] = grad
            sum_ref[0:1, cols] = jnp.sum(grad, axis=0, keepdims=True)
            sum_ref[1:2, cols] = jnp.sum(grad * normed_ref[:, cols], axis=0, keepdims=True)
            query = query_ref[:, cols]
            key_ref[side, h] = lax.dot_general(high, query, TN, preferred_element_type=F32) + lax.dot_general(
                rest, query, TN, preferred_element_type=F32
            )


def call(kernel, out_shape, limit=40, **more):
    return pl.pallas_call(
        kernel,
        out_shape=out_shape,
        compiler_params=pltpu.CompilerParams(vmem_limit_bytes=limit << 20),
        **more,
    )


def shape(dims, dtype):
    return jax.ShapeDtypeStruct(dims, dtype)


def swap_core(value):
    return lax.ppermute(value, "c", [(0, 1), (1, 0)])


def everyone(value, axis):
    size = lax.axis_size(axis)
    wide = jnp.broadcast_to(value[None], (size,) + value.shape)
    return lax.all_to_all(wide, axis, split_axis=0, concat_axis=0, tiled=True)


def all_sum(value):
    value = value + swap_core(value)
    for axis in ("y", "z", "x"):
        value = jnp.sum(everyone(value, axis), axis=0)
    return value


def all_moments(mean, spread, count):
    for axis in ("c", "y", "z", "x"):
        both = jnp.stack([mean, spread])
        parts = jnp.stack([both, swap_core(both)]) if axis == "c" else everyone(both, axis)
        mean = jnp.mean(parts[:, 0], axis=0)
        spread = jnp.sum(parts[:, 1] + count * jnp.square(parts[:, 0] - mean), axis=0)
        count = count * parts.shape[0]
    return mean, spread / count


def pair_halves(blocks):
    core = lax.axis_index("c")
    own = lax.dynamic_index_in_dim(blocks, core, 1, keepdims=False)
    other = lax.dynamic_index_in_dim(blocks, 1 - core, 1, keepdims=False)
    return own + swap_core(other)


def scatter_sum(blocks, dtype):
    chips = pair_halves(blocks).astype(dtype)
    arrived = lax.all_to_all(chips, CHIPS, split_axis=0, concat_axis=0, tiled=True)
    return jnp.sum(arrived.astype(F32), axis=0)


def per_device(
    tokens, out_grad, query_weight, gain, shift, first_keys, second_keys, values, pick_shard, pick_low,
    pick_second,
):
    devices = lax.axis_size(ALL)
    n = tokens.shape[0]
    heads, rows_dev, width = values.shape
    subkeys, half = first_keys.shape[1:]
    top = pick_shard.shape[2]
    everything = n * devices
    rows = heads * rows_dev

    tiles = out_grad.reshape(n, 8, width // 8)
    all_grad = lax.all_gather(tiles, ALL, axis=0, tiled=True)

    raw_query = jnp.dot(tokens, query_weight, preferred_element_type=F32)
    local_mean = jnp.mean(raw_query, axis=0)
    local_spread = jnp.sum(jnp.square(raw_query - local_mean), axis=0)
    centre, spread = all_moments(local_mean, local_spread, n)
    inverse = 1.0 / jnp.sqrt(spread + epsilon)

    shard_ids = pick_shard.reshape(n, heads * top)
    second_ids = pick_second.reshape(n, heads * top)
    code = pick_low.reshape(n, heads * top) * subkeys + second_ids
    pos, dense, slot_index = call(
        functools.partial(slots_kernel, heads, top),
        (shape((heads * n, LANES), F32), shape((heads * n, LANES), I32), shape((devices, LANES), I32)),
    )(shard_ids, code)
    slot_index = lax.all_to_all(slot_index.reshape(devices, 1, LANES), ALL, split_axis=0, concat_axis=0, tiled=True)

    first_split = first_keys.reshape(heads, devices, subkeys // devices, half).swapaxes(1, 2)
    first_split = first_split.reshape(heads, subkeys, half)
    query, normed, weight, slot_weight = call(
        functools.partial(score_kernel, heads, half),
        (
            shape((n, width), BF16),
            shape((n, width), F32),
            shape((heads * n, LANES), F32),
            shape((devices, LANES), F32),
        ),
    )(
        raw_query, jnp.stack([centre, inverse]), gain[None], shift[None], first_split, second_keys, pos, dense
    )
    slot_weight = lax.all_to_all(slot_weight.reshape(devices, 1, LANES), ALL, split_axis=0, concat_axis=0, tiled=True)

    vmem = pl.BlockSpec(memory_space=pltpu.VMEM)
    smem = pl.BlockSpec(memory_space=pltpu.SMEM)
    value_tiles = values.reshape(rows, 8, width // 8)
    value_grad, product = call(
        functools.partial(serve_kernel, n, rows),
        (shape((rows, width), BF16), shape((devices, LANES), F32)),
        limit=60,
        grid=(devices // GROUP,),
        in_specs=[
            smem,
            smem,
            pl.BlockSpec((GROUP * n, 8, width // 8), lambda i: (i, 0, 0)),
            vmem,
        ],
        out_specs=[vmem, vmem],
        scratch_shapes=[pltpu.VMEM((rows * 8, LANES), F32), pltpu.VMEM((CAP * 8, LANES), F32)],
    )(slot_index.reshape(devices, LANES), slot_weight.reshape(devices, LANES), all_grad, value_tiles)
    returned = lax.all_to_all(product.reshape(devices, 1, LANES), ALL, split_axis=0, concat_axis=0, tiled=True)

    query_grad, key_grad, sums = call(
        functools.partial(back_kernel, heads, top, half),
        (shape((n, width), F32), shape((2, heads, subkeys, half), F32), shape((2, width), F32)),
    )(
        returned.reshape(devices, LANES), shard_ids, second_ids, pos, dense, weight, query, normed,
        first_split, second_keys,
    )
    shift_grad, gain_grad = all_sum(sums)
    raw_grad = (
        gain * inverse * (query_grad - shift_grad / everything - normed * gain_grad / everything)
    ).astype(BF16)
    token_grad = lax.dot_general(raw_grad, query_weight, NT, preferred_element_type=F32).astype(BF16)
    weight_part = lax.dot_general(raw_grad, tokens, TN, preferred_element_type=F32)
    query_weight_grad = scatter_sum(weight_part.reshape(devices // 2, 2, width // devices, width), BF16)

    blocks = key_grad.reshape(devices // 2, 2, -1, half)
    own_keys = scatter_sum(blocks, BF16)
    chip_keys = everyone(own_keys, CHIPS)
    other_keys = swap_core(chip_keys)
    core = lax.axis_index("c")
    key_grad = jnp.where(
        core == 0, jnp.stack([chip_keys, other_keys], 1), jnp.stack([other_keys, chip_keys], 1)
    ).reshape(2, heads, subkeys, half)
    first_key_grad = key_grad[0].reshape(heads, subkeys // devices, devices, half).swapaxes(1, 2)
    return (
        token_grad,
        query_weight_grad,
        gain_grad,
        shift_grad,
        first_key_grad.reshape(heads, subkeys, half),
        key_grad[1],
        value_grad.reshape(heads, rows_dev, width),
    )


def solution(mesh):
    fine = Mesh(mesh.devices.reshape(4, 4, 4, 2), ALL)
    split_rows = P(ALL, None)
    in_specs = (
        split_rows, split_rows, P(), P(), P(), P(), P(), P(None, ALL, None),
        P(ALL, None, None), P(ALL, None, None), P(ALL, None, None),
    )
    out_specs = (split_rows, split_rows, P(), P(), P(), P(), P(None, ALL, None))
    return jax.shard_map(per_device, mesh=fine, in_specs=in_specs, out_specs=out_specs, check_vma=False)
```

time: 1380 us -> 340 us (0.25)
  waiting for transfers between devices: 764 us -> 93 us
  local copies, waits for them, and re-layouts: 260 us -> 34.8 us
  blocking collectives: 196 us -> 31.4 us
  other arithmetic: 98.5 us -> 11.3 us
  Pallas kernels: 0 us -> 66.7 us
  starting transfers between devices: 24.5 us -> 79.8 us
    reduce_scatter x1 -> x0, waiting for transfers between devices: 639 us -> none  [per_device(): lax.psum_scatter(jnp.einsum('tk,td->kd', raw_grad, tokens, preferred_elem...]
    gather x29 -> x0, local copies, waits for them, and re-layouts: 230 us -> none  [the longest x10 34.5 us: per_device(): jnp.take_along_axis(far_full, pick_second[:, head_id], axis=1)]
    psum x3 -> x0, blocking collectives: 196 us -> none  [the longest x1 68.7 us: per_device(): lax.psum(jnp.sum(raw_query, axis=0), ('outer', 'inner')) / all_tokens]
    pallas_call x0 -> x4, Pallas kernels: none -> 66.7 us  [the longest x1 58.8 us: per_device(): call(functools.partial(serve_kernel, n, rows), (shape((rows, width), BF16...]
    all_to_all x3 -> x9, waiting for transfers between devices: 109 us -> 44.3 us  [the longest x5 21.3 us: everyone(): return lax.all_to_all(wide, axis, split_axis=0, concat_axis=0, tiled=True)]
    scatter-add x1 -> x0, other arithmetic: 50 us -> none  [serve_rows(): jnp.zeros(value_table.shape, jnp.float32).at[row_index]]
    all_gather x0 -> x1, waiting for transfers between devices: none -> 47 us  [per_device(): all_grad = lax.all_gather(tiles, ALL, axis=0, tiled=True)]
    all_to_all x3 -> x9, starting transfers between devices: 24.4 us -> 68.5 us  [the longest x1 26.5 us: per_device(): lax.all_to_all(product.reshape(devices, 1, LANES), ALL, split_axis=0, con...]
  transfers between devices with their start and end apart: 5 -> 15, of which waited for: 4 -> 10; matrix products, arithmetic and copies ran while one was open for 10% -> 10% of each run, Pallas kernels for 0% -> 1%
where the time goes in v1:
time: 340 us; the launch traced here: 336 us
  waiting for transfers between devices  93 us (27%)
  starting transfers between devices  79.8 us (23%)
  Pallas kernels  66.7 us (20%)
  local copies, waits for them, and re-layouts  34.8 us (10%)
  blocking collectives  31.4 us (9%)
  between operations  14.4 us (4%)
  other arithmetic  11.3 us (3%)
  matrix products  4.68 us (1%)
    pallas_call x1, Pallas kernels, per_device(): call(functools.partial(serve_kernel, n, rows), (shape((rows, width), BF16...  58.8 us
    all_gather x1, waiting for transfers between devices, per_device(): all_grad = lax.all_gather(tiles, ALL, axis=0, tiled=True)  47 us
    all_to_all x1, starting transfers between devices, per_device(): lax.all_to_all(product.reshape(devices, 1, LANES), ALL, split_axis=0, con...  26.5 us
    all_to_all x5, waiting for transfers between devices, everyone(): return lax.all_to_all(wide, axis, split_axis=0, concat_axis=0, tiled=True)  21.3 us
    unnamed x50, local copies, waits for them, and re-layouts  21 us
    all_to_all x5, starting transfers between devices, everyone(): return lax.all_to_all(wide, axis, split_axis=0, concat_axis=0, tiled=True)  20.5 us
    all_to_all x1, blocking collectives, scatter_sum(): lax.all_to_all(chips, CHIPS, split_axis=0, concat_axis=0, tiled=True)  16.4 us
    all_to_all x2, blocking collectives, everyone(): return lax.all_to_all(wide, axis, split_axis=0, concat_axis=0, tiled=True)  15 us
  transfers between devices with their start and end apart: 15, of which 10 were waited for; matrix products, arithmetic and copies ran while one was open for 10% of the time, Pallas kernels for 1%

profile of v1, /device:TPU:1, one launch (start us, length us, event | category | flops | bytes accessed | tf_op | source)
XLA Modules:
  0.0 336.2 jit_solution(144770419794625416)
XLA Ops:
  13.2 8.4 %all_to_all.60 = f32[4,2,1024]{2,1,0:T(2,128)S(1)} all-to-all(f32[4,2,1024]{2,1,0:T(2,128)S(1)} %broadcast_in_dim.18), channel_id=1, replica_groups=mesh['x'=4,'z'=4,'y'=4,'c'=2] {'y'}, dimensions={0} | all-to-all | bytes 65536 | tf_op jit(solution)/shard_map/all_to_all | solution.py:226
  22.3 5.0 %all-to-all-start.1 = ((f32[4,2,1024]{2,1,0:T(2,128)}), f32[4,2,1024]{2,1,0:T(2,128)S(1)}, u32[]{:S(2)}, u32[]{:S(2)}) async-start(f32[4,2,1024]{2,1,0:T(2,128)} %broadcast_in_dim.19), calls=%async_computation.1 | async-start | bytes 65536 | tf_op jit(solution)/shard_map/all_to_all | solution.py:226
  27.3 4.3 %all-to-all-done.1 = f32[4,2,1024]{2,1,0:T(2,128)S(1)} async-done(((f32[4,2,1024]{2,1,0:T(2,128)}), f32[4,2,1024]{2,1,0:T(2,128)S(1)}, u32[]{:S(2)}, u32[]{:S(2)}) %all-to-all-start.1) | async-done | bytes 32800 | tf_op jit(solution)/shard_map/all_to_all | solution.py:226
  32.3 4.0 %all-to-all-start.2 = ((f32[4,2,1024]{2,1,0:T(2,128)}), f32[4,2,1024]{2,1,0:T(2,128)}, u32[]{:S(2)}, u32[]{:S(2)}) async-start(f32[4,2,1024]{2,1,0:T(2,128)} %broadcast_in_dim.20), calls=%async_computation.2 | async-start | bytes 65536 | tf_op jit(solution)/shard_map/all_to_all | solution.py:226
  41.1 9.1 %all-to-all-start.3 = ((s32[128,1,128]{2,1,0:T(1,128)}), s32[128,1,128]{2,1,0:T(1,128)S(1)}, u32[]{:S(2)}, u32[]{:S(2)}) async-start(s32[128,1,128]{2,1,0:T(1,128)} %bitcast.130), calls=%async_computation.3 | async-start | bytes 131072 | tf_op jit(solution)/shard_map/all_to_all | solution.py:287
  56.6 3.2 all-to-all-done.3
  59.8 6.6 %all-to-all-start.4 = ((f32[128,1,128]{2,1,0:T(1,128)}), f32[128,1,128]{2,1,0:T(1,128)S(1)}, u32[]{:S(2)}, u32[]{:S(2)}) async-start(f32[128,1,128]{2,1,0:T(1,128)} %bitcast.27), calls=%async_computation.4 | async-start | bytes 131072 | tf_op jit(solution)/shard_map/all_to_all | solution.py:302
  66.4 9.1 %copy.113 = bf16[512,8,8,128]{3,2,1,0:T(8,128)(2,1)} copy(bf16[512,8,8,128]{3,1,2,0:T(8,128)(2,1)} %bitcast.136) | data formatting | bytes 16777216
  75.8 47.0 %all-gather.2.cloned.1.call-done.grad_ref = bf16[16384,8,128]{2,1,0:T(8,128)(2,1)} async-done(((bf16[128,8,128]{2,1,0:T(8,128)(2,1)}), bf16[16384,8,128]{2,1,0:T(8,128)(2,1)}) %all-gather.2.cloned.1.call-update) | async-done | bytes 33554448 | tf_op jit(solution)/shard_map/all_gather | solution.py:272
  122.8 58.8 %shard_map.164 = (bf16[4096,1024]{1,0:T(8,128)(2,1)}, f32[128,128]{1,0:T(8,128)}) custom-call(s32[128,128]{1,0:T(8,128)} %bitcast.142, f32[128,128]{1,0:T(8,128)} %bitcast.143, bf16[16384,8,128]{2,1,0:T(8,128)(2,1)} %all-gather.2.cloned.1.call-done.grad_ref, bf16[4096,8,128]{2,1,0:T(8,128)(2,1)} %bitcast.133), custom_call_target="tpu_custom_call" | custom-call | tf_op jit(solution)/shard_map/pallas_call | solution.py:307
  181.6 26.5 %all-to-all-start.5 = ((f32[128,1,128]{2,1,0:T(1,128)}), f32[128,1,128]{2,1,0:T(1,128)}, u32[]{:S(2)}, u32[]{:S(2)}) async-start(f32[128,1,128]{2,1,0:T(1,128)} %bitcast.146), calls=%async_computation.5 | async-start | bytes 131072 | tf_op jit(solution)/shard_map/all_to_all | solution.py:321
  209.0 8.5 %all-to-all-done.5 = f32[128,1,128]{2,1,0:T(1,128)} async-done(((f32[128,1,128]{2,1,0:T(1,128)}), f32[128,1,128]{2,1,0:T(1,128)}, u32[]{:S(2)}, u32[]{:S(2)}) %all-to-all-start.5) | async-done | bytes 65568 | tf_op jit(solution)/shard_map/all_to_all | solution.py:321
  220.4 3.8 %shard_map.165 = (f32[128,1024]{1,0:T(8,128)S(1)}, f32[2,2,512,256]{3,2,1,0:T(8,128)S(1)}, f32[2,1024]{1,0:T(2,128)S(1)}) custom-call(f32[128,128]{1,0:T(8,128)} %bitcast.31.back_ref, s32[128,32]{1,0:T(8,128)S(1)} %copy.86.shard_ref, s32[128,32]{1,0:T(8,128)S(1)} %copy.93.second_ids_ref, f32[256,128]{1,0:T(8,128)S(1)} %get-tuple-element.20.pos_ref, ...), custom_call_target="tpu_custom_call" | custom-call | tf_op jit(solution)/shard_map/pallas_call | solution.py:323
  228.2 6.7 %all_to_all.61 = f32[4,2,1024]{2,1,0:T(2,128)S(1)} all-to-all(f32[4,2,1024]{2,1,0:T(2,128)S(1)} %broadcast_in_dim.23), channel_id=1, replica_groups=mesh['x'=4,'z'=4,'y'=4,'c'=2] {'y'}, dimensions={0} | all-to-all | bytes 65536 | tf_op jit(solution)/shard_map/all_to_all | solution.py:226
  235.5 3.3 all-to-all-start.7
  238.7 4.3 %all-to-all-done.7 = f32[4,2,1024]{2,1,0:T(2,128)S(1)} async-done(((f32[4,2,1024]{2,1,0:T(2,128)}), f32[4,2,1024]{2,1,0:T(2,128)S(1)}, u32[]{:S(2)}, u32[]{:S(2)}) %all-to-all-start.7) | async-done | bytes 32800 | tf_op jit(solution)/shard_map/all_to_all | solution.py:226
  243.6 3.3 all-to-all-start.8
  257.0 3.1 collective-permute-start.2
  261.8 16.4 %all_to_all.62 = bf16[64,16,256]{2,1,0:T(8,128)(2,1)S(1)} all-to-all(bf16[64,16,256]{2,1,0:T(8,128)(2,1)S(1)} %fusion.1), channel_id=1, replica_groups=mesh['x'=4,'z'=4,'y'=4,'c'=2] {'x','z','y'}, dimensions={0} | all-to-all | bytes 1048576 | tf_op jit(solution)/shard_map/all_to_all | solution.py:255
  279.5 4.9 %all-to-all-start.11 = ((f32[64,16,256]{2,1,0:T(8,128)}), f32[64,16,256]{2,1,0:T(8,128)S(1)}, u32[]{:S(2)}, u32[]{:S(2)}) async-start(f32[64,16,256]{2,1,0:T(8,128)} %broadcast_in_dim.26), calls=%async_computation.11 | async-start | bytes 2097152 | tf_op jit(solution)/shard_map/all_to_all | solution.py:226
  284.4 3.5 %fusion = bf16[64,8,1024]{2,1,0:T(8,128)(2,1)} fusion(f32[64,8,1024]{2,1,0:T(8,128)} %collective-permute-done.2, f32[64,2,8,1024]{3,2,1,0:T(8,128)} %bitcast.135, s32[]{:T(128)S(6)} %select_n.18), kind=kLoop, calls=%fused_computation.2 | loop fusion | flops 1048576 | bytes 5242884 | tf_op jit(solution)/shard_map/convert_element_type | solution.py:254
  287.9 12.7 %all-to-all-done.11 = f32[64,16,256]{2,1,0:T(8,128)S(1)} async-done(((f32[64,16,256]{2,1,0:T(8,128)}), f32[64,16,256]{2,1,0:T(8,128)S(1)}, u32[]{:S(2)}, u32[]{:S(2)}) %all-to-all-start.11) | async-done | bytes 1048608 | tf_op jit(solution)/shard_map/all_to_all | solution.py:226
  300.6 5.8 %all-to-all-start.9 = ((bf16[64,8,1024]{2,1,0:T(8,128)(2,1)}), bf16[64,8,1024]{2,1,0:T(8,128)(2,1)}, u32[]{:S(2)}, u32[]{:S(2)}) async-start(bf16[64,8,1024]{2,1,0:T(8,128)(2,1)} %fusion), calls=%async_computation.9 | async-start | bytes 2097152 | tf_op jit(solution)/shard_map/all_to_all | solution.py:255
  311.0 11.1 %all-to-all-done.9 = bf16[64,8,1024]{2,1,0:T(8,128)(2,1)} async-done(((bf16[64,8,1024]{2,1,0:T(8,128)(2,1)}), bf16[64,8,1024]{2,1,0:T(8,128)(2,1)}, u32[]{:S(2)}, u32[]{:S(2)}) %all-to-all-start.9) | async-done | bytes 1048608 | tf_op jit(solution)/shard_map/all_to_all | solution.py:255
  (119 shorter events, 52.3 us)
Async XLA Ops:
  7.2 115.6 %all-gather.2.cloned.1.call-start = ((), (), s32[]{:S(2)}) async-start(), calls=%async_computation.12 | async-start | bytes 33816576 | tf_op jit(solution)/shard_map/all_gather | solution.py:272
  9.1 27.2 %copy-start.20 = (s32[128,2,16]{0,2,1:T(8,128)S(1)}, s32[128,2,16]{0,2,1:T(8,128)}, u32[]{:S(2)}) copy-start(s32[128,2,16]{0,2,1:T(8,128)} %param.21) | copy-start | bytes 49156
  9.1 27.2 %copy-start.22 = (s32[128,2,16]{0,2,1:T(8,128)S(1)}, s32[128,2,16]{0,2,1:T(8,128)}, u32[]{:S(2)}) copy-start(s32[128,2,16]{0,2,1:T(8,128)} %param.19) | copy-start | bytes 49156
  9.1 27.4 %copy-start.17 = (bf16[2,512,256]{2,1,0:T(8,128)(2,1)S(1)}, bf16[2,512,256]{2,1,0:T(8,128)(2,1)}, u32[]{:S(2)}) copy-start(bf16[2,512,256]{2,1,0:T(8,128)(2,1)} %param.16) | copy-start | bytes 1572868
  10.6 40.5 %copy-start.14 = (f32[1024]{0:T(1024)S(1)}, f32[1024]{0:T(1024)}, u32[]{:S(2)}) copy-start(f32[1024]{0:T(1024)} %param.14) | copy-start | bytes 12292
  10.6 40.6 %copy-start.15 = (f32[1024]{0:T(1024)S(1)}, f32[1024]{0:T(1024)}, u32[]{:S(2)}) copy-start(f32[1024]{0:T(1024)} %param.15) | copy-start | bytes 12292
  10.7 2.3 collective-permute-start
  22.3 9.3 %all-to-all-start.1 = ((f32[4,2,1024]{2,1,0:T(2,128)}), f32[4,2,1024]{2,1,0:T(2,128)S(1)}, u32[]{:S(2)}, u32[]{:S(2)}) async-start(f32[4,2,1024]{2,1,0:T(2,128)} %broadcast_in_dim.19), calls=%async_computation.1 | async-start | bytes 65536 | tf_op jit(solution)/shard_map/all_to_all | solution.py:226
  32.3 8.8 %all-to-all-start.2 = ((f32[4,2,1024]{2,1,0:T(2,128)}), f32[4,2,1024]{2,1,0:T(2,128)}, u32[]{:S(2)}, u32[]{:S(2)}) async-start(f32[4,2,1024]{2,1,0:T(2,128)} %broadcast_in_dim.20), calls=%async_computation.2 | async-start | bytes 65536 | tf_op jit(solution)/shard_map/all_to_all | solution.py:226
  41.1 18.6 %all-to-all-start.3 = ((s32[128,1,128]{2,1,0:T(1,128)}), s32[128,1,128]{2,1,0:T(1,128)S(1)}, u32[]{:S(2)}, u32[]{:S(2)}) async-start(s32[128,1,128]{2,1,0:T(1,128)} %bitcast.130), calls=%async_computation.3 | async-start | bytes 131072 | tf_op jit(solution)/shard_map/all_to_all | solution.py:287
  59.8 16.0 %all-to-all-start.4 = ((f32[128,1,128]{2,1,0:T(1,128)}), f32[128,1,128]{2,1,0:T(1,128)S(1)}, u32[]{:S(2)}, u32[]{:S(2)}) async-start(f32[128,1,128]{2,1,0:T(1,128)} %bitcast.27), calls=%async_computation.4 | async-start | bytes 131072 | tf_op jit(solution)/shard_map/all_to_all | solution.py:302
  75.8 47.0 %copy-start.19 = (f32[128,1,128]{2,1,0:T(1,128)}, f32[128,1,128]{2,1,0:T(1,128)S(1)}, u32[]{:S(2)}) copy-start(f32[128,1,128]{2,1,0:T(1,128)S(1)} %all-to-all-done.4) | copy-start | bytes 196612
  122.8 94.6 %copy-start.2 = (bf16[2,512,256]{2,1,0:T(8,128)(2,1)S(1)}, bf16[2,512,256]{2,1,0:T(8,128)(2,1)}, u32[]{:S(2)}) copy-start(bf16[2,512,256]{2,1,0:T(8,128)(2,1)} %second_ref.3) | copy-start | bytes 1572868
  181.6 35.8 %all-to-all-start.5 = ((f32[128,1,128]{2,1,0:T(1,128)}), f32[128,1,128]{2,1,0:T(1,128)}, u32[]{:S(2)}, u32[]{:S(2)}) async-start(f32[128,1,128]{2,1,0:T(1,128)} %bitcast.146), calls=%async_computation.5 | async-start | bytes 131072 | tf_op jit(solution)/shard_map/all_to_all | solution.py:321
  226.4 26.1 %copy-start.5 = (f32[128,1024]{1,0:T(8,128)S(1)}, f32[128,1024]{1,0:T(8,128)}, u32[]{:S(2)}) copy-start(f32[128,1024]{1,0:T(8,128)} %copy-done.3) | copy-start | bytes 1572868
  226.4 26.1 %copy-start.8 = (f32[128,1024]{1,0:T(8,128)S(1)}, f32[128,1024]{1,0:T(8,128)}, u32[]{:S(2)}) copy-start(f32[128,1024]{1,0:T(8,128)} %copy-done.7) | copy-start | bytes 1572868
  226.4 1.8 collective-permute-start.1
  235.5 7.5 %all-to-all-start.7 = ((f32[4,2,1024]{2,1,0:T(2,128)}), f32[4,2,1024]{2,1,0:T(2,128)S(1)}, u32[]{:S(2)}, u32[]{:S(2)}) async-start(f32[4,2,1024]{2,1,0:T(2,128)} %broadcast_in_dim.24), calls=%async_computation.7 | async-start | bytes 65536 | tf_op jit(solution)/shard_map/all_to_all | solution.py:226
  243.6 8.2 %all-to-all-start.8 = ((f32[4,2,1024]{2,1,0:T(2,128)}), f32[4,2,1024]{2,1,0:T(2,128)S(1)}, u32[]{:S(2)}, u32[]{:S(2)}) async-start(f32[4,2,1024]{2,1,0:T(2,128)} %broadcast_in_dim.25), calls=%async_computation.8 | async-start | bytes 65536 | tf_op jit(solution)/shard_map/all_to_all | solution.py:226
  249.2 10.9 %collective-permute-start.3 = (f32[64,16,256]{2,1,0:T(8,128)}, f32[64,16,256]{2,1,0:T(8,128)}, u32[]{:S(2)}, u32[]{:S(2)}) collective-permute-start(f32[64,16,256]{2,1,0:T(8,128)} %dynamic-slice_bitcast_fusion.1), channel_id=1, source_target_pairs={{0,1},{1,0},{2,3},{3,2},{4,5},{5,4},{6,7},{7,6},{8,9},{9,8},{10,11... | collective-permute-start | bytes 3145736 | tf_op jit(solution)/shard_map/ppermute | solution.py:220
  257.0 27.4 %collective-permute-start.2 = (f32[64,8,1024]{2,1,0:T(8,128)}, f32[64,8,1024]{2,1,0:T(8,128)}, u32[]{:S(2)}, u32[]{:S(2)}) collective-permute-start(f32[64,8,1024]{2,1,0:T(8,128)} %dynamic-slice_bitcast_fusion), channel_id=1, source_target_pairs={{0,1},{1,0},{2,3},{3,2},{4,5},{5,4},{6,7},{7,6},{8,9},{9,8},{10,11... | collective-permute-start | bytes 6291464 | tf_op jit(solution)/shard_map/ppermute | solution.py:220
  279.5 21.2 %all-to-all-start.11 = ((f32[64,16,256]{2,1,0:T(8,128)}), f32[64,16,256]{2,1,0:T(8,128)S(1)}, u32[]{:S(2)}, u32[]{:S(2)}) async-start(f32[64,16,256]{2,1,0:T(8,128)} %broadcast_in_dim.26), calls=%async_computation.11 | async-start | bytes 2097152 | tf_op jit(solution)/shard_map/all_to_all | solution.py:226
  300.6 21.6 %all-to-all-start.9 = ((bf16[64,8,1024]{2,1,0:T(8,128)(2,1)}), bf16[64,8,1024]{2,1,0:T(8,128)(2,1)}, u32[]{:S(2)}, u32[]{:S(2)}) async-start(bf16[64,8,1024]{2,1,0:T(8,128)(2,1)} %fusion), calls=%async_computation.9 | async-start | bytes 2097152 | tf_op jit(solution)/shard_map/all_to_all | solution.py:255
  306.4 17.8 %collective-permute-start.4 = (f32[64,16,256]{2,1,0:T(8,128)S(1)}, f32[64,16,256]{2,1,0:T(8,128)}, u32[]{:S(2)}, u32[]{:S(2)}) collective-permute-start(f32[64,16,256]{2,1,0:T(8,128)S(1)} %all-to-all-done.11), channel_id=1, source_target_pairs={{0,1},{1,0},{2,3},{3,2},{4,5},{5,4},{6,7},{7,6},{8,9},{9,8},{10,11... | collective-permute-start | bytes 3145736 | tf_op jit(solution)/shard_map/ppermute | solution.py:220
  (15 other events, 49.3 us)
Sparse Core Ops, SparseCore 0:
  11.6 111.2 all-gather.1

commit v2 on v1

--- a/solution.py
+++ b/solution.py
@@ -48,12 +48,19 @@
         before = before + jnp.sum(ones, axis=0, keepdims=True)
         place = jnp.where(hit, place, -1.0)
         pos.append(place)
-        packed.append(((h * 2048 + code) * n + row).astype(F32))
+        packed.append(((h * 2048 + code) * n + row + 1).astype(F32))
         pos_ref[h * n : (h + 1) * n, :] = place
         dense_ref[h * n : (h + 1) * n, :] = code
-    lines = slot_table(pos, packed)
-    table = jnp.concatenate(lines[:CAP] + [before, lines[CAP][1:]], axis=0)
-    slot_ref[...] = table.T.astype(I32)
+    table = jnp.concatenate(slot_table(pos, packed)[:CAP], axis=0).astype(I32) - 1
+    table = jnp.where(table < 0, (heads * 2048 + iota((CAP, LANES), 0)) * n, table)
+    clash = jnp.zeros((8, LANES), I32)
+    for b in range(CAP // 8):
+        target = table[b * 8 : b * 8 + 8, :] >> 7
+        for d in range(1, 5):
+            clash = jnp.where(pltpu.roll(target, d, 0) == target, 1, clash)
+    clash = jnp.max(clash.astype(F32), axis=0, keepdims=True)
+    rest = jnp.zeros((LANES - CAP - 1, LANES), F32)
+    slot_ref[...] = jnp.concatenate([table.astype(F32), clash, rest], axis=0).T.astype(I32)
 
 
 def score_kernel(
@@ -97,61 +104,112 @@
     slot_ref[...] = jnp.concatenate(slot_table(pos, weights), axis=0).T
 
 
-def serve_kernel(tokens, rows, index_ref, weight_ref, grad_ref, value_ref, out_ref, product_ref, total, held):
+def slot_of(index_ref, weight_ref, grad_ref, sender, g, j, tokens):
+    packed = index_ref[sender, j]
+    grad = grad_ref[g * tokens + (packed & (tokens - 1))].astype(F32)
+    message = (grad * weight_ref[sender, j]).astype(BF16).astype(F32)
+    return packed >> 7, message
+
+
+def product_kernel(tokens, rows, index_ref, weight_ref, grad_ref, value_ref, product_ref, held):
     step = pl.program_id(0)
+    eye = iota((CAP, LANES), 0) == iota((CAP, LANES), 1)
+
+    def one_sender(g, carry):
+        for j in range(CAP):
+            row, message = slot_of(index_ref, weight_ref, grad_ref, step * GROUP + g, g, j, tokens)
+            value = value_ref[row & (rows - 1)].astype(F32)
+            held[pl.ds(pl.multiple_of((g * CAP + j) * 8, 8), 8), :] = message * value
+        return carry
+
+    lax.fori_loop(0, GROUP, one_sender, 0)
+    for g in range(GROUP):
+        part = held[pl.ds(g * CAP * 8, CAP, stride=8), :]
+        for c in range(1, 8):
+            part = part + held[pl.ds(g * CAP * 8 + c, CAP, stride=8), :]
+        summed = jnp.sum(part, axis=1, keepdims=True)
+        product_ref[g : g + 1, :] = jnp.sum(jnp.where(eye, summed, 0.0), axis=0, keepdims=True)
+
+
+def spot(row):
+    return pl.ds(pl.multiple_of(row * 8, 8), 8)
+
+
+def add_messages(tokens, first, index_ref, weight_ref, grad_ref, total):
+    def one_sender(g, carry):
+        sender = first + g
+        clash = index_ref[sender, CAP]
+
+        @pl.when(clash == 0)
+        def _():
+            for b in range(CAP // 8):
+                slots = [
+                    slot_of(index_ref, weight_ref, grad_ref, sender, g, b * 8 + u, tokens) for u in range(8)
+                ]
+                sums = [total[spot(row), :] + message for row, message in slots]
+                for (row, _), value in zip(slots, sums):
+                    total[spot(row), :] = value
+
+        @pl.when(clash != 0)
+        def _():
+            def one(j, inner):
+                row, message = slot_of(index_ref, weight_ref, grad_ref, sender, g, j, tokens)
+                total[spot(row), :] += message
+                return inner
+
+            lax.fori_loop(0, CAP, one, 0)
+
+        return carry
+
+    lax.fori_loop(0, GROUP, one_sender, 0)
+
+
+def clear_all(total):
+    def clear(i, carry):
+        at = pl.multiple_of(i * 352, 8)
+        total[pl.ds(at, 352), :] = jnp.zeros((352, LANES), F32)
+        return carry
+
+    lax.fori_loop(0, total.shape[0] // 352, clear, 0)
+
+
+def early_kernel(tokens, index_ref, weight_ref, grad_ref, after_ref, total, done_ref):
+    step = pl.program_id(0)
+    done_ref[...] = jnp.zeros((8, LANES), F32)
 
     @pl.when(step == 0)
     def _():
-        def clear(i, carry):
-            at = pl.multiple_of(i * 256, 256)
-            total[pl.ds(at, 256), :] = jnp.zeros((256, LANES), F32)
-            return carry
-
-        lax.fori_loop(0, rows * 8 // 256, clear, 0)
-
-    eye = iota((CAP, LANES), 0) == iota((CAP, LANES), 1)
-
-    def one_sender(g, carry):
-        sender = step * GROUP + g
-        count = index_ref[sender, CAP]
-
-        def eight(b, inner):
-            for u in range(8):
-                j = b * 8 + u
-                packed = index_ref[sender, j]
-                weight = weight_ref[sender, j]
-                row = packed // tokens
-                token = packed % tokens
-                grad = grad_ref[g * tokens + token].astype(F32)
-                message = (grad * weight).astype(BF16).astype(F32)
-                value = value_ref[row].astype(F32)
-                held[pl.ds(pl.multiple_of(j * 8, 8), 8), :] = message * value
-                at = pl.ds(pl.multiple_of(row * 8, 8), 8)
-                total[at, :] += message
-            return inner
-
-        lax.fori_loop(0, (count + 7) // 8, eight, 0)
-        part = held[pl.ds(0, CAP, stride=8), :]
-        for c in range(1, 8):
-            part = part + held[pl.ds(c, CAP, stride=8), :]
-        summed = jnp.sum(part, axis=1, keepdims=True)
-        line = jnp.sum(jnp.where(eye, summed, 0.0), axis=0, keepdims=True)
-        product_ref[pl.ds(sender, 1), :] = line
-        return carry
-
-    lax.fori_loop(0, GROUP, one_sender, 0)
+        clear_all(total)
+
+    add_messages(tokens, step * GROUP, index_ref, weight_ref, grad_ref, total)
+
+
+def late_kernel(
+    tokens, senders, index_ref, weight_ref, grad_ref, early_ref, after_ref, out_ref, done_ref, total, sem
+):
+    step = pl.program_id(0)
+    done_ref[...] = jnp.zeros((8, LANES), F32)
+
+    @pl.when(step == 0)
+    def _():
+        copy = pltpu.make_async_copy(early_ref, total, sem)
+        copy.start()
+        copy.wait()
+
+    add_messages(tokens, senders + step * GROUP, index_ref, weight_ref, grad_ref, total)
 
     @pl.when(step == pl.num_programs(0) - 1)
     def _():
         def emit(i, carry):
-            at = pl.multiple_of(i * 16, 16)
-            for c in range(8):
-                out_ref[pl.ds(at, 16), c * LANES : (c + 1) * LANES] = total[
-                    pl.ds(at * 8 + c, 16, stride=8), :
-                ].astype(BF16)
+            for u in range(4):
+                at = pl.multiple_of(i * 64 + u * 16, 16)
+                for c in range(8):
+                    out_ref[pl.ds(at, 16), c * LANES : (c + 1) * LANES] = total[
+                        pl.ds(at * 8 + c, 16, stride=8), :
+                    ].astype(BF16)
             return carry
 
-        lax.fori_loop(0, rows // 16, emit, 0)
+        lax.fori_loop(0, out_ref.shape[0] // 64, emit, 0)
 
 
 def split(value):
@@ -161,9 +219,10 @@
 
 def back_kernel(
     heads, top, half, back_ref, shard_ref, second_ids_ref, pos_ref, dense_ref, weight_ref, query_ref,
-    normed_ref, first_ref, second_ref, grad_ref, key_ref, sum_ref,
+    normed_ref, first_ref, second_ref, core_ref, grad_ref, own_ref, other_ref, sum_ref, held,
 ):
     n = query_ref.shape[0]
+    core = core_ref[0]
     table = back_ref[...].T
     wide = iota((n, 4 * LANES), 1)
     for h in range(heads):
@@ -195,15 +254,75 @@
                 rest, table_h, preferred_element_type=F32
             )
             grad_ref[:, cols] = grad
-            sum_ref[0:1, cols] = jnp.sum(grad, axis=0, keepdims=True)
-            sum_ref[1:2, cols] = jnp.sum(grad * normed_ref[:, cols], axis=0, keepdims=True)
+            at = h * 2 + side
+            sum_ref[at : at + 1, :] = jnp.sum(grad, axis=0, keepdims=True)
+            sum_ref[at + 4 : at + 5, :] = jnp.sum(grad * normed_ref[:, cols], axis=0, keepdims=True)
             query = query_ref[:, cols]
-            key_ref[side, h] = lax.dot_general(high, query, TN, preferred_element_type=F32) + lax.dot_general(
+            keys_grad = lax.dot_general(high, query, TN, preferred_element_type=F32) + lax.dot_general(
                 rest, query, TN, preferred_element_type=F32
             )
-
-
-def call(kernel, out_shape, limit=40, **more):
+            blocks = keys_grad.reshape(16, 2, 2, 8, half)
+            first = (side * heads + h) * 16
+            held[first : first + 16, :, :, 0:half] = blocks[:, :, 0]
+            held[first : first + 16, :, :, half : 2 * half] = blocks[:, :, 1]
+    own_ref[...] = held[:, core]
+    other_ref[...] = held[:, 1 - core]
+
+
+def tail_kernel(
+    everything, arrived_ref, query_grad_ref, normed_ref, gain_ref, stat_ref, tokens_ref, core_ref, after_ref,
+    raw_ref, own_ref, other_ref, sum_ref, block_ref, held,
+):
+    core = core_ref[0]
+    half = 256
+    reduced = jnp.sum(arrived_ref[...], axis=0)
+    block_ref[...] = reduced[:, half:].astype(BF16)
+    shift_sum = jnp.concatenate([reduced[i : i + 1, :half] for i in range(4)], axis=1)
+    gain_sum = jnp.concatenate([reduced[i : i + 1, :half] for i in range(4, 8)], axis=1)
+    sum_ref[0:1, :] = shift_sum
+    sum_ref[1:2, :] = gain_sum
+    raw_grad = (
+        gain_ref[...]
+        * stat_ref[1:2, :]
+        * (query_grad_ref[...] - shift_sum / everything - normed_ref[...] * gain_sum / everything)
+    ).astype(BF16)
+    raw_ref[...] = raw_grad
+    part = lax.dot_general(raw_grad, tokens_ref[...], TN, preferred_element_type=F32)
+    held[...] = part.reshape(held.shape)
+    own_ref[...] = held[:, core]
+    other_ref[...] = held[:, 1 - core]
+
+
+def sum_kernel(arrived_ref, after_ref, sum_ref, mine_ref):
+    width = sum_ref.shape[1]
+    sum_ref[...] = jnp.sum(arrived_ref[:, :, :width].astype(F32), axis=0)
+    mine_ref[...] = arrived_ref[:, :, width:]
+
+
+def keys_kernel(heads, mine_ref, theirs_ref, core_ref, first_ref, second_ref, held):
+    subkeys, half = first_ref.shape[1:]
+    at_zero = core_ref[0] == 0
+    each = subkeys // 32
+    source = iota((subkeys, subkeys), 0)
+    source = (source & 3) * LANES + (source >> 2)
+    order = (iota((subkeys, subkeys), 1) == source).astype(BF16)
+    for side in range(2):
+        for h in range(heads):
+            at = (side * heads + h) * each
+            mine = mine_ref[at : at + each].astype(F32)
+            theirs = theirs_ref[at : at + each].astype(F32)
+            pair = (jnp.where(at_zero, mine, theirs), jnp.where(at_zero, theirs, mine))
+            for c in range(2):
+                held[:, c, 0] = pair[c][:, :, :half]
+                held[:, c, 1] = pair[c][:, :, half:]
+            keys = held[...].reshape(subkeys, half)
+            if side == 0:
+                first_ref[h] = jnp.dot(order, keys.astype(BF16), preferred_element_type=F32)
+            else:
+                second_ref[h] = keys
+
+
+def call(kernel, out_shape, limit=16, **more):
     return pl.pallas_call(
         kernel,
         out_shape=out_shape,
@@ -224,13 +343,6 @@
     size = lax.axis_size(axis)
     wide = jnp.broadcast_to(value[None], (size,) + value.shape)
     return lax.all_to_all(wide, axis, split_axis=0, concat_axis=0, tiled=True)
-
-
-def all_sum(value):
-    value = value + swap_core(value)
-    for axis in ("y", "z", "x"):
-        value = jnp.sum(everyone(value, axis), axis=0)
-    return value
 
 
 def all_moments(mean, spread, count):
@@ -243,17 +355,8 @@
     return mean, spread / count
 
 
-def pair_halves(blocks):
-    core = lax.axis_index("c")
-    own = lax.dynamic_index_in_dim(blocks, core, 1, keepdims=False)
-    other = lax.dynamic_index_in_dim(blocks, 1 - core, 1, keepdims=False)
-    return own + swap_core(other)
-
-
-def scatter_sum(blocks, dtype):
-    chips = pair_halves(blocks).astype(dtype)
-    arrived = lax.all_to_all(chips, CHIPS, split_axis=0, concat_axis=0, tiled=True)
-    return jnp.sum(arrived.astype(F32), axis=0)
+def exchange(value, axis):
+    return lax.all_to_all(value, axis, split_axis=0, concat_axis=0, tiled=True)
 
 
 def per_device(
@@ -277,6 +380,7 @@
     centre, spread = all_moments(local_mean, local_spread, n)
     inverse = 1.0 / jnp.sqrt(spread + epsilon)
 
+    stats = jnp.stack([centre, inverse])
     shard_ids = pick_shard.reshape(n, heads * top)
     second_ids = pick_second.reshape(n, heads * top)
     code = pick_low.reshape(n, heads * top) * subkeys + second_ids
@@ -297,60 +401,114 @@
             shape((devices, LANES), F32),
         ),
     )(
-        raw_query, jnp.stack([centre, inverse]), gain[None], shift[None], first_split, second_keys, pos, dense
+        raw_query, stats, gain[None], shift[None], first_split, second_keys, pos, dense
     )
     slot_weight = lax.all_to_all(slot_weight.reshape(devices, 1, LANES), ALL, split_axis=0, concat_axis=0, tiled=True)
 
     vmem = pl.BlockSpec(memory_space=pltpu.VMEM)
     smem = pl.BlockSpec(memory_space=pltpu.SMEM)
+    hbm = pl.BlockSpec(memory_space=pltpu.HBM)
     value_tiles = values.reshape(rows, 8, width // 8)
-    value_grad, product = call(
-        functools.partial(serve_kernel, n, rows),
-        (shape((rows, width), BF16), shape((devices, LANES), F32)),
-        limit=60,
+    index_table = slot_index.reshape(devices, LANES)
+    weight_table = slot_weight.reshape(devices, LANES)
+    grad_spec = pl.BlockSpec((GROUP * n, 8, width // 8), lambda i: (i, 0, 0))
+    product = call(
+        functools.partial(product_kernel, n, rows),
+        shape((devices, LANES), F32),
+        limit=28,
         grid=(devices // GROUP,),
+        in_specs=[smem, smem, grad_spec, vmem],
+        out_specs=pl.BlockSpec((GROUP, LANES), lambda i: (i, 0)),
+        scratch_shapes=[pltpu.VMEM((GROUP * CAP * 8, LANES), F32)],
+    )(index_table, weight_table, all_grad, value_tiles)
+    returned = exchange(product.reshape(devices, 1, LANES), ALL)
+
+    chips = devices // 2
+    core = jnp.reshape(lax.axis_index("c"), (1,)).astype(I32)
+    query_grad, own_keys, other_keys, sums = call(
+        functools.partial(back_kernel, heads, top, half),
+        (
+            shape((n, width), F32),
+            shape((chips, 8, 2 * half), F32),
+            shape((chips, 8, 2 * half), F32),
+            shape((8, half), F32),
+        ),
+        in_specs=[vmem] * 10 + [smem],
+        scratch_shapes=[pltpu.VMEM((chips, 2, 8, 2 * half), F32)],
+    )(
+        returned.reshape(devices, LANES), shard_ids, second_ids, pos, dense, weight, query, normed,
+        first_split, second_keys, core,
+    )
+    keys_in, sums_in = swap_core((other_keys, sums))
+    sums = jnp.broadcast_to((sums + sums_in)[None], (chips, 8, half))
+    sent = jnp.concatenate([sums, own_keys + keys_in], axis=2)
+    arrived = exchange(sent, CHIPS)
+    steps = devices // GROUP // 2
+    early, early_done = call(
+        functools.partial(early_kernel, n),
+        (shape(((rows + CAP) * 8, LANES), F32), shape((8, LANES), F32)),
+        limit=32,
+        grid=(steps,),
+        in_specs=[smem, smem, grad_spec, vmem],
+        out_specs=[vmem, vmem],
+    )(index_table, weight_table, all_grad, sent[0, :, :LANES])
+
+    raw_grad, own_part, other_part, sums, key_block = call(
+        functools.partial(tail_kernel, everything),
+        (
+            shape((n, width), BF16),
+            shape((chips, 8, width), F32),
+            shape((chips, 8, width), F32),
+            shape((2, width), F32),
+            shape((8, 2 * half), BF16),
+        ),
+        in_specs=[vmem] * 6 + [smem, vmem],
+        scratch_shapes=[pltpu.VMEM((chips, 2, 8, width), F32)],
+        limit=24,
+    )(arrived, query_grad, normed, gain[None], stats, tokens, core, early_done)
+    shift_grad, gain_grad = sums
+    other_part = swap_core(other_part)
+    own_part = (own_part + other_part).astype(BF16)
+    key_wide = jnp.broadcast_to(key_block[None], (chips, 8, 2 * half))
+    sent = jnp.concatenate([own_part, key_wide], axis=2)
+    arrived = exchange(sent, CHIPS)
+    token_grad = lax.dot_general(raw_grad, query_weight, NT, preferred_element_type=F32).astype(BF16)
+    value_grad, late_done = call(
+        functools.partial(late_kernel, n, steps * GROUP),
+        (shape((rows, width), BF16), shape((8, LANES), F32)),
+        limit=50,
+        grid=(steps,),
         in_specs=[
             smem,
             smem,
-            pl.BlockSpec((GROUP * n, 8, width // 8), lambda i: (i, 0, 0)),
+            pl.BlockSpec((GROUP * n, 8, width // 8), lambda i: (i + steps, 0, 0)),
+            hbm,
             vmem,
         ],
         out_specs=[vmem, vmem],
-        scratch_shapes=[pltpu.VMEM((rows * 8, LANES), F32), pltpu.VMEM((CAP * 8, LANES), F32)],
-    )(slot_index.reshape(devices, LANES), slot_weight.reshape(devices, LANES), all_grad, value_tiles)
-    returned = lax.all_to_all(product.reshape(devices, 1, LANES), ALL, split_axis=0, concat_axis=0, tiled=True)
-
-    query_grad, key_grad, sums = call(
-        functools.partial(back_kernel, heads, top, half),
-        (shape((n, width), F32), shape((2, heads, subkeys, half), F32), shape((2, width), F32)),
-    )(
-        returned.reshape(devices, LANES), shard_ids, second_ids, pos, dense, weight, query, normed,
-        first_split, second_keys,
-    )
-    shift_grad, gain_grad = all_sum(sums)
-    raw_grad = (
-        gain * inverse * (query_grad - shift_grad / everything - normed * gain_grad / everything)
-    ).astype(BF16)
-    token_grad = lax.dot_general(raw_grad, query_weight, NT, preferred_element_type=F32).astype(BF16)
-    weight_part = lax.dot_general(raw_grad, tokens, TN, preferred_element_type=F32)
-    query_weight_grad = scatter_sum(weight_part.reshape(devices // 2, 2, width // devices, width), BF16)
-
-    blocks = key_grad.reshape(devices // 2, 2, -1, half)
-    own_keys = scatter_sum(blocks, BF16)
-    chip_keys = everyone(own_keys, CHIPS)
-    other_keys = swap_core(chip_keys)
-    core = lax.axis_index("c")
-    key_grad = jnp.where(
-        core == 0, jnp.stack([chip_keys, other_keys], 1), jnp.stack([other_keys, chip_keys], 1)
-    ).reshape(2, heads, subkeys, half)
-    first_key_grad = key_grad[0].reshape(heads, subkeys // devices, devices, half).swapaxes(1, 2)
+        scratch_shapes=[pltpu.VMEM(((rows + CAP) * 8, LANES), F32), pltpu.SemaphoreType.DMA],
+    )(index_table, weight_table, all_grad, early, other_part[0, :, :LANES])
+
+    query_weight_grad, mine = call(
+        sum_kernel,
+        (shape((8, width), F32), shape((chips, 8, 2 * half), BF16)),
+        in_specs=[vmem, vmem],
+        limit=16,
+    )(arrived, late_done)
+    first_key_grad, second_key_grad = call(
+        functools.partial(keys_kernel, heads),
+        (shape(first_keys.shape, F32), shape(second_keys.shape, F32)),
+        in_specs=[vmem, vmem, smem],
+        scratch_shapes=[pltpu.VMEM((chips // 4, 2, 2, 8, half), F32)],
+        limit=16,
+    )(mine, swap_core(mine), core)
     return (
         token_grad,
         query_weight_grad,
         gain_grad,
         shift_grad,
-        first_key_grad.reshape(heads, subkeys, half),
-        key_grad[1],
+        first_key_grad,
+        second_key_grad,
         value_grad.reshape(heads, rows_dev, width),
     )
 

time: 340 us -> 277 us (0.81)
  waiting for transfers between devices: 93 us -> 68.3 us
  starting transfers between devices: 79.8 us -> 55.4 us
  blocking collectives: 31.4 us -> 8.37 us
  Pallas kernels: 66.7 us -> 83.7 us
  other arithmetic: 11.3 us -> 4.47 us
    pallas_call x1 -> x6, Pallas kernels: 58.8 us -> 75.8 us  [the longest x1 26.9 us: per_device(): call(functools.partial(product_kernel, n, rows), shape((devices, LANES),...]
    all_to_all x5 -> x2, waiting for transfers between devices: 21.3 us -> 4.29 us  [everyone(): return lax.all_to_all(wide, axis, split_axis=0, concat_axis=0, tiled=True)]
    all_to_all x1 -> x0, blocking collectives: 16.4 us -> none  [scatter_sum(): lax.all_to_all(chips, CHIPS, split_axis=0, concat_axis=0, tiled=True)]
    all_to_all x5 -> x2, starting transfers between devices: 20.5 us -> 9.04 us  [everyone(): return lax.all_to_all(wide, axis, split_axis=0, concat_axis=0, tiled=True)]
    all_to_all x2 -> x3, waiting for transfers between devices: 19.6 us -> 8.83 us  [exchange(): return lax.all_to_all(value, axis, split_axis=0, concat_axis=0, tiled=True)]
    all_to_all x2 -> x3, starting transfers between devices: 32.3 us -> 21.5 us  [exchange(): return lax.all_to_all(value, axis, split_axis=0, concat_axis=0, tiled=True)]
    unnamed x50 -> x54, local copies, waits for them, and re-layouts: 21 us -> 31.3 us
    all_to_all x2 -> x1, blocking collectives: 15 us -> 8.37 us  [everyone(): return lax.all_to_all(wide, axis, split_axis=0, concat_axis=0, tiled=True)]
  transfers between devices with their start and end apart: 15 -> 13, of which waited for: 10 -> 9; matrix products, arithmetic and copies ran while one was open for 10% -> 7% of each run, Pallas kernels for 1% -> 17%
where the time goes in v2:
time: 277 us; the launch traced here: 275 us
  Pallas kernels  83.7 us (30%)
  waiting for transfers between devices  68.3 us (25%)
  starting transfers between devices  55.4 us (20%)
  local copies, waits for them, and re-layouts  37 us (13%)
  between operations  14.5 us (5%)
  blocking collectives  8.37 us (3%)
  other arithmetic  4.47 us (2%)
  matrix products  3 us (1%)
    all_gather x1, waiting for transfers between devices, per_device(): all_grad = lax.all_gather(tiles, ALL, axis=0, tiled=True)  45.8 us
    unnamed x54, local copies, waits for them, and re-layouts  31.3 us
    pallas_call x1, Pallas kernels, per_device(): call(functools.partial(product_kernel, n, rows), shape((devices, LANES),...  26.9 us
    pallas_call x1, Pallas kernels, per_device(): call(functools.partial(late_kernel, n, steps * GROUP), (shape((rows, widt...  26.2 us
    all_to_all x3, starting transfers between devices, exchange(): return lax.all_to_all(value, axis, split_axis=0, concat_axis=0, tiled=True)  21.5 us
    pallas_call x1, Pallas kernels, per_device(): call(functools.partial(early_kernel, n), (shape(((rows + CAP) * 8, LANES)...  16.1 us
    all_to_all x1, starting transfers between devices, per_device(): lax.all_to_all(slot_index.reshape(devices, 1, LANES), ALL, split_axis=0,...  9.08 us
    all_to_all x2, starting transfers between devices, everyone(): return lax.all_to_all(wide, axis, split_axis=0, concat_axis=0, tiled=True)  9.04 us
  transfers between devices with their start and end apart: 13, of which 9 were waited for; matrix products, arithmetic and copies ran while one was open for 7% of the time, Pallas kernels for 17%

profile of v2, /device:TPU:1, one launch (start us, length us, event | category | flops | bytes accessed | tf_op | source)
XLA Modules:
  0.0 274.7 jit_solution(5245019288071783864)
XLA Ops:
  13.2 8.4 %all_to_all.40 = f32[4,2,1024]{2,1,0:T(2,128)S(1)} all-to-all(f32[4,2,1024]{2,1,0:T(2,128)S(1)} %broadcast_in_dim.14), channel_id=1, replica_groups=mesh['x'=4,'z'=4,'y'=4,'c'=2] {'y'}, dimensions={0} | all-to-all | bytes 65536 | tf_op jit(solution)/shard_map/all_to_all | solution.py:345
  22.3 5.0 %all-to-all-start.2 = ((f32[4,2,1024]{2,1,0:T(2,128)}), f32[4,2,1024]{2,1,0:T(2,128)S(1)}, u32[]{:S(2)}, u32[]{:S(2)}) async-start(f32[4,2,1024]{2,1,0:T(2,128)} %broadcast_in_dim.15), calls=%async_computation.2 | async-start | bytes 65536 | tf_op jit(solution)/shard_map/all_to_all | solution.py:345
  27.3 4.3 %all-to-all-done.2 = f32[4,2,1024]{2,1,0:T(2,128)S(1)} async-done(((f32[4,2,1024]{2,1,0:T(2,128)}), f32[4,2,1024]{2,1,0:T(2,128)S(1)}, u32[]{:S(2)}, u32[]{:S(2)}) %all-to-all-start.2) | async-done | bytes 32800 | tf_op jit(solution)/shard_map/all_to_all | solution.py:345
  32.3 4.0 %all-to-all-start.3 = ((f32[4,2,1024]{2,1,0:T(2,128)}), f32[4,2,1024]{2,1,0:T(2,128)}, u32[]{:S(2)}, u32[]{:S(2)}) async-start(f32[4,2,1024]{2,1,0:T(2,128)} %broadcast_in_dim.16), calls=%async_computation.3 | async-start | bytes 65536 | tf_op jit(solution)/shard_map/all_to_all | solution.py:345
  41.8 9.1 %all-to-all-start = ((s32[128,1,128]{2,1,0:T(1,128)}), s32[128,1,128]{2,1,0:T(1,128)S(1)}, u32[]{:S(2)}, u32[]{:S(2)}) async-start(s32[128,1,128]{2,1,0:T(1,128)} %bitcast.114), calls=%async_computation | async-start | bytes 131072 | tf_op jit(solution)/shard_map/all_to_all | solution.py:391
  58.1 2.3 all-to-all-done
  60.4 7.4 %all-to-all-start.4 = ((f32[128,1,128]{2,1,0:T(1,128)}), f32[128,1,128]{2,1,0:T(1,128)S(1)}, u32[]{:S(2)}, u32[]{:S(2)}) async-start(f32[128,1,128]{2,1,0:T(1,128)} %bitcast.27), calls=%async_computation.4 | async-start | bytes 131072 | tf_op jit(solution)/shard_map/all_to_all | solution.py:406
  67.9 9.2 %copy.94 = bf16[512,8,8,128]{3,2,1,0:T(8,128)(2,1)} copy(bf16[512,8,8,128]{3,1,2,0:T(8,128)(2,1)} %bitcast.118) | data formatting | bytes 16777216
  77.4 45.8 %all-gather.2.cloned.1.call-done.grad_ref = bf16[16384,8,128]{2,1,0:T(8,128)(2,1)} async-done(((bf16[128,8,128]{2,1,0:T(8,128)(2,1)}), bf16[16384,8,128]{2,1,0:T(8,128)(2,1)}) %all-gather.2.cloned.1.call-update) | async-done | bytes 33554448 | tf_op jit(solution)/shard_map/all_gather | solution.py:375
  123.1 3.4 %copy-done.1 = bf16[512,8,8,128]{3,2,1,0:T(8,128)(2,1)S(1)} copy-done((bf16[512,8,8,128]{3,2,1,0:T(8,128)(2,1)S(1)}, bf16[512,8,8,128]{3,2,1,0:T(8,128)(2,1)}, u32[]{:S(2)}) %copy-start.1) | copy-done | bytes 8388632
  126.5 26.9 %shard_map.164 = f32[128,128]{1,0:T(8,128)} custom-call(s32[128,128]{1,0:T(8,128)S(1)} %bitcast.108, f32[128,128]{1,0:T(8,128)S(1)} %bitcast.111, bf16[16384,8,128]{2,1,0:T(8,128)(2,1)} %all-gather.2.cloned.1.call-done.grad_ref, bf16[4096,8,128]{2,1,0:T(8,128)(2,1)S(1)} %bitcast.105), custom_call_target="tpu_custom_call" | custom-call | tf_op jit(solution)/shard_map/pallas_call | solution.py:415
  153.4 7.1 %all-to-all-start.5 = ((f32[128,1,128]{2,1,0:T(1,128)}), f32[128,1,128]{2,1,0:T(1,128)}, u32[]{:S(2)}, u32[]{:S(2)}) async-start(f32[128,1,128]{2,1,0:T(1,128)} %bitcast.30), calls=%async_computation.5 | async-start | bytes 131072 | tf_op jit(solution)/shard_map/all_to_all | solution.py:359
  161.4 8.5 %all-to-all-done.5 = f32[128,1,128]{2,1,0:T(1,128)} async-done(((f32[128,1,128]{2,1,0:T(1,128)}), f32[128,1,128]{2,1,0:T(1,128)}, u32[]{:S(2)}, u32[]{:S(2)}) %all-to-all-start.5) | async-done | bytes 65568 | tf_op jit(solution)/shard_map/all_to_all | solution.py:359
  173.7 3.9 %shard_map.165 = (f32[128,1024]{1,0:T(8,128)S(1)}, f32[64,8,512]{2,1,0:T(8,128)S(1)}, f32[64,8,512]{2,1,0:T(8,128)S(1)}, f32[8,256]{1,0:T(8,128)S(1)}) custom-call(f32[128,128]{1,0:T(8,128)} %bitcast.31.back_ref, s32[128,32]{1,0:T(8,128)S(1)} %copy.72.shard_ref, s32[128,32]{1,0:T(8,128)S(1)} %copy.83.second_ids_ref, ...), custom_call_target="tpu_custom_call" | custom-call | tf_op jit(solution)/shard_map/pallas_call | solution.py:428
  182.4 5.5 %all-to-all-start.6 = ((f32[64,8,768]{2,1,0:T(8,128)}), f32[64,8,768]{2,1,0:T(8,128)}, u32[]{:S(2)}, u32[]{:S(2)}) async-start(f32[64,8,768]{2,1,0:T(8,128)} %pad_maximum_fusion), calls=%async_computation.6 | async-start | bytes 3145728 | tf_op jit(solution)/shard_map/all_to_all | solution.py:359
  188.0 16.1 %shard_map.166 = (f32[33088,128]{1,0:T(8,128)S(1)}, f32[8,128]{1,0:T(8,128)S(1)}) custom-call(s32[128,128]{1,0:T(8,128)S(1)} %bitcast.109, f32[128,128]{1,0:T(8,128)S(1)} %bitcast.112, bf16[16384,8,128]{2,1,0:T(8,128)(2,1)} %all-gather.2.cloned.1.call-done.grad_ref, f32[8,128]{1,0:T(8,128)S(1)} %slice.53.after_ref), custom_call_target="tpu_custom_call" | custom-call | tf_op jit(solution)/shard_map/pallas_call | solution.py:447
  204.1 5.8 %copy-done.2 = f32[33088,128]{1,0:T(8,128)} copy-done((f32[33088,128]{1,0:T(8,128)}, f32[33088,128]{1,0:T(8,128)S(1)}, u32[]{:S(2)}) %copy-start.2) | copy-done | bytes 16941080
  211.3 2.5 shard_map.167
  213.8 2.8 %collective-permute-start.3 = (f32[64,8,1024]{2,1,0:T(8,128)S(1)}, f32[64,8,1024]{2,1,0:T(8,128)S(1)}, u32[]{:S(2)}, u32[]{:S(2)}) collective-permute-start(f32[64,8,1024]{2,1,0:T(8,128)S(1)} %get-tuple-element.45), channel_id=1, source_target_pairs={{0,1},{1,0},{2,3},{3,2},{4,5},{5,4},{6,7},{7,6},{8,9},{9,8},{10,11... | collective-permute-start | bytes 6291464 | tf_op jit(solution)/shard_map/ppermute | solution.py:339
  216.6 3.8 %collective-permute-done.3 = f32[64,8,1024]{2,1,0:T(8,128)S(1)} collective-permute-done((f32[64,8,1024]{2,1,0:T(8,128)S(1)}, f32[64,8,1024]{2,1,0:T(8,128)S(1)}, u32[]{:S(2)}, u32[]{:S(2)}) %collective-permute-start.3) | collective-permute-done | bytes 2097184 | tf_op jit(solution)/shard_map/ppermute | solution.py:339
  223.0 8.9 %all-to-all-start.7 = ((bf16[64,8,1536]{2,1,0:T(8,128)(2,1)}), bf16[64,8,1536]{2,1,0:T(8,128)(2,1)}, u32[]{:S(2)}, u32[]{:S(2)}) async-start(bf16[64,8,1536]{2,1,0:T(8,128)(2,1)} %pad_maximum_fusion.1), calls=%async_computation.7 | async-start | bytes 3145728 | tf_op jit(solution)/shard_map/all_to_all | solution.py:359
  232.6 26.2 %shard_map.168 = (bf16[4096,1024]{1,0:T(8,128)(2,1)}, f32[8,128]{1,0:T(8,128)S(1)}) custom-call(s32[128,128]{1,0:T(8,128)S(1)} %bitcast.110, f32[128,128]{1,0:T(8,128)S(1)} %bitcast.113, bf16[16384,8,128]{2,1,0:T(8,128)(2,1)} %all-gather.2.cloned.1.call-done.grad_ref, f32[33088,128]{1,0:T(8,128)} %copy-done.2, f32[8,128]{1,0:T(8,128)S(1)} %slice_bitcast_fusion.after_ref), custom_call_target="tpu_custom_call" | custom-call | tf_op jit(solution)/shard_map/pallas_call | solution.py:476
  258.8 2.2 shard_map.169
  261.0 2.9 %collective-permute-start.4 = (bf16[64,8,512]{2,1,0:T(8,128)(2,1)S(1)}, bf16[64,8,512]{2,1,0:T(8,128)(2,1)S(1)}, u32[]{:S(2)}, u32[]{:S(2)}) collective-permute-start(bf16[64,8,512]{2,1,0:T(8,128)(2,1)S(1)} %get-tuple-element.51.mine_ref), channel_id=1, source_target_pairs={{0,1},{1,0},{2,3},{3,2},{4,5},{5,4},{6,7},{7,6},{8,9},{9,8},{10,11... | collective-permute-start | bytes 1572872 | tf_op jit(solution)/shard_map/ppermute | solution.py:339
  (111 shorter events, 38.3 us)
Async XLA Ops:
  7.2 115.9 %all-gather.2.cloned.1.call-start = ((), (), s32[]{:S(2)}) async-start(), calls=%async_computation.8 | async-start | bytes 33816576 | tf_op jit(solution)/shard_map/all_gather | solution.py:375
  9.1 18.2 %copy-start.25 = (s32[128,2,16]{0,2,1:T(8,128)S(1)}, s32[128,2,16]{0,2,1:T(8,128)}, u32[]{:S(2)}) copy-start(s32[128,2,16]{0,2,1:T(8,128)} %param.20) | copy-start | bytes 49156
  9.1 27.2 %copy-start.23 = (s32[128,2,16]{0,2,1:T(8,128)S(1)}, s32[128,2,16]{0,2,1:T(8,128)}, u32[]{:S(2)}) copy-start(s32[128,2,16]{0,2,1:T(8,128)} %param.21) | copy-start | bytes 49156
  9.1 27.3 %copy-start.24 = (s32[128,2,16]{0,2,1:T(8,128)S(1)}, s32[128,2,16]{0,2,1:T(8,128)}, u32[]{:S(2)}) copy-start(s32[128,2,16]{0,2,1:T(8,128)} %param.19) | copy-start | bytes 49156
  9.1 27.4 %copy-start.22 = (bf16[2,512,256]{2,1,0:T(8,128)(2,1)S(1)}, bf16[2,512,256]{2,1,0:T(8,128)(2,1)}, u32[]{:S(2)}) copy-start(bf16[2,512,256]{2,1,0:T(8,128)(2,1)} %param.16) | copy-start | bytes 1572868
  10.6 41.2 %copy-start.19 = (f32[1024]{0:T(1024)S(1)}, f32[1024]{0:T(1024)}, u32[]{:S(2)}) copy-start(f32[1024]{0:T(1024)} %param.14) | copy-start | bytes 12292
  10.6 41.2 %copy-start.20 = (f32[1024]{0:T(1024)S(1)}, f32[1024]{0:T(1024)}, u32[]{:S(2)}) copy-start(f32[1024]{0:T(1024)} %param.15) | copy-start | bytes 12292
  10.7 2.3 collective-permute-start
  22.3 9.3 %all-to-all-start.2 = ((f32[4,2,1024]{2,1,0:T(2,128)}), f32[4,2,1024]{2,1,0:T(2,128)S(1)}, u32[]{:S(2)}, u32[]{:S(2)}) async-start(f32[4,2,1024]{2,1,0:T(2,128)} %broadcast_in_dim.15), calls=%async_computation.2 | async-start | bytes 65536 | tf_op jit(solution)/shard_map/all_to_all | solution.py:345
  32.3 9.5 %all-to-all-start.3 = ((f32[4,2,1024]{2,1,0:T(2,128)}), f32[4,2,1024]{2,1,0:T(2,128)}, u32[]{:S(2)}, u32[]{:S(2)}) async-start(f32[4,2,1024]{2,1,0:T(2,128)} %broadcast_in_dim.16), calls=%async_computation.3 | async-start | bytes 65536 | tf_op jit(solution)/shard_map/all_to_all | solution.py:345
  41.8 18.6 %all-to-all-start = ((s32[128,1,128]{2,1,0:T(1,128)}), s32[128,1,128]{2,1,0:T(1,128)S(1)}, u32[]{:S(2)}, u32[]{:S(2)}) async-start(s32[128,1,128]{2,1,0:T(1,128)} %bitcast.114), calls=%async_computation | async-start | bytes 131072 | tf_op jit(solution)/shard_map/all_to_all | solution.py:391
  60.4 16.9 %all-to-all-start.4 = ((f32[128,1,128]{2,1,0:T(1,128)}), f32[128,1,128]{2,1,0:T(1,128)S(1)}, u32[]{:S(2)}, u32[]{:S(2)}) async-start(f32[128,1,128]{2,1,0:T(1,128)} %bitcast.27), calls=%async_computation.4 | async-start | bytes 131072 | tf_op jit(solution)/shard_map/all_to_all | solution.py:406
  126.5 43.4 %copy-start.4 = (bf16[2,512,256]{2,1,0:T(8,128)(2,1)S(1)}, bf16[2,512,256]{2,1,0:T(8,128)(2,1)}, u32[]{:S(2)}) copy-start(bf16[2,512,256]{2,1,0:T(8,128)(2,1)} %second_ref.3) | copy-start | bytes 1572868
  153.4 16.5 %all-to-all-start.5 = ((f32[128,1,128]{2,1,0:T(1,128)}), f32[128,1,128]{2,1,0:T(1,128)}, u32[]{:S(2)}, u32[]{:S(2)}) async-start(f32[128,1,128]{2,1,0:T(1,128)} %bitcast.30), calls=%async_computation.5 | async-start | bytes 131072 | tf_op jit(solution)/shard_map/all_to_all | solution.py:359
  177.6 3.6 %copy-start.9 = (f32[128,1024]{1,0:T(8,128)}, f32[128,1024]{1,0:T(8,128)S(1)}, u32[]{:S(2)}) copy-start(f32[128,1024]{1,0:T(8,128)S(1)} %get-tuple-element.41.query_grad_ref) | copy-start | bytes 1572868
  177.6 3.3 %collective-permute-start.2 = (f32[64,8,512]{2,1,0:T(8,128)S(1)}, f32[64,8,512]{2,1,0:T(8,128)S(1)}, u32[]{:S(2)}, u32[]{:S(2)}) collective-permute-start(f32[64,8,512]{2,1,0:T(8,128)S(1)} %get-tuple-element.40), channel_id=1, source_target_pairs={{0,1},{1,0},{2,3},{3,2},{4,5},{5,4},{6,7},{7,6},{8,9},{9,8},{10,11... | collective-permute-start | bytes 3145736 | tf_op jit(solution)/shard_map/ppermute | solution.py:339
  178.6 2.3 collective-permute-start.1
  182.4 27.8 %all-to-all-start.6 = ((f32[64,8,768]{2,1,0:T(8,128)}), f32[64,8,768]{2,1,0:T(8,128)}, u32[]{:S(2)}, u32[]{:S(2)}) async-start(f32[64,8,768]{2,1,0:T(8,128)} %pad_maximum_fusion), calls=%async_computation.6 | async-start | bytes 3145728 | tf_op jit(solution)/shard_map/all_to_all | solution.py:359
  187.9 22.3 %copy-start.7 = (f32[128,1024]{1,0:T(8,128)S(1)}, f32[128,1024]{1,0:T(8,128)}, u32[]{:S(2)}) copy-start(f32[128,1024]{1,0:T(8,128)} %copy-done.5) | copy-start | bytes 1572868
  187.9 22.3 %copy-start.8 = (bf16[128,1024]{1,0:T(8,128)(2,1)S(1)}, bf16[128,1024]{1,0:T(8,128)(2,1)}, u32[]{:S(2)}) copy-start(bf16[128,1024]{1,0:T(8,128)(2,1)} %tokens_ref.1) | copy-start | bytes 786436
  204.1 5.8 %copy-start.2 = (f32[33088,128]{1,0:T(8,128)}, f32[33088,128]{1,0:T(8,128)S(1)}, u32[]{:S(2)}) copy-start(f32[33088,128]{1,0:T(8,128)S(1)} %get-tuple-element.47.early_ref) | copy-start | bytes 50823172
  213.8 6.6 %collective-permute-start.3 = (f32[64,8,1024]{2,1,0:T(8,128)S(1)}, f32[64,8,1024]{2,1,0:T(8,128)S(1)}, u32[]{:S(2)}, u32[]{:S(2)}) collective-permute-start(f32[64,8,1024]{2,1,0:T(8,128)S(1)} %get-tuple-element.45), channel_id=1, source_target_pairs={{0,1},{1,0},{2,3},{3,2},{4,5},{5,4},{6,7},{7,6},{8,9},{9,8},{10,11... | collective-permute-start | bytes 6291464 | tf_op jit(solution)/shard_map/ppermute | solution.py:339
  223.0 35.8 %all-to-all-start.7 = ((bf16[64,8,1536]{2,1,0:T(8,128)(2,1)}), bf16[64,8,1536]{2,1,0:T(8,128)(2,1)}, u32[]{:S(2)}, u32[]{:S(2)}) async-start(bf16[64,8,1536]{2,1,0:T(8,128)(2,1)} %pad_maximum_fusion.1), calls=%async_computation.7 | async-start | bytes 3145728 | tf_op jit(solution)/shard_map/all_to_all | solution.py:359
  261.0 5.0 %collective-permute-start.4 = (bf16[64,8,512]{2,1,0:T(8,128)(2,1)S(1)}, bf16[64,8,512]{2,1,0:T(8,128)(2,1)S(1)}, u32[]{:S(2)}, u32[]{:S(2)}) collective-permute-start(bf16[64,8,512]{2,1,0:T(8,128)(2,1)S(1)} %get-tuple-element.51.mine_ref), channel_id=1, source_target_pairs={{0,1},{1,0},{2,3},{3,2},{4,5},{5,4},{6,7},{7,6},{8,9},{9,8},{10,11... | collective-permute-start | bytes 1572872 | tf_op jit(solution)/shard_map/ppermute | solution.py:339
  (15 other events, 16.9 us)
Sparse Core Ops, SparseCore 0:
  11.6 111.5 all-gather.1

commit v3 on v2

--- a/solution.py
+++ b/solution.py
@@ -12,6 +12,7 @@
 CHIPS = ("x", "z", "y")
 CAP = 40
 GROUP = 8
+BLOCK = 1024
 LANES = 128
 NT = (((1,), (1,)), ((), ()))
 TN = (((0,), (0,)), ((), ()))
@@ -30,8 +31,9 @@
     return lines
 
 
-def slots_kernel(heads, top, shard_ref, code_ref, pos_ref, dense_ref, slot_ref):
+def slots_kernel(heads, top, shard_ref, code_ref, place_ref, pos_ref, dense_ref, slot_ref):
     n = shard_ref.shape[0]
+    offset = place_ref[0]
     lane = iota((n, LANES), 1)
     row = iota((n, LANES), 0)
     below = (iota((n, n), 1) < iota((n, n), 0)).astype(BF16)
@@ -48,17 +50,17 @@
         before = before + jnp.sum(ones, axis=0, keepdims=True)
         place = jnp.where(hit, place, -1.0)
         pos.append(place)
-        packed.append(((h * 2048 + code) * n + row + 1).astype(F32))
+        packed.append(((h * 2048 + code) * BLOCK + offset + row + 1).astype(F32))
         pos_ref[h * n : (h + 1) * n, :] = place
         dense_ref[h * n : (h + 1) * n, :] = code
     table = jnp.concatenate(slot_table(pos, packed)[:CAP], axis=0).astype(I32) - 1
-    table = jnp.where(table < 0, (heads * 2048 + iota((CAP, LANES), 0)) * n, table)
+    table = jnp.where(table < 0, (heads * 2048 + iota((CAP, LANES), 0)) * BLOCK, table)
     clash = jnp.zeros((8, LANES), I32)
     for b in range(CAP // 8):
-        target = table[b * 8 : b * 8 + 8, :] >> 7
+        target = table[b * 8 : b * 8 + 8, :] >> 10
         for d in range(1, 5):
             clash = jnp.where(pltpu.roll(target, d, 0) == target, 1, clash)
-    clash = jnp.max(clash.astype(F32), axis=0, keepdims=True)
+    clash = jnp.max(clash.astype(F32), axis=0, keepdims=True) * BLOCK
     rest = jnp.zeros((LANES - CAP - 1, LANES), F32)
     slot_ref[...] = jnp.concatenate([table.astype(F32), clash, rest], axis=0).T.astype(I32)
 
@@ -104,21 +106,20 @@
     slot_ref[...] = jnp.concatenate(slot_table(pos, weights), axis=0).T
 
 
-def slot_of(index_ref, weight_ref, grad_ref, sender, g, j, tokens):
-    packed = index_ref[sender, j]
-    grad = grad_ref[g * tokens + (packed & (tokens - 1))].astype(F32)
+def slot_of(row_ref, token_ref, weight_ref, grad_ref, sender, j):
+    grad = grad_ref[token_ref[sender, j]].astype(F32)
     message = (grad * weight_ref[sender, j]).astype(BF16).astype(F32)
-    return packed >> 7, message
-
-
-def product_kernel(tokens, rows, index_ref, weight_ref, grad_ref, value_ref, product_ref, held):
+    return row_ref[sender, j], message
+
+
+def product_kernel(row_ref, token_ref, weight_ref, grad_ref, value_ref, product_ref, held):
     step = pl.program_id(0)
     eye = iota((CAP, LANES), 0) == iota((CAP, LANES), 1)
 
     def one_sender(g, carry):
         for j in range(CAP):
-            row, message = slot_of(index_ref, weight_ref, grad_ref, step * GROUP + g, g, j, tokens)
-            value = value_ref[row & (rows - 1)].astype(F32)
+            row, message = slot_of(row_ref, token_ref, weight_ref, grad_ref, step * GROUP + g, j)
+            value = value_ref[row].astype(F32)
             held[pl.ds(pl.multiple_of((g * CAP + j) * 8, 8), 8), :] = message * value
         return carry
 
@@ -135,16 +136,16 @@
     return pl.ds(pl.multiple_of(row * 8, 8), 8)
 
 
-def add_messages(tokens, first, index_ref, weight_ref, grad_ref, total):
+def add_messages(first, row_ref, token_ref, weight_ref, grad_ref, total):
     def one_sender(g, carry):
         sender = first + g
-        clash = index_ref[sender, CAP]
+        clash = row_ref[sender, CAP]
 
         @pl.when(clash == 0)
         def _():
             for b in range(CAP // 8):
                 slots = [
-                    slot_of(index_ref, weight_ref, grad_ref, sender, g, b * 8 + u, tokens) for u in range(8)
+                    slot_of(row_ref, token_ref, weight_ref, grad_ref, sender, b * 8 + u) for u in range(8)
                 ]
                 sums = [total[spot(row), :] + message for row, message in slots]
                 for (row, _), value in zip(slots, sums):
@@ -153,7 +154,7 @@
         @pl.when(clash != 0)
         def _():
             def one(j, inner):
-                row, message = slot_of(index_ref, weight_ref, grad_ref, sender, g, j, tokens)
+                row, message = slot_of(row_ref, token_ref, weight_ref, grad_ref, sender, j)
                 total[spot(row), :] += message
                 return inner
 
@@ -173,7 +174,7 @@
     lax.fori_loop(0, total.shape[0] // 352, clear, 0)
 
 
-def early_kernel(tokens, index_ref, weight_ref, grad_ref, after_ref, total, done_ref):
+def early_kernel(row_ref, token_ref, weight_ref, grad_ref, after_ref, total, done_ref):
     step = pl.program_id(0)
     done_ref[...] = jnp.zeros((8, LANES), F32)
 
@@ -181,11 +182,11 @@
     def _():
         clear_all(total)
 
-    add_messages(tokens, step * GROUP, index_ref, weight_ref, grad_ref, total)
+    add_messages(step * GROUP, row_ref, token_ref, weight_ref, grad_ref, total)
 
 
 def late_kernel(
-    tokens, senders, index_ref, weight_ref, grad_ref, early_ref, after_ref, out_ref, done_ref, total, sem
+    senders, row_ref, token_ref, weight_ref, grad_ref, early_ref, after_ref, out_ref, done_ref, total, sem
 ):
     step = pl.program_id(0)
     done_ref[...] = jnp.zeros((8, LANES), F32)
@@ -196,7 +197,7 @@
         copy.start()
         copy.wait()
 
-    add_messages(tokens, senders + step * GROUP, index_ref, weight_ref, grad_ref, total)
+    add_messages(senders + step * GROUP, row_ref, token_ref, weight_ref, grad_ref, total)
 
     @pl.when(step == pl.num_programs(0) - 1)
     def _():
@@ -384,10 +385,15 @@
     shard_ids = pick_shard.reshape(n, heads * top)
     second_ids = pick_second.reshape(n, heads * top)
     code = pick_low.reshape(n, heads * top) * subkeys + second_ids
+    vmem = pl.BlockSpec(memory_space=pltpu.VMEM)
+    smem = pl.BlockSpec(memory_space=pltpu.SMEM)
+    hbm = pl.BlockSpec(memory_space=pltpu.HBM)
+    place = jnp.reshape(lax.axis_index(ALL) % GROUP * n, (1,)).astype(I32)
     pos, dense, slot_index = call(
         functools.partial(slots_kernel, heads, top),
         (shape((heads * n, LANES), F32), shape((heads * n, LANES), I32), shape((devices, LANES), I32)),
-    )(shard_ids, code)
+        in_specs=[vmem, vmem, smem],
+    )(shard_ids, code, place)
     slot_index = lax.all_to_all(slot_index.reshape(devices, 1, LANES), ALL, split_axis=0, concat_axis=0, tiled=True)
 
     first_split = first_keys.reshape(heads, devices, subkeys // devices, half).swapaxes(1, 2)
@@ -405,22 +411,21 @@
     )
     slot_weight = lax.all_to_all(slot_weight.reshape(devices, 1, LANES), ALL, split_axis=0, concat_axis=0, tiled=True)
 
-    vmem = pl.BlockSpec(memory_space=pltpu.VMEM)
-    smem = pl.BlockSpec(memory_space=pltpu.SMEM)
-    hbm = pl.BlockSpec(memory_space=pltpu.HBM)
     value_tiles = values.reshape(rows, 8, width // 8)
-    index_table = slot_index.reshape(devices, LANES)
+    slot_index = slot_index.reshape(devices, LANES)
+    row_table = slot_index >> 10
+    token_table = slot_index & (BLOCK - 1)
     weight_table = slot_weight.reshape(devices, LANES)
     grad_spec = pl.BlockSpec((GROUP * n, 8, width // 8), lambda i: (i, 0, 0))
     product = call(
-        functools.partial(product_kernel, n, rows),
+        product_kernel,
         shape((devices, LANES), F32),
         limit=28,
         grid=(devices // GROUP,),
-        in_specs=[smem, smem, grad_spec, vmem],
+        in_specs=[smem, smem, smem, grad_spec, vmem],
         out_specs=pl.BlockSpec((GROUP, LANES), lambda i: (i, 0)),
         scratch_shapes=[pltpu.VMEM((GROUP * CAP * 8, LANES), F32)],
-    )(index_table, weight_table, all_grad, value_tiles)
+    )(row_table & (rows - 1), token_table, weight_table, all_grad, value_tiles)
     returned = exchange(product.reshape(devices, 1, LANES), ALL)
 
     chips = devices // 2
@@ -443,15 +448,16 @@
     sums = jnp.broadcast_to((sums + sums_in)[None], (chips, 8, half))
     sent = jnp.concatenate([sums, own_keys + keys_in], axis=2)
     arrived = exchange(sent, CHIPS)
-    steps = devices // GROUP // 2
+    steps = 10
+    rest = devices // GROUP - steps
     early, early_done = call(
-        functools.partial(early_kernel, n),
+        early_kernel,
         (shape(((rows + CAP) * 8, LANES), F32), shape((8, LANES), F32)),
         limit=32,
         grid=(steps,),
-        in_specs=[smem, smem, grad_spec, vmem],
+        in_specs=[smem, smem, smem, grad_spec, vmem],
         out_specs=[vmem, vmem],
-    )(index_table, weight_table, all_grad, sent[0, :, :LANES])
+    )(row_table, token_table, weight_table, all_grad, sent[0, :, :LANES])
 
     raw_grad, own_part, other_part, sums, key_block = call(
         functools.partial(tail_kernel, everything),
@@ -474,11 +480,12 @@
     arrived = exchange(sent, CHIPS)
     token_grad = lax.dot_general(raw_grad, query_weight, NT, preferred_element_type=F32).astype(BF16)
     value_grad, late_done = call(
-        functools.partial(late_kernel, n, steps * GROUP),
+        functools.partial(late_kernel, steps * GROUP),
         (shape((rows, width), BF16), shape((8, LANES), F32)),
         limit=50,
-        grid=(steps,),
+        grid=(rest,),
         in_specs=[
+            smem,
             smem,
             smem,
             pl.BlockSpec((GROUP * n, 8, width // 8), lambda i: (i + steps, 0, 0)),
@@ -487,7 +494,7 @@
         ],
         out_specs=[vmem, vmem],
         scratch_shapes=[pltpu.VMEM(((rows + CAP) * 8, LANES), F32), pltpu.SemaphoreType.DMA],
-    )(index_table, weight_table, all_grad, early, other_part[0, :, :LANES])
+    )(row_table, token_table, weight_table, all_grad, early, other_part[0, :, :LANES])
 
     query_weight_grad, mine = call(
         sum_kernel,

time: 277 us -> 276 us (level)
  blocking collectives: 8.37 us -> 0 us
  local copies, waits for them, and re-layouts: 37 us -> 41.3 us
  other arithmetic: 4.47 us -> 8.26 us
    all_gather x1, waiting for transfers between devices: 45.8 us -> 29.9 us  [per_device(): all_grad = lax.all_gather(tiles, ALL, axis=0, tiled=True)]
    all_to_all x1 -> x0, blocking collectives: 8.37 us -> none  [everyone(): return lax.all_to_all(wide, axis, split_axis=0, concat_axis=0, tiled=True)]
    all_to_all x1, waiting for transfers between devices: 0.27 us -> 8.26 us  [per_device(): lax.all_to_all(slot_weight.reshape(devices, 1, LANES), ALL, split_axis=0,...]
    all_to_all x1, waiting for transfers between devices: 2.3 us -> 7.9 us  [per_device(): lax.all_to_all(slot_index.reshape(devices, 1, LANES), ALL, split_axis=0,...]
    all_to_all x2 -> x3, starting transfers between devices: 9.04 us -> 13.2 us  [everyone(): return lax.all_to_all(wide, axis, split_axis=0, concat_axis=0, tiled=True)]
    all_to_all x2 -> x3, waiting for transfers between devices: 4.29 us -> 7.78 us  [everyone(): return lax.all_to_all(wide, axis, split_axis=0, concat_axis=0, tiled=True)]
    ppermute x5, starting transfers between devices: 8.27 us -> 5.06 us  [swap_core(): return lax.ppermute(value, 'c', [(0, 1), (1, 0)])]
    unnamed x54 -> x64, local copies, waits for them, and re-layouts: 31.3 us -> 33.6 us
  transfers between devices with their start and end apart: 13 -> 14, of which waited for: 9 -> 9; matrix products, arithmetic and copies ran while one was open for 7% -> 9% of each run, Pallas kernels for 17% -> 17%
where the time goes in v3:
time: 276 us; the launch traced here: 274 us
  Pallas kernels  81.4 us (29%)
  waiting for transfers between devices  68.4 us (25%)
  starting transfers between devices  57.5 us (21%)
  local copies, waits for them, and re-layouts  41.3 us (15%)
  between operations  14.5 us (5%)
  other arithmetic  8.26 us (3%)
  matrix products  3 us (1%)
    unnamed x64, local copies, waits for them, and re-layouts  33.6 us
    all_gather x1, waiting for transfers between devices, per_device(): all_grad = lax.all_gather(tiles, ALL, axis=0, tiled=True)  29.9 us
    pallas_call x1, Pallas kernels, per_device(): call(product_kernel, shape((devices, LANES), F32), limit=28, grid=(device...  24.8 us
    pallas_call x1, Pallas kernels, per_device(): call(functools.partial(late_kernel, steps * GROUP), (shape((rows, width),...  24.6 us
    all_to_all x3, starting transfers between devices, exchange(): return lax.all_to_all(value, axis, split_axis=0, concat_axis=0, tiled=True)  23.9 us
    pallas_call x1, Pallas kernels, per_device(): call(early_kernel, (shape(((rows + CAP) * 8, LANES), F32), shape((8, LANE...  18.1 us
    all_to_all x3, starting transfers between devices, everyone(): return lax.all_to_all(wide, axis, split_axis=0, concat_axis=0, tiled=True)  13.2 us
    all_to_all x1, starting transfers between devices, per_device(): lax.all_to_all(slot_index.reshape(devices, 1, LANES), ALL, split_axis=0,...  9.47 us
  transfers between devices with their start and end apart: 14, of which 9 were waited for; matrix products, arithmetic and copies ran while one was open for 9% of the time, Pallas kernels for 17%

profile of v3, /device:TPU:1, one launch (start us, length us, event | category | flops | bytes accessed | tf_op | source)
XLA Modules:
  0.0 274.3 jit_solution(17427492697106952994)
XLA Ops:
  13.8 4.3 %all-to-all-start.1 = ((f32[4,2,1024]{2,1,0:T(2,128)}), f32[4,2,1024]{2,1,0:T(2,128)S(1)}, u32[]{:S(2)}, u32[]{:S(2)}) async-start(f32[4,2,1024]{2,1,0:T(2,128)} %broadcast_in_dim.14), calls=%async_computation.1 | async-start | bytes 65536 | tf_op jit(solution)/shard_map/all_to_all | solution.py:346
  18.0 4.3 %all-to-all-done.1 = f32[4,2,1024]{2,1,0:T(2,128)S(1)} async-done(((f32[4,2,1024]{2,1,0:T(2,128)}), f32[4,2,1024]{2,1,0:T(2,128)S(1)}, u32[]{:S(2)}, u32[]{:S(2)}) %all-to-all-start.1) | async-done | bytes 32800 | tf_op jit(solution)/shard_map/all_to_all | solution.py:346
  23.1 5.0 %all-to-all-start.2 = ((f32[4,2,1024]{2,1,0:T(2,128)}), f32[4,2,1024]{2,1,0:T(2,128)}, u32[]{:S(2)}, u32[]{:S(2)}) async-start(f32[4,2,1024]{2,1,0:T(2,128)} %broadcast_in_dim.15), calls=%async_computation.2 | async-start | bytes 65536 | tf_op jit(solution)/shard_map/all_to_all | solution.py:346
  30.4 9.0 %copy.102 = bf16[512,8,8,128]{3,2,1,0:T(8,128)(2,1)} copy(bf16[512,8,8,128]{3,1,2,0:T(8,128)(2,1)} %bitcast.125) | data formatting | bytes 16777216
  42.0 9.5 %all-to-all-start = ((s32[128,1,128]{2,1,0:T(1,128)}), s32[128,1,128]{2,1,0:T(1,128)S(1)}, u32[]{:S(2)}, u32[]{:S(2)}) async-start(s32[128,1,128]{2,1,0:T(1,128)} %bitcast.120), calls=%async_computation | async-start | bytes 131072 | tf_op jit(solution)/shard_map/all_to_all | solution.py:397
  53.0 7.9 %all-to-all-done = s32[128,1,128]{2,1,0:T(1,128)S(1)} async-done(((s32[128,1,128]{2,1,0:T(1,128)}), s32[128,1,128]{2,1,0:T(1,128)S(1)}, u32[]{:S(2)}, u32[]{:S(2)}) %all-to-all-start) | async-done | bytes 65568 | tf_op jit(solution)/shard_map/all_to_all | solution.py:397
  62.2 3.9 %all-to-all-start.3 = ((f32[4,2,1024]{2,1,0:T(2,128)}), f32[4,2,1024]{2,1,0:T(2,128)}, u32[]{:S(2)}, u32[]{:S(2)}) async-start(f32[4,2,1024]{2,1,0:T(2,128)} %broadcast_in_dim.16), calls=%async_computation.3 | async-start | bytes 65536 | tf_op jit(solution)/shard_map/all_to_all | solution.py:346
  67.0 3.5 %all-to-all-done.3 = f32[4,2,1024]{2,1,0:T(2,128)} async-done(((f32[4,2,1024]{2,1,0:T(2,128)}), f32[4,2,1024]{2,1,0:T(2,128)}, u32[]{:S(2)}, u32[]{:S(2)}) %all-to-all-start.3) | async-done | bytes 32800 | tf_op jit(solution)/shard_map/all_to_all | solution.py:346
  77.9 5.9 %all-to-all-start.4 = ((f32[128,1,128]{2,1,0:T(1,128)}), f32[128,1,128]{2,1,0:T(1,128)S(1)}, u32[]{:S(2)}, u32[]{:S(2)}) async-start(f32[128,1,128]{2,1,0:T(1,128)} %bitcast.121), calls=%async_computation.4 | async-start | bytes 131072 | tf_op jit(solution)/shard_map/all_to_all | solution.py:412
  85.3 8.3 %all-to-all-done.4 = f32[128,1,128]{2,1,0:T(1,128)S(1)} async-done(((f32[128,1,128]{2,1,0:T(1,128)}), f32[128,1,128]{2,1,0:T(1,128)S(1)}, u32[]{:S(2)}, u32[]{:S(2)}) %all-to-all-start.4) | async-done | bytes 65568 | tf_op jit(solution)/shard_map/all_to_all | solution.py:412
  93.5 29.9 %all-gather.2.cloned.1.call-done.grad_ref = bf16[16384,8,128]{2,1,0:T(8,128)(2,1)} async-done(((bf16[128,8,128]{2,1,0:T(8,128)(2,1)}), bf16[16384,8,128]{2,1,0:T(8,128)(2,1)}) %all-gather.2.cloned.1.call-update) | async-done | bytes 33554448 | tf_op jit(solution)/shard_map/all_gather | solution.py:376
  123.4 3.4 %copy-done.1 = bf16[512,8,8,128]{3,2,1,0:T(8,128)(2,1)S(1)} copy-done((bf16[512,8,8,128]{3,2,1,0:T(8,128)(2,1)S(1)}, bf16[512,8,8,128]{3,2,1,0:T(8,128)(2,1)}, u32[]{:S(2)}) %copy-start.1) | copy-done | bytes 8388632
  127.6 24.8 %shard_map.164 = f32[128,128]{1,0:T(8,128)S(1)} custom-call(s32[128,128]{1,0:T(8,128)S(1)} %copy-done.14, s32[128,128]{1,0:T(8,128)S(1)} %get-tuple-element.58.token_ref, f32[128,128]{1,0:T(8,128)S(1)} %bitcast.116, bf16[16384,8,128]{2,1,0:T(8,128)(2,1)} %all-gather.2.cloned.1.call-done.grad_ref, bf16[4096,8,128]{2,1,0:T(8,128)(2,1)S(1)} %bitcast.113), custom_call_target="tpu_custom_call" | custom-call | tf_op jit(solution)/shard_map/pallas_call | solution.py:420
  153.1 7.7 %all-to-all-start.5 = ((f32[128,1,128]{2,1,0:T(1,128)}), f32[128,1,128]{2,1,0:T(1,128)}, u32[]{:S(2)}, u32[]{:S(2)}) async-start(f32[128,1,128]{2,1,0:T(1,128)} %bitcast.119), calls=%async_computation.5 | async-start | bytes 131072 | tf_op jit(solution)/shard_map/all_to_all | solution.py:360
  162.2 7.7 %all-to-all-done.5 = f32[128,1,128]{2,1,0:T(1,128)} async-done(((f32[128,1,128]{2,1,0:T(1,128)}), f32[128,1,128]{2,1,0:T(1,128)}, u32[]{:S(2)}, u32[]{:S(2)}) %all-to-all-start.5) | async-done | bytes 65568 | tf_op jit(solution)/shard_map/all_to_all | solution.py:360
  174.6 3.9 %shard_map.165 = (f32[128,1024]{1,0:T(8,128)S(1)}, f32[64,8,512]{2,1,0:T(8,128)S(1)}, f32[64,8,512]{2,1,0:T(8,128)S(1)}, f32[8,256]{1,0:T(8,128)S(1)}) custom-call(f32[128,128]{1,0:T(8,128)} %bitcast.35.back_ref, s32[128,32]{1,0:T(8,128)S(1)} %copy.78.shard_ref, s32[128,32]{1,0:T(8,128)S(1)} %copy-done.18, f32[256,128]{1,0:T(8,128)S(1)} %get-tuple-element.32.pos_ref, ...), custom_call_target="tpu_custom_call" | custom-call | tf_op jit(solution)/shard_map/pallas_call | solution.py:433
  183.6 5.5 %all-to-all-start.6 = ((f32[64,8,768]{2,1,0:T(8,128)}), f32[64,8,768]{2,1,0:T(8,128)}, u32[]{:S(2)}, u32[]{:S(2)}) async-start(f32[64,8,768]{2,1,0:T(8,128)} %pad_maximum_fusion), calls=%async_computation.6 | async-start | bytes 3145728 | tf_op jit(solution)/shard_map/all_to_all | solution.py:360
  189.1 18.1 %shard_map.166 = (f32[33088,128]{1,0:T(8,128)S(1)}, f32[8,128]{1,0:T(8,128)S(1)}) custom-call(s32[128,128]{1,0:T(8,128)S(1)} %get-tuple-element.57.row_ref, s32[128,128]{1,0:T(8,128)S(1)} %get-tuple-element.58.token_ref, f32[128,128]{1,0:T(8,128)S(1)} %bitcast.117, bf16[16384,8,128]{2,1,0:T(8,128)(2,1)} %all-gather.2.cloned.1.call-done.grad_ref, ...), custom_call_target="tpu_custom_call" | custom-call | tf_op jit(solution)/shard_map/pallas_call | solution.py:453
  207.2 5.8 %copy-done.2 = f32[33088,128]{1,0:T(8,128)} copy-done((f32[33088,128]{1,0:T(8,128)}, f32[33088,128]{1,0:T(8,128)S(1)}, u32[]{:S(2)}) %copy-start.2) | copy-done | bytes 16941080
  214.1 2.5 shard_map.167
  217.8 3.8 %collective-permute-done.3 = f32[64,8,1024]{2,1,0:T(8,128)S(1)} collective-permute-done((f32[64,8,1024]{2,1,0:T(8,128)S(1)}, f32[64,8,1024]{2,1,0:T(8,128)S(1)}, u32[]{:S(2)}, u32[]{:S(2)}) %collective-permute-start.3) | collective-permute-done | bytes 2097184 | tf_op jit(solution)/shard_map/ppermute | solution.py:340
  224.2 10.7 %all-to-all-start.7 = ((bf16[64,8,1536]{2,1,0:T(8,128)(2,1)}), bf16[64,8,1536]{2,1,0:T(8,128)(2,1)}, u32[]{:S(2)}, u32[]{:S(2)}) async-start(bf16[64,8,1536]{2,1,0:T(8,128)(2,1)} %pad_maximum_fusion.1), calls=%async_computation.7 | async-start | bytes 3145728 | tf_op jit(solution)/shard_map/all_to_all | solution.py:360
  235.6 24.6 %shard_map.168 = (bf16[4096,1024]{1,0:T(8,128)(2,1)}, f32[8,128]{1,0:T(8,128)S(1)}) custom-call(s32[128,128]{1,0:T(8,128)S(1)} %get-tuple-element.57.row_ref, s32[128,128]{1,0:T(8,128)S(1)} %get-tuple-element.58.token_ref, f32[128,128]{1,0:T(8,128)S(1)} %bitcast.118, bf16[16384,8,128]{2,1,0:T(8,128)(2,1)} %all-gather.2.cloned.1.call-done.grad_ref, ...), custom_call_target="tpu_custom_call" | custom-call | tf_op jit(solution)/shard_map/pallas_call | solution.py:482
  260.2 2.2 shard_map.169
  (124 shorter events, 47.7 us)
Async XLA Ops:
  7.2 116.2 %all-gather.2.cloned.1.call-start = ((), (), s32[]{:S(2)}) async-start(), calls=%async_computation.8 | async-start | bytes 33816576 | tf_op jit(solution)/shard_map/all_gather | solution.py:376
  9.1 9.0 %copy-start.30 = (s32[128,2,16]{0,2,1:T(8,128)S(1)}, s32[128,2,16]{0,2,1:T(8,128)}, u32[]{:S(2)}) copy-start(s32[128,2,16]{0,2,1:T(8,128)} %param.20) | copy-start | bytes 49156
  9.1 19.0 %copy-start.28 = (s32[128,2,16]{0,2,1:T(8,128)S(1)}, s32[128,2,16]{0,2,1:T(8,128)}, u32[]{:S(2)}) copy-start(s32[128,2,16]{0,2,1:T(8,128)} %param.21) | copy-start | bytes 49156
  9.1 19.1 %copy-start.29 = (s32[128,2,16]{0,2,1:T(8,128)S(1)}, s32[128,2,16]{0,2,1:T(8,128)}, u32[]{:S(2)}) copy-start(s32[128,2,16]{0,2,1:T(8,128)} %param.19) | copy-start | bytes 49156
  9.1 19.2 %copy-start.27 = (bf16[2,512,256]{2,1,0:T(8,128)(2,1)S(1)}, bf16[2,512,256]{2,1,0:T(8,128)(2,1)}, u32[]{:S(2)}) copy-start(bf16[2,512,256]{2,1,0:T(8,128)(2,1)} %param.16) | copy-start | bytes 1572868
  10.7 2.3 collective-permute-start
  13.8 8.6 %all-to-all-start.1 = ((f32[4,2,1024]{2,1,0:T(2,128)}), f32[4,2,1024]{2,1,0:T(2,128)S(1)}, u32[]{:S(2)}, u32[]{:S(2)}) async-start(f32[4,2,1024]{2,1,0:T(2,128)} %broadcast_in_dim.14), calls=%async_computation.1 | async-start | bytes 65536 | tf_op jit(solution)/shard_map/all_to_all | solution.py:346
  23.1 18.9 %all-to-all-start.2 = ((f32[4,2,1024]{2,1,0:T(2,128)}), f32[4,2,1024]{2,1,0:T(2,128)}, u32[]{:S(2)}, u32[]{:S(2)}) async-start(f32[4,2,1024]{2,1,0:T(2,128)} %broadcast_in_dim.15), calls=%async_computation.2 | async-start | bytes 65536 | tf_op jit(solution)/shard_map/all_to_all | solution.py:346
  30.4 41.0 %copy-start.23 = (f32[1024]{0:T(1024)S(1)}, f32[1024]{0:T(1024)}, u32[]{:S(2)}) copy-start(f32[1024]{0:T(1024)} %param.14) | copy-start | bytes 12292
  30.4 41.0 %copy-start.24 = (f32[1024]{0:T(1024)S(1)}, f32[1024]{0:T(1024)}, u32[]{:S(2)}) copy-start(f32[1024]{0:T(1024)} %param.15) | copy-start | bytes 12292
  42.0 24.1 %copy-start.11 = (s32[256,128]{1,0:T(8,128)}, s32[256,128]{1,0:T(8,128)S(1)}, u32[]{:S(2)}) copy-start(s32[256,128]{1,0:T(8,128)S(1)} %get-tuple-element.33.dense_ref) | copy-start | bytes 393220
  42.0 18.9 %all-to-all-start = ((s32[128,1,128]{2,1,0:T(1,128)}), s32[128,1,128]{2,1,0:T(1,128)S(1)}, u32[]{:S(2)}, u32[]{:S(2)}) async-start(s32[128,1,128]{2,1,0:T(1,128)} %bitcast.120), calls=%async_computation | async-start | bytes 131072 | tf_op jit(solution)/shard_map/all_to_all | solution.py:397
  62.2 8.2 %all-to-all-start.3 = ((f32[4,2,1024]{2,1,0:T(2,128)}), f32[4,2,1024]{2,1,0:T(2,128)}, u32[]{:S(2)}, u32[]{:S(2)}) async-start(f32[4,2,1024]{2,1,0:T(2,128)} %broadcast_in_dim.16), calls=%async_computation.3 | async-start | bytes 65536 | tf_op jit(solution)/shard_map/all_to_all | solution.py:346
  77.9 15.7 %all-to-all-start.4 = ((f32[128,1,128]{2,1,0:T(1,128)}), f32[128,1,128]{2,1,0:T(1,128)S(1)}, u32[]{:S(2)}, u32[]{:S(2)}) async-start(f32[128,1,128]{2,1,0:T(1,128)} %bitcast.121), calls=%async_computation.4 | async-start | bytes 131072 | tf_op jit(solution)/shard_map/all_to_all | solution.py:412
  127.6 42.3 %copy-start.4 = (bf16[2,512,256]{2,1,0:T(8,128)(2,1)S(1)}, bf16[2,512,256]{2,1,0:T(8,128)(2,1)}, u32[]{:S(2)}) copy-start(bf16[2,512,256]{2,1,0:T(8,128)(2,1)} %second_ref.3) | copy-start | bytes 1572868
  153.1 16.9 %all-to-all-start.5 = ((f32[128,1,128]{2,1,0:T(1,128)}), f32[128,1,128]{2,1,0:T(1,128)}, u32[]{:S(2)}, u32[]{:S(2)}) async-start(f32[128,1,128]{2,1,0:T(1,128)} %bitcast.119), calls=%async_computation.5 | async-start | bytes 131072 | tf_op jit(solution)/shard_map/all_to_all | solution.py:360
  178.5 3.6 %collective-permute-start.2 = (f32[64,8,512]{2,1,0:T(8,128)S(1)}, f32[64,8,512]{2,1,0:T(8,128)S(1)}, u32[]{:S(2)}, u32[]{:S(2)}) collective-permute-start(f32[64,8,512]{2,1,0:T(8,128)S(1)} %get-tuple-element.40), channel_id=1, source_target_pairs={{0,1},{1,0},{2,3},{3,2},{4,5},{5,4},{6,7},{7,6},{8,9},{9,8},{10,11... | collective-permute-start | bytes 3145736 | tf_op jit(solution)/shard_map/ppermute | solution.py:340
  179.8 2.3 collective-permute-start.1
  183.6 29.4 %all-to-all-start.6 = ((f32[64,8,768]{2,1,0:T(8,128)}), f32[64,8,768]{2,1,0:T(8,128)}, u32[]{:S(2)}, u32[]{:S(2)}) async-start(f32[64,8,768]{2,1,0:T(8,128)} %pad_maximum_fusion), calls=%async_computation.6 | async-start | bytes 3145728 | tf_op jit(solution)/shard_map/all_to_all | solution.py:360
  189.1 23.9 %copy-start.7 = (f32[128,1024]{1,0:T(8,128)S(1)}, f32[128,1024]{1,0:T(8,128)}, u32[]{:S(2)}) copy-start(f32[128,1024]{1,0:T(8,128)} %copy-done.5) | copy-start | bytes 1572868
  189.1 23.9 %copy-start.8 = (bf16[128,1024]{1,0:T(8,128)(2,1)S(1)}, bf16[128,1024]{1,0:T(8,128)(2,1)}, u32[]{:S(2)}) copy-start(bf16[128,1024]{1,0:T(8,128)(2,1)} %tokens_ref.1) | copy-start | bytes 786436
  216.6 4.9 %collective-permute-start.3 = (f32[64,8,1024]{2,1,0:T(8,128)S(1)}, f32[64,8,1024]{2,1,0:T(8,128)S(1)}, u32[]{:S(2)}, u32[]{:S(2)}) collective-permute-start(f32[64,8,1024]{2,1,0:T(8,128)S(1)} %get-tuple-element.45), channel_id=1, source_target_pairs={{0,1},{1,0},{2,3},{3,2},{4,5},{5,4},{6,7},{7,6},{8,9},{9,8},{10,11... | collective-permute-start | bytes 6291464 | tf_op jit(solution)/shard_map/ppermute | solution.py:340
  224.2 36.0 %all-to-all-start.7 = ((bf16[64,8,1536]{2,1,0:T(8,128)(2,1)}), bf16[64,8,1536]{2,1,0:T(8,128)(2,1)}, u32[]{:S(2)}, u32[]{:S(2)}) async-start(bf16[64,8,1536]{2,1,0:T(8,128)(2,1)} %pad_maximum_fusion.1), calls=%async_computation.7 | async-start | bytes 3145728 | tf_op jit(solution)/shard_map/all_to_all | solution.py:360
  262.4 3.2 %collective-permute-start.4 = (bf16[64,8,512]{2,1,0:T(8,128)(2,1)S(1)}, bf16[64,8,512]{2,1,0:T(8,128)(2,1)S(1)}, u32[]{:S(2)}, u32[]{:S(2)}) collective-permute-start(bf16[64,8,512]{2,1,0:T(8,128)(2,1)S(1)} %get-tuple-element.51.mine_ref), channel_id=1, source_target_pairs={{0,1},{1,0},{2,3},{3,2},{4,5},{5,4},{6,7},{7,6},{8,9},{9,8},{10,11... | collective-permute-start | bytes 1572872 | tf_op jit(solution)/shard_map/ppermute | solution.py:340
  (21 other events, 34.2 us)
Sparse Core Ops, SparseCore 0:
  11.6 111.7 all-gather.1

commit v4 on v3

--- a/solution.py
+++ b/solution.py
@@ -31,8 +31,9 @@
     return lines
 
 
-def slots_kernel(heads, top, shard_ref, code_ref, place_ref, pos_ref, dense_ref, slot_ref):
-    n = shard_ref.shape[0]
+def slots_kernel(heads, top, id_ref, place_ref, pos_ref, dense_ref, slot_ref):
+    n = id_ref.shape[0]
+    codes = heads * top
     offset = place_ref[0]
     lane = iota((n, LANES), 1)
     row = iota((n, LANES), 0)
@@ -43,7 +44,8 @@
         code = jnp.full((n, LANES), -1, I32)
         for k in range(top):
             at = h * top + k
-            code = jnp.where(shard_ref[:, at : at + 1] == lane, code_ref[:, at : at + 1], code)
+            shard, own = id_ref[:, at : at + 1], id_ref[:, codes + at : codes + at + 1]
+            code = jnp.where(shard == lane, own, code)
         hit = code >= 0
         ones = jnp.where(hit, 1.0, 0.0)
         place = jnp.dot(below, ones.astype(BF16), preferred_element_type=F32) + before
@@ -67,7 +69,7 @@
 
 def score_kernel(
     heads, half, raw_ref, stat_ref, gain_ref, shift_ref, first_ref, second_ref, pos_ref, dense_ref,
-    query_ref, normed_ref, weight_ref, slot_ref,
+    query_ref, normed_ref, state_ref, slot_ref,
 ):
     n = raw_ref.shape[0]
     normed = (raw_ref[...] - stat_ref[0:1, :]) * stat_ref[1:2, :]
@@ -100,8 +102,10 @@
         most = jnp.max(score, axis=1, keepdims=True)
         power = jnp.where(hit, jnp.exp(score - most), 0.0)
         weight = power / jnp.sum(power, axis=1, keepdims=True)
-        weight_ref[h * n : (h + 1) * n, :] = weight
         pos.append(pos_ref[h * n : (h + 1) * n, :])
+        state_ref[3 * h * n : (3 * h + 1) * n, :] = pos[h]
+        state_ref[(3 * h + 1) * n : (3 * h + 2) * n, :] = weight
+        state_ref[(3 * h + 2) * n : (3 * h + 3) * n, :] = code.astype(F32)
         weights.append(weight)
     slot_ref[...] = jnp.concatenate(slot_table(pos, weights), axis=0).T
 
@@ -186,7 +190,7 @@
 
 
 def late_kernel(
-    senders, row_ref, token_ref, weight_ref, grad_ref, early_ref, after_ref, out_ref, done_ref, total, sem
+    senders, steps, row_ref, token_ref, weight_ref, grad_ref, early_ref, after_ref, out_ref, done_ref, total, sem
 ):
     step = pl.program_id(0)
     done_ref[...] = jnp.zeros((8, LANES), F32)
@@ -197,20 +201,25 @@
         copy.start()
         copy.wait()
 
-    add_messages(senders + step * GROUP, row_ref, token_ref, weight_ref, grad_ref, total)
-
-    @pl.when(step == pl.num_programs(0) - 1)
+    @pl.when(step < steps)
     def _():
+        add_messages(senders + step * GROUP, row_ref, token_ref, weight_ref, grad_ref, total)
+
+    @pl.when(step >= steps)
+    def _():
+        lines = out_ref.shape[0]
+        first = (step - steps) * lines * 8
+
         def emit(i, carry):
             for u in range(4):
                 at = pl.multiple_of(i * 64 + u * 16, 16)
                 for c in range(8):
                     out_ref[pl.ds(at, 16), c * LANES : (c + 1) * LANES] = total[
-                        pl.ds(at * 8 + c, 16, stride=8), :
+                        pl.ds(first + at * 8 + c, 16, stride=8), :
                     ].astype(BF16)
             return carry
 
-        lax.fori_loop(0, out_ref.shape[0] // 64, emit, 0)
+        lax.fori_loop(0, lines // 64, emit, 0)
 
 
 def split(value):
@@ -219,7 +228,7 @@
 
 
 def back_kernel(
-    heads, top, half, back_ref, shard_ref, second_ids_ref, pos_ref, dense_ref, weight_ref, query_ref,
+    heads, top, half, back_ref, id_ref, state_ref, query_ref,
     normed_ref, first_ref, second_ref, core_ref, grad_ref, own_ref, other_ref, sum_ref, held,
 ):
     n = query_ref.shape[0]
@@ -227,24 +236,24 @@
     table = back_ref[...].T
     wide = iota((n, 4 * LANES), 1)
     for h in range(heads):
-        pos = pos_ref[h * n : (h + 1) * n, :]
+        pos = state_ref[3 * h * n : (3 * h + 1) * n, :]
         product = jnp.zeros((n, LANES), F32)
         for j in range(CAP):
             product = jnp.where(pos == j, table[j : j + 1, :], product)
-        weight = weight_ref[h * n : (h + 1) * n, :]
+        weight = state_ref[(3 * h + 1) * n : (3 * h + 2) * n, :]
         score = product - weight * jnp.sum(product, axis=1, keepdims=True)
-        code = dense_ref[h * n : (h + 1) * n, :]
+        code = state_ref[(3 * h + 2) * n : (3 * h + 3) * n, :].astype(I32)
         low = code >> 9
         near_dense = jnp.concatenate([jnp.where(low == part, score, 0.0) for part in range(4)], axis=1)
         shards = jnp.concatenate(
-            [shard_ref[:, h * top : (h + 1) * top], jnp.zeros((n, LANES - top), I32)], axis=1
+            [id_ref[:, h * top : (h + 1) * top], jnp.zeros((n, LANES - top), I32)], axis=1
         )
         picked = jnp.take_along_axis(score, shards, axis=1)
         far_dense = jnp.zeros((n, 4 * LANES), F32)
         for k in range(top):
-            at = h * top + k
+            at = (heads + h) * top + k
             far_dense = far_dense + jnp.where(
-                second_ids_ref[:, at : at + 1] == wide, picked[:, k : k + 1], 0.0
+                (id_ref[:, at : at + 1] & 511) == wide, picked[:, k : k + 1], 0.0
             )
         base = h * 2 * half
         for side, dense, keys in ((0, near_dense, first_ref), (1, far_dense, second_ref)):
@@ -385,6 +394,7 @@
     shard_ids = pick_shard.reshape(n, heads * top)
     second_ids = pick_second.reshape(n, heads * top)
     code = pick_low.reshape(n, heads * top) * subkeys + second_ids
+    ids = jnp.concatenate([shard_ids, code], axis=1)
     vmem = pl.BlockSpec(memory_space=pltpu.VMEM)
     smem = pl.BlockSpec(memory_space=pltpu.SMEM)
     hbm = pl.BlockSpec(memory_space=pltpu.HBM)
@@ -392,18 +402,18 @@
     pos, dense, slot_index = call(
         functools.partial(slots_kernel, heads, top),
         (shape((heads * n, LANES), F32), shape((heads * n, LANES), I32), shape((devices, LANES), I32)),
-        in_specs=[vmem, vmem, smem],
-    )(shard_ids, code, place)
+        in_specs=[vmem, smem],
+    )(ids, place)
     slot_index = lax.all_to_all(slot_index.reshape(devices, 1, LANES), ALL, split_axis=0, concat_axis=0, tiled=True)
 
     first_split = first_keys.reshape(heads, devices, subkeys // devices, half).swapaxes(1, 2)
     first_split = first_split.reshape(heads, subkeys, half)
-    query, normed, weight, slot_weight = call(
+    query, normed, state, slot_weight = call(
         functools.partial(score_kernel, heads, half),
         (
             shape((n, width), BF16),
             shape((n, width), F32),
-            shape((heads * n, LANES), F32),
+            shape((3 * heads * n, LANES), F32),
             shape((devices, LANES), F32),
         ),
     )(
@@ -438,17 +448,17 @@
             shape((chips, 8, 2 * half), F32),
             shape((8, half), F32),
         ),
-        in_specs=[vmem] * 10 + [smem],
+        in_specs=[vmem] * 7 + [smem],
         scratch_shapes=[pltpu.VMEM((chips, 2, 8, 2 * half), F32)],
     )(
-        returned.reshape(devices, LANES), shard_ids, second_ids, pos, dense, weight, query, normed,
+        returned.reshape(devices, LANES), ids, state, query, normed,
         first_split, second_keys, core,
     )
     keys_in, sums_in = swap_core((other_keys, sums))
     sums = jnp.broadcast_to((sums + sums_in)[None], (chips, 8, half))
     sent = jnp.concatenate([sums, own_keys + keys_in], axis=2)
     arrived = exchange(sent, CHIPS)
-    steps = 10
+    steps = 9
     rest = devices // GROUP - steps
     early, early_done = call(
         early_kernel,
@@ -479,20 +489,21 @@
     sent = jnp.concatenate([own_part, key_wide], axis=2)
     arrived = exchange(sent, CHIPS)
     token_grad = lax.dot_general(raw_grad, query_weight, NT, preferred_element_type=F32).astype(BF16)
+    lines = 512
     value_grad, late_done = call(
-        functools.partial(late_kernel, steps * GROUP),
+        functools.partial(late_kernel, steps * GROUP, rest),
         (shape((rows, width), BF16), shape((8, LANES), F32)),
         limit=50,
-        grid=(rest,),
+        grid=(rest + rows // lines,),
         in_specs=[
             smem,
             smem,
             smem,
-            pl.BlockSpec((GROUP * n, 8, width // 8), lambda i: (i + steps, 0, 0)),
+            pl.BlockSpec((GROUP * n, 8, width // 8), lambda i: (jnp.minimum(i, rest - 1) + steps, 0, 0)),
             hbm,
             vmem,
         ],
-        out_specs=[vmem, vmem],
+        out_specs=[pl.BlockSpec((lines, width), lambda i: (jnp.maximum(i - rest, 0), 0)), vmem],
         scratch_shapes=[pltpu.VMEM(((rows + CAP) * 8, LANES), F32), pltpu.SemaphoreType.DMA],
     )(row_table, token_table, weight_table, all_grad, early, other_part[0, :, :LANES])
 

time: 276 us -> 267 us (0.967)
  blocking collectives: 0 us -> 16.5 us
  starting transfers between devices: 57.5 us -> 48.5 us
  waiting for transfers between devices: 68.4 us -> 60.5 us
  local copies, waits for them, and re-layouts: 41.3 us -> 33.8 us
    all_to_all x0 -> x1, blocking collectives: none -> 16.5 us  [exchange(): return lax.all_to_all(value, axis, split_axis=0, concat_axis=0, tiled=True)]
    all_to_all x3 -> x2, starting transfers between devices: 23.9 us -> 14.7 us  [exchange(): return lax.all_to_all(value, axis, split_axis=0, concat_axis=0, tiled=True)]
    all_to_all x3 -> x2, waiting for transfers between devices: 7.73 us -> 0.01 us  [exchange(): return lax.all_to_all(value, axis, split_axis=0, concat_axis=0, tiled=True)]
    unnamed x64 -> x54, local copies, waits for them, and re-layouts: 33.6 us -> 27.6 us
  transfers between devices with their start and end apart: 14 -> 13, of which waited for: 9 -> 8; matrix products, arithmetic and copies ran while one was open for 9% -> 9% of each run, Pallas kernels for 17% -> 17%
where the time goes in v4:
time: 267 us; the launch traced here: 265 us
  Pallas kernels  80.7 us (30%)
  waiting for transfers between devices  60.5 us (23%)
  starting transfers between devices  48.5 us (18%)
  local copies, waits for them, and re-layouts  33.8 us (13%)
  blocking collectives  16.5 us (6%)
  between operations  14.5 us (5%)
  other arithmetic  7.7 us (3%)
  matrix products  2.99 us (1%)
    all_gather x1, waiting for transfers between devices, per_device(): all_grad = lax.all_gather(tiles, ALL, axis=0, tiled=True)  29.3 us
    unnamed x54, local copies, waits for them, and re-layouts  27.6 us
    pallas_call x1, Pallas kernels, per_device(): call(product_kernel, shape((devices, LANES), F32), limit=28, grid=(device...  24.8 us
    pallas_call x1, Pallas kernels, per_device(): call(functools.partial(late_kernel, steps * GROUP, rest), (shape((rows, w...  24.8 us
    pallas_call x1, Pallas kernels, per_device(): call(early_kernel, (shape(((rows + CAP) * 8, LANES), F32), shape((8, LANE...  17.3 us
    all_to_all x1, blocking collectives, exchange(): return lax.all_to_all(value, axis, split_axis=0, concat_axis=0, tiled=True)  16.5 us
    all_to_all x2, starting transfers between devices, exchange(): return lax.all_to_all(value, axis, split_axis=0, concat_axis=0, tiled=True)  14.7 us
    all_to_all x3, starting transfers between devices, everyone(): return lax.all_to_all(wide, axis, split_axis=0, concat_axis=0, tiled=True)  13.2 us
  transfers between devices with their start and end apart: 13, of which 8 were waited for; matrix products, arithmetic and copies ran while one was open for 9% of the time, Pallas kernels for 17%

profile of v4, /device:TPU:1, one launch (start us, length us, event | category | flops | bytes accessed | tf_op | source)
XLA Modules:
  0.0 265.2 jit_solution(16129699518495388900)
XLA Ops:
  13.7 4.3 %all-to-all-start.1 = ((f32[4,2,1024]{2,1,0:T(2,128)}), f32[4,2,1024]{2,1,0:T(2,128)S(1)}, u32[]{:S(2)}, u32[]{:S(2)}) async-start(f32[4,2,1024]{2,1,0:T(2,128)} %broadcast_in_dim.14), calls=%async_computation.1 | async-start | bytes 65536 | tf_op jit(solution)/shard_map/all_to_all | solution.py:355
  18.2 4.1 %all-to-all-done.1 = f32[4,2,1024]{2,1,0:T(2,128)S(1)} async-done(((f32[4,2,1024]{2,1,0:T(2,128)}), f32[4,2,1024]{2,1,0:T(2,128)S(1)}, u32[]{:S(2)}, u32[]{:S(2)}) %all-to-all-start.1) | async-done | bytes 32800 | tf_op jit(solution)/shard_map/all_to_all | solution.py:355
  23.0 5.0 %all-to-all-start.2 = ((f32[4,2,1024]{2,1,0:T(2,128)}), f32[4,2,1024]{2,1,0:T(2,128)S(1)}, u32[]{:S(2)}, u32[]{:S(2)}) async-start(f32[4,2,1024]{2,1,0:T(2,128)} %broadcast_in_dim.15), calls=%async_computation.2 | async-start | bytes 65536 | tf_op jit(solution)/shard_map/all_to_all | solution.py:355
  30.2 9.0 %copy.75 = bf16[512,8,8,128]{3,2,1,0:T(8,128)(2,1)} copy(bf16[512,8,8,128]{3,1,2,0:T(8,128)(2,1)} %bitcast.122) | data formatting | bytes 16777216
  39.3 2.6 shard_map.162
  42.6 9.5 %all-to-all-start = ((s32[128,1,128]{2,1,0:T(1,128)}), s32[128,1,128]{2,1,0:T(1,128)S(1)}, u32[]{:S(2)}, u32[]{:S(2)}) async-start(s32[128,1,128]{2,1,0:T(1,128)} %bitcast.4), calls=%async_computation | async-start | bytes 131072 | tf_op jit(solution)/shard_map/all_to_all | solution.py:407
  53.6 7.9 %all-to-all-done = s32[128,1,128]{2,1,0:T(1,128)S(1)} async-done(((s32[128,1,128]{2,1,0:T(1,128)}), s32[128,1,128]{2,1,0:T(1,128)S(1)}, u32[]{:S(2)}, u32[]{:S(2)}) %all-to-all-start) | async-done | bytes 65568 | tf_op jit(solution)/shard_map/all_to_all | solution.py:407
  62.8 3.9 %all-to-all-start.3 = ((f32[4,2,1024]{2,1,0:T(2,128)}), f32[4,2,1024]{2,1,0:T(2,128)}, u32[]{:S(2)}, u32[]{:S(2)}) async-start(f32[4,2,1024]{2,1,0:T(2,128)} %broadcast_in_dim.16), calls=%async_computation.3 | async-start | bytes 65536 | tf_op jit(solution)/shard_map/all_to_all | solution.py:355
  67.6 3.5 %all-to-all-done.3 = f32[4,2,1024]{2,1,0:T(2,128)} async-done(((f32[4,2,1024]{2,1,0:T(2,128)}), f32[4,2,1024]{2,1,0:T(2,128)}, u32[]{:S(2)}, u32[]{:S(2)}) %all-to-all-start.3) | async-done | bytes 32800 | tf_op jit(solution)/shard_map/all_to_all | solution.py:355
  78.6 5.9 %all-to-all-start.4 = ((f32[128,1,128]{2,1,0:T(1,128)}), f32[128,1,128]{2,1,0:T(1,128)S(1)}, u32[]{:S(2)}, u32[]{:S(2)}) async-start(f32[128,1,128]{2,1,0:T(1,128)} %bitcast.118), calls=%async_computation.4 | async-start | bytes 131072 | tf_op jit(solution)/shard_map/all_to_all | solution.py:422
  85.3 8.9 %all-to-all-done.4 = f32[128,1,128]{2,1,0:T(1,128)S(1)} async-done(((f32[128,1,128]{2,1,0:T(1,128)}), f32[128,1,128]{2,1,0:T(1,128)S(1)}, u32[]{:S(2)}, u32[]{:S(2)}) %all-to-all-start.4) | async-done | bytes 65568 | tf_op jit(solution)/shard_map/all_to_all | solution.py:422
  94.2 29.3 %all-gather.2.cloned.1.call-done.grad_ref = bf16[16384,8,128]{2,1,0:T(8,128)(2,1)} async-done(((bf16[128,8,128]{2,1,0:T(8,128)(2,1)}), bf16[16384,8,128]{2,1,0:T(8,128)(2,1)}) %all-gather.2.cloned.1.call-update) | async-done | bytes 33554448 | tf_op jit(solution)/shard_map/all_gather | solution.py:385
  123.5 3.4 %copy-done.1 = bf16[512,8,8,128]{3,2,1,0:T(8,128)(2,1)S(1)} copy-done((bf16[512,8,8,128]{3,2,1,0:T(8,128)(2,1)S(1)}, bf16[512,8,8,128]{3,2,1,0:T(8,128)(2,1)}, u32[]{:S(2)}) %copy-start.1) | copy-done | bytes 8388632
  126.9 24.8 %shard_map.164 = f32[128,128]{1,0:T(8,128)S(1)} custom-call(s32[128,128]{1,0:T(8,128)S(1)} %broadcast_and_fusion.row_ref, s32[128,128]{1,0:T(8,128)S(1)} %get-tuple-element.58.token_ref, f32[128,128]{1,0:T(8,128)S(1)} %bitcast.113, bf16[16384,8,128]{2,1,0:T(8,128)(2,1)} %all-gather.2.cloned.1.call-done.grad_ref, bf16[4096,8,128]{2,1,0:T(8,128)(2,1)S(1)} %bitcast.110), custom_call_target="tpu_custom_call" | custom-call | tf_op jit(solution)/shard_map/pallas_call | solution.py:430
  151.7 16.5 %all_to_all.40 = f32[128,1,128]{2,1,0:T(1,128)S(1)} all-to-all(f32[128,1,128]{2,1,0:T(1,128)S(1)} %bitcast.116), channel_id=1, replica_groups=mesh['x'=4,'z'=4,'y'=4,'c'=2] {'x','z','y','c'}, dimensions={0} | all-to-all | bytes 131072 | tf_op jit(solution)/shard_map/all_to_all | solution.py:369
  168.3 3.0 %shard_map.165 = (f32[128,1024]{1,0:T(8,128)S(1)}, f32[64,8,512]{2,1,0:T(8,128)S(1)}, f32[64,8,512]{2,1,0:T(8,128)S(1)}, f32[8,256]{1,0:T(8,128)S(1)}) custom-call(f32[128,128]{1,0:T(8,128)S(1)} %bitcast.117, s32[128,64]{1,0:T(8,128)S(1)} %pad_add_fusion.id_ref, f32[768,128]{1,0:T(8,128)S(1)} %copy-done.11, bf16[128,1024]{1,0:T(8,128)(2,1)S(1)} %copy-done.13, ...), custom_call_target="tpu_custom_call" | custom-call | tf_op jit(solution)/shard_map/pallas_call | solution.py:443
  176.1 5.5 %all-to-all-start.6 = ((f32[64,8,768]{2,1,0:T(8,128)}), f32[64,8,768]{2,1,0:T(8,128)}, u32[]{:S(2)}, u32[]{:S(2)}) async-start(f32[64,8,768]{2,1,0:T(8,128)} %pad_maximum_fusion), calls=%async_computation.6 | async-start | bytes 3145728 | tf_op jit(solution)/shard_map/all_to_all | solution.py:369
  181.7 17.3 %shard_map.166 = (f32[33088,128]{1,0:T(8,128)S(1)}, f32[8,128]{1,0:T(8,128)S(1)}) custom-call(s32[128,128]{1,0:T(8,128)S(1)} %get-tuple-element.57.row_ref, s32[128,128]{1,0:T(8,128)S(1)} %get-tuple-element.58.token_ref, f32[128,128]{1,0:T(8,128)S(1)} %bitcast.114, bf16[16384,8,128]{2,1,0:T(8,128)(2,1)} %all-gather.2.cloned.1.call-done.grad_ref, ...), custom_call_target="tpu_custom_call" | custom-call | tf_op jit(solution)/shard_map/pallas_call | solution.py:463
  199.0 5.8 %copy-done.2 = f32[33088,128]{1,0:T(8,128)} copy-done((f32[33088,128]{1,0:T(8,128)}, f32[33088,128]{1,0:T(8,128)S(1)}, u32[]{:S(2)}) %copy-start.2) | copy-done | bytes 16941080
  205.8 2.5 shard_map.167
  210.3 3.8 %collective-permute-done.3 = f32[64,8,1024]{2,1,0:T(8,128)S(1)} collective-permute-done((f32[64,8,1024]{2,1,0:T(8,128)S(1)}, f32[64,8,1024]{2,1,0:T(8,128)S(1)}, u32[]{:S(2)}, u32[]{:S(2)}) %collective-permute-start.3) | collective-permute-done | bytes 2097184 | tf_op jit(solution)/shard_map/ppermute | solution.py:349
  216.7 9.2 %all-to-all-start.7 = ((bf16[64,8,1536]{2,1,0:T(8,128)(2,1)}), bf16[64,8,1536]{2,1,0:T(8,128)(2,1)}, u32[]{:S(2)}, u32[]{:S(2)}) async-start(bf16[64,8,1536]{2,1,0:T(8,128)(2,1)} %pad_maximum_fusion.1), calls=%async_computation.7 | async-start | bytes 3145728 | tf_op jit(solution)/shard_map/all_to_all | solution.py:369
  226.6 24.8 %shard_map.168 = (bf16[4096,1024]{1,0:T(8,128)(2,1)}, f32[8,128]{1,0:T(8,128)S(1)}) custom-call(s32[128,128]{1,0:T(8,128)S(1)} %get-tuple-element.57.row_ref, s32[128,128]{1,0:T(8,128)S(1)} %get-tuple-element.58.token_ref, f32[128,128]{1,0:T(8,128)S(1)} %bitcast.115, bf16[16384,8,128]{2,1,0:T(8,128)(2,1)} %all-gather.2.cloned.1.call-done.grad_ref, ...), custom_call_target="tpu_custom_call" | custom-call | tf_op jit(solution)/shard_map/pallas_call | solution.py:493
  251.4 2.2 shard_map.169
  (112 shorter events, 37.9 us)
Async XLA Ops:
  7.2 116.3 %all-gather.2.cloned.1.call-start = ((), (), s32[]{:S(2)}) async-start(), calls=%async_computation.8 | async-start | bytes 33816576 | tf_op jit(solution)/shard_map/all_gather | solution.py:385
  9.1 8.9 %copy-start.24 = (s32[128,2,16]{0,2,1:T(8,128)S(1)}, s32[128,2,16]{0,2,1:T(8,128)}, u32[]{:S(2)}) copy-start(s32[128,2,16]{0,2,1:T(8,128)} %param.20) | copy-start | bytes 49156
  9.1 9.1 %copy-start.25 = (s32[128,2,16]{0,2,1:T(8,128)S(1)}, s32[128,2,16]{0,2,1:T(8,128)}, u32[]{:S(2)}) copy-start(s32[128,2,16]{0,2,1:T(8,128)} %param.19) | copy-start | bytes 49156
  9.1 19.1 %copy-start.21 = (bf16[2,512,256]{2,1,0:T(8,128)(2,1)S(1)}, bf16[2,512,256]{2,1,0:T(8,128)(2,1)}, u32[]{:S(2)}) copy-start(bf16[2,512,256]{2,1,0:T(8,128)(2,1)} %param.16) | copy-start | bytes 1572868
  10.7 2.3 collective-permute-start
  13.7 8.6 %all-to-all-start.1 = ((f32[4,2,1024]{2,1,0:T(2,128)}), f32[4,2,1024]{2,1,0:T(2,128)S(1)}, u32[]{:S(2)}, u32[]{:S(2)}) async-start(f32[4,2,1024]{2,1,0:T(2,128)} %broadcast_in_dim.14), calls=%async_computation.1 | async-start | bytes 65536 | tf_op jit(solution)/shard_map/all_to_all | solution.py:355
  23.0 18.9 %all-to-all-start.2 = ((f32[4,2,1024]{2,1,0:T(2,128)}), f32[4,2,1024]{2,1,0:T(2,128)S(1)}, u32[]{:S(2)}, u32[]{:S(2)}) async-start(f32[4,2,1024]{2,1,0:T(2,128)} %broadcast_in_dim.15), calls=%async_computation.2 | async-start | bytes 65536 | tf_op jit(solution)/shard_map/all_to_all | solution.py:355
  30.2 41.8 %copy-start.17 = (f32[1024]{0:T(1024)S(1)}, f32[1024]{0:T(1024)}, u32[]{:S(2)}) copy-start(f32[1024]{0:T(1024)} %param.14) | copy-start | bytes 12292
  30.2 41.8 %copy-start.18 = (f32[1024]{0:T(1024)S(1)}, f32[1024]{0:T(1024)}, u32[]{:S(2)}) copy-start(f32[1024]{0:T(1024)} %param.15) | copy-start | bytes 12292
  41.9 24.8 %copy-start.14 = (s32[256,128]{1,0:T(8,128)}, s32[256,128]{1,0:T(8,128)S(1)}, u32[]{:S(2)}) copy-start(s32[256,128]{1,0:T(8,128)S(1)} %get-tuple-element.33.dense_ref) | copy-start | bytes 393220
  42.6 18.9 %all-to-all-start = ((s32[128,1,128]{2,1,0:T(1,128)}), s32[128,1,128]{2,1,0:T(1,128)S(1)}, u32[]{:S(2)}, u32[]{:S(2)}) async-start(s32[128,1,128]{2,1,0:T(1,128)} %bitcast.4), calls=%async_computation | async-start | bytes 131072 | tf_op jit(solution)/shard_map/all_to_all | solution.py:407
  62.8 8.2 %all-to-all-start.3 = ((f32[4,2,1024]{2,1,0:T(2,128)}), f32[4,2,1024]{2,1,0:T(2,128)}, u32[]{:S(2)}, u32[]{:S(2)}) async-start(f32[4,2,1024]{2,1,0:T(2,128)} %broadcast_in_dim.16), calls=%async_computation.3 | async-start | bytes 65536 | tf_op jit(solution)/shard_map/all_to_all | solution.py:355
  78.6 15.7 %all-to-all-start.4 = ((f32[128,1,128]{2,1,0:T(1,128)}), f32[128,1,128]{2,1,0:T(1,128)S(1)}, u32[]{:S(2)}, u32[]{:S(2)}) async-start(f32[128,1,128]{2,1,0:T(1,128)} %bitcast.118), calls=%async_computation.4 | async-start | bytes 131072 | tf_op jit(solution)/shard_map/all_to_all | solution.py:422
  126.9 41.4 %copy-start.4 = (bf16[2,512,256]{2,1,0:T(8,128)(2,1)S(1)}, bf16[2,512,256]{2,1,0:T(8,128)(2,1)}, u32[]{:S(2)}) copy-start(bf16[2,512,256]{2,1,0:T(8,128)(2,1)} %second_ref.3) | copy-start | bytes 1572868
  126.9 41.4 %copy-start.6 = (f32[128,1024]{1,0:T(8,128)S(1)}, f32[128,1024]{1,0:T(8,128)}, u32[]{:S(2)}) copy-start(f32[128,1024]{1,0:T(8,128)} %copy-done.5) | copy-start | bytes 1572868
  126.9 41.4 %copy-start.11 = (f32[768,128]{1,0:T(8,128)S(1)}, f32[768,128]{1,0:T(8,128)}, u32[]{:S(2)}) copy-start(f32[768,128]{1,0:T(8,128)} %copy-done.10) | copy-start | bytes 1179652
  126.9 41.4 %copy-start.13 = (bf16[128,1024]{1,0:T(8,128)(2,1)S(1)}, bf16[128,1024]{1,0:T(8,128)(2,1)}, u32[]{:S(2)}) copy-start(bf16[128,1024]{1,0:T(8,128)(2,1)} %copy-done.12) | copy-start | bytes 786436
  171.3 3.3 %collective-permute-start.2 = (f32[64,8,512]{2,1,0:T(8,128)S(1)}, f32[64,8,512]{2,1,0:T(8,128)S(1)}, u32[]{:S(2)}, u32[]{:S(2)}) collective-permute-start(f32[64,8,512]{2,1,0:T(8,128)S(1)} %get-tuple-element.40), channel_id=1, source_target_pairs={{0,1},{1,0},{2,3},{3,2},{4,5},{5,4},{6,7},{7,6},{8,9},{9,8},{10,11... | collective-permute-start | bytes 3145736 | tf_op jit(solution)/shard_map/ppermute | solution.py:349
  172.3 2.3 collective-permute-start.1
  176.1 28.6 %all-to-all-start.6 = ((f32[64,8,768]{2,1,0:T(8,128)}), f32[64,8,768]{2,1,0:T(8,128)}, u32[]{:S(2)}, u32[]{:S(2)}) async-start(f32[64,8,768]{2,1,0:T(8,128)} %pad_maximum_fusion), calls=%async_computation.6 | async-start | bytes 3145728 | tf_op jit(solution)/shard_map/all_to_all | solution.py:369
  181.6 23.1 %copy-start.7 = (bf16[128,1024]{1,0:T(8,128)(2,1)S(1)}, bf16[128,1024]{1,0:T(8,128)(2,1)}, u32[]{:S(2)}) copy-start(bf16[128,1024]{1,0:T(8,128)(2,1)} %tokens_ref.1) | copy-start | bytes 786436
  208.3 5.7 %collective-permute-start.3 = (f32[64,8,1024]{2,1,0:T(8,128)S(1)}, f32[64,8,1024]{2,1,0:T(8,128)S(1)}, u32[]{:S(2)}, u32[]{:S(2)}) collective-permute-start(f32[64,8,1024]{2,1,0:T(8,128)S(1)} %get-tuple-element.45), channel_id=1, source_target_pairs={{0,1},{1,0},{2,3},{3,2},{4,5},{5,4},{6,7},{7,6},{8,9},{9,8},{10,11... | collective-permute-start | bytes 6291464 | tf_op jit(solution)/shard_map/ppermute | solution.py:349
  216.7 34.7 %all-to-all-start.7 = ((bf16[64,8,1536]{2,1,0:T(8,128)(2,1)}), bf16[64,8,1536]{2,1,0:T(8,128)(2,1)}, u32[]{:S(2)}, u32[]{:S(2)}) async-start(bf16[64,8,1536]{2,1,0:T(8,128)(2,1)} %pad_maximum_fusion.1), calls=%async_computation.7 | async-start | bytes 3145728 | tf_op jit(solution)/shard_map/all_to_all | solution.py:369
  253.6 2.9 %collective-permute-start.4 = (bf16[64,8,512]{2,1,0:T(8,128)(2,1)S(1)}, bf16[64,8,512]{2,1,0:T(8,128)(2,1)S(1)}, u32[]{:S(2)}, u32[]{:S(2)}) collective-permute-start(bf16[64,8,512]{2,1,0:T(8,128)(2,1)S(1)} %get-tuple-element.51.mine_ref), channel_id=1, source_target_pairs={{0,1},{1,0},{2,3},{3,2},{4,5},{5,4},{6,7},{7,6},{8,9},{9,8},{10,11... | collective-permute-start | bytes 1572872 | tf_op jit(solution)/shard_map/ppermute | solution.py:349
  (15 other events, 36.8 us)
Sparse Core Ops, SparseCore 0:
  11.6 111.8 all-gather.1

commit v5 on v4

--- a/solution.py
+++ b/solution.py
@@ -458,7 +458,7 @@
     sums = jnp.broadcast_to((sums + sums_in)[None], (chips, 8, half))
     sent = jnp.concatenate([sums, own_keys + keys_in], axis=2)
     arrived = exchange(sent, CHIPS)
-    steps = 9
+    steps = 10
     rest = devices // GROUP - steps
     early, early_done = call(
         early_kernel,
@@ -505,7 +505,7 @@
         ],
         out_specs=[pl.BlockSpec((lines, width), lambda i: (jnp.maximum(i - rest, 0), 0)), vmem],
         scratch_shapes=[pltpu.VMEM(((rows + CAP) * 8, LANES), F32), pltpu.SemaphoreType.DMA],
-    )(row_table, token_table, weight_table, all_grad, early, other_part[0, :, :LANES])
+    )(row_table, token_table, weight_table, all_grad, early, key_wide[0, :, :LANES])
 
     query_weight_grad, mine = call(
         sum_kernel,

time: 267 us -> 266 us (level)
    unnamed x54 -> x52, local copies, waits for them, and re-layouts: 27.6 us -> 26.8 us
  transfers between devices with their start and end apart: 13 -> 13, of which waited for: 8 -> 8; matrix products, arithmetic and copies ran while one was open for 9% -> 8% of each run, Pallas kernels for 17% -> 18%
where the time goes in v5:
time: 266 us; the launch traced here: 264 us
  Pallas kernels  81.2 us (31%)
  waiting for transfers between devices  60.6 us (23%)
  starting transfers between devices  48.4 us (18%)
  local copies, waits for them, and re-layouts  32.2 us (12%)
  blocking collectives  16.5 us (6%)
  between operations  14.5 us (5%)
  other arithmetic  7.68 us (3%)
  matrix products  3 us (1%)
    all_gather x1, waiting for transfers between devices, per_device(): all_grad = lax.all_gather(tiles, ALL, axis=0, tiled=True)  29.3 us
    unnamed x52, local copies, waits for them, and re-layouts  26.8 us
    pallas_call x1, Pallas kernels, per_device(): call(product_kernel, shape((devices, LANES), F32), limit=28, grid=(device...  24.8 us
    pallas_call x1, Pallas kernels, per_device(): call(functools.partial(late_kernel, steps * GROUP, rest), (shape((rows, w...  24.5 us
    pallas_call x1, Pallas kernels, per_device(): call(early_kernel, (shape(((rows + CAP) * 8, LANES), F32), shape((8, LANE...  18.2 us
    all_to_all x1, blocking collectives, exchange(): return lax.all_to_all(value, axis, split_axis=0, concat_axis=0, tiled=True)  16.5 us
    all_to_all x2, starting transfers between devices, exchange(): return lax.all_to_all(value, axis, split_axis=0, concat_axis=0, tiled=True)  15.7 us
    all_to_all x3, starting transfers between devices, everyone(): return lax.all_to_all(wide, axis, split_axis=0, concat_axis=0, tiled=True)  13.2 us
  transfers between devices with their start and end apart: 13, of which 8 were waited for; matrix products, arithmetic and copies ran while one was open for 8% of the time, Pallas kernels for 18%

profile of v5, /device:TPU:1, one launch (start us, length us, event | category | flops | bytes accessed | tf_op | source)
XLA Modules:
  0.0 264.1 jit_solution(11582779532721410008)
XLA Ops:
  13.7 4.3 %all-to-all-start.1 = ((f32[4,2,1024]{2,1,0:T(2,128)}), f32[4,2,1024]{2,1,0:T(2,128)S(1)}, u32[]{:S(2)}, u32[]{:S(2)}) async-start(f32[4,2,1024]{2,1,0:T(2,128)} %broadcast_in_dim.14), calls=%async_computation.1 | async-start | bytes 65536 | tf_op jit(solution)/shard_map/all_to_all | solution.py:355
  18.2 4.1 %all-to-all-done.1 = f32[4,2,1024]{2,1,0:T(2,128)S(1)} async-done(((f32[4,2,1024]{2,1,0:T(2,128)}), f32[4,2,1024]{2,1,0:T(2,128)S(1)}, u32[]{:S(2)}, u32[]{:S(2)}) %all-to-all-start.1) | async-done | bytes 32800 | tf_op jit(solution)/shard_map/all_to_all | solution.py:355
  23.0 5.0 %all-to-all-start.2 = ((f32[4,2,1024]{2,1,0:T(2,128)}), f32[4,2,1024]{2,1,0:T(2,128)S(1)}, u32[]{:S(2)}, u32[]{:S(2)}) async-start(f32[4,2,1024]{2,1,0:T(2,128)} %broadcast_in_dim.15), calls=%async_computation.2 | async-start | bytes 65536 | tf_op jit(solution)/shard_map/all_to_all | solution.py:355
  30.2 9.0 %copy.75 = bf16[512,8,8,128]{3,2,1,0:T(8,128)(2,1)} copy(bf16[512,8,8,128]{3,1,2,0:T(8,128)(2,1)} %bitcast.120) | data formatting | bytes 16777216
  39.3 2.6 shard_map.162
  42.6 9.5 %all-to-all-start = ((s32[128,1,128]{2,1,0:T(1,128)}), s32[128,1,128]{2,1,0:T(1,128)S(1)}, u32[]{:S(2)}, u32[]{:S(2)}) async-start(s32[128,1,128]{2,1,0:T(1,128)} %bitcast.4), calls=%async_computation | async-start | bytes 131072 | tf_op jit(solution)/shard_map/all_to_all | solution.py:407
  53.6 8.0 %all-to-all-done = s32[128,1,128]{2,1,0:T(1,128)S(1)} async-done(((s32[128,1,128]{2,1,0:T(1,128)}), s32[128,1,128]{2,1,0:T(1,128)S(1)}, u32[]{:S(2)}, u32[]{:S(2)}) %all-to-all-start) | async-done | bytes 65568 | tf_op jit(solution)/shard_map/all_to_all | solution.py:407
  62.9 3.9 %all-to-all-start.3 = ((f32[4,2,1024]{2,1,0:T(2,128)}), f32[4,2,1024]{2,1,0:T(2,128)}, u32[]{:S(2)}, u32[]{:S(2)}) async-start(f32[4,2,1024]{2,1,0:T(2,128)} %broadcast_in_dim.16), calls=%async_computation.3 | async-start | bytes 65536 | tf_op jit(solution)/shard_map/all_to_all | solution.py:355
  67.6 3.5 %all-to-all-done.3 = f32[4,2,1024]{2,1,0:T(2,128)} async-done(((f32[4,2,1024]{2,1,0:T(2,128)}), f32[4,2,1024]{2,1,0:T(2,128)}, u32[]{:S(2)}, u32[]{:S(2)}) %all-to-all-start.3) | async-done | bytes 32800 | tf_op jit(solution)/shard_map/all_to_all | solution.py:355
  78.5 5.9 %all-to-all-start.4 = ((f32[128,1,128]{2,1,0:T(1,128)}), f32[128,1,128]{2,1,0:T(1,128)S(1)}, u32[]{:S(2)}, u32[]{:S(2)}) async-start(f32[128,1,128]{2,1,0:T(1,128)} %bitcast.116), calls=%async_computation.4 | async-start | bytes 131072 | tf_op jit(solution)/shard_map/all_to_all | solution.py:422
  85.3 8.9 %all-to-all-done.4 = f32[128,1,128]{2,1,0:T(1,128)S(1)} async-done(((f32[128,1,128]{2,1,0:T(1,128)}), f32[128,1,128]{2,1,0:T(1,128)S(1)}, u32[]{:S(2)}, u32[]{:S(2)}) %all-to-all-start.4) | async-done | bytes 65568 | tf_op jit(solution)/shard_map/all_to_all | solution.py:422
  94.2 29.3 %all-gather.2.cloned.1.call-done.grad_ref = bf16[16384,8,128]{2,1,0:T(8,128)(2,1)} async-done(((bf16[128,8,128]{2,1,0:T(8,128)(2,1)}), bf16[16384,8,128]{2,1,0:T(8,128)(2,1)}) %all-gather.2.cloned.1.call-update) | async-done | bytes 33554448 | tf_op jit(solution)/shard_map/all_gather | solution.py:385
  123.5 3.4 %copy-done.1 = bf16[512,8,8,128]{3,2,1,0:T(8,128)(2,1)S(1)} copy-done((bf16[512,8,8,128]{3,2,1,0:T(8,128)(2,1)S(1)}, bf16[512,8,8,128]{3,2,1,0:T(8,128)(2,1)}, u32[]{:S(2)}) %copy-start.1) | copy-done | bytes 8388632
  126.9 24.8 %shard_map.164 = f32[128,128]{1,0:T(8,128)S(1)} custom-call(s32[128,128]{1,0:T(8,128)S(1)} %broadcast_and_fusion.row_ref, s32[128,128]{1,0:T(8,128)S(1)} %get-tuple-element.58.token_ref, f32[128,128]{1,0:T(8,128)S(1)} %bitcast.111, bf16[16384,8,128]{2,1,0:T(8,128)(2,1)} %all-gather.2.cloned.1.call-done.grad_ref, bf16[4096,8,128]{2,1,0:T(8,128)(2,1)S(1)} %bitcast.108), custom_call_target="tpu_custom_call" | custom-call | tf_op jit(solution)/shard_map/pallas_call | solution.py:430
  151.7 16.5 %all_to_all.40 = f32[128,1,128]{2,1,0:T(1,128)S(1)} all-to-all(f32[128,1,128]{2,1,0:T(1,128)S(1)} %bitcast.114), channel_id=1, replica_groups=mesh['x'=4,'z'=4,'y'=4,'c'=2] {'x','z','y','c'}, dimensions={0} | all-to-all | bytes 131072 | tf_op jit(solution)/shard_map/all_to_all | solution.py:369
  168.3 3.0 %shard_map.165 = (f32[128,1024]{1,0:T(8,128)S(1)}, f32[64,8,512]{2,1,0:T(8,128)S(1)}, f32[64,8,512]{2,1,0:T(8,128)S(1)}, f32[8,256]{1,0:T(8,128)S(1)}) custom-call(f32[128,128]{1,0:T(8,128)S(1)} %bitcast.115, s32[128,64]{1,0:T(8,128)S(1)} %pad_add_fusion.id_ref, f32[768,128]{1,0:T(8,128)S(1)} %copy-done.11, bf16[128,1024]{1,0:T(8,128)(2,1)S(1)} %copy-done.13, ...), custom_call_target="tpu_custom_call" | custom-call | tf_op jit(solution)/shard_map/pallas_call | solution.py:443
  176.1 5.5 %all-to-all-start.6 = ((f32[64,8,768]{2,1,0:T(8,128)}), f32[64,8,768]{2,1,0:T(8,128)}, u32[]{:S(2)}, u32[]{:S(2)}) async-start(f32[64,8,768]{2,1,0:T(8,128)} %pad_maximum_fusion), calls=%async_computation.6 | async-start | bytes 3145728 | tf_op jit(solution)/shard_map/all_to_all | solution.py:369
  181.6 18.2 %shard_map.166 = (f32[33088,128]{1,0:T(8,128)S(1)}, f32[8,128]{1,0:T(8,128)S(1)}) custom-call(s32[128,128]{1,0:T(8,128)S(1)} %get-tuple-element.57.row_ref, s32[128,128]{1,0:T(8,128)S(1)} %get-tuple-element.58.token_ref, f32[128,128]{1,0:T(8,128)S(1)} %bitcast.112, bf16[16384,8,128]{2,1,0:T(8,128)(2,1)} %all-gather.2.cloned.1.call-done.grad_ref, ...), custom_call_target="tpu_custom_call" | custom-call | tf_op jit(solution)/shard_map/pallas_call | solution.py:463
  199.8 5.8 %copy-done.2 = f32[33088,128]{1,0:T(8,128)} copy-done((f32[33088,128]{1,0:T(8,128)}, f32[33088,128]{1,0:T(8,128)S(1)}, u32[]{:S(2)}) %copy-start.2) | copy-done | bytes 16941080
  206.7 2.5 shard_map.167
  210.3 3.8 %collective-permute-done.3 = f32[64,8,1024]{2,1,0:T(8,128)S(1)} collective-permute-done((f32[64,8,1024]{2,1,0:T(8,128)S(1)}, f32[64,8,1024]{2,1,0:T(8,128)S(1)}, u32[]{:S(2)}, u32[]{:S(2)}) %collective-permute-start.3) | collective-permute-done | bytes 2097184 | tf_op jit(solution)/shard_map/ppermute | solution.py:349
  215.9 10.2 %all-to-all-start.7 = ((bf16[64,8,1536]{2,1,0:T(8,128)(2,1)}), bf16[64,8,1536]{2,1,0:T(8,128)(2,1)}, u32[]{:S(2)}, u32[]{:S(2)}) async-start(bf16[64,8,1536]{2,1,0:T(8,128)(2,1)} %pad_maximum_fusion.1), calls=%async_computation.7 | async-start | bytes 3145728 | tf_op jit(solution)/shard_map/all_to_all | solution.py:369
  226.1 24.5 %shard_map.168 = (bf16[4096,1024]{1,0:T(8,128)(2,1)}, f32[8,128]{1,0:T(8,128)S(1)}) custom-call(s32[128,128]{1,0:T(8,128)S(1)} %get-tuple-element.57.row_ref, s32[128,128]{1,0:T(8,128)S(1)} %get-tuple-element.58.token_ref, f32[128,128]{1,0:T(8,128)S(1)} %bitcast.113, bf16[16384,8,128]{2,1,0:T(8,128)(2,1)} %all-gather.2.cloned.1.call-done.grad_ref, ...), custom_call_target="tpu_custom_call" | custom-call | tf_op jit(solution)/shard_map/pallas_call | solution.py:493
  250.6 2.2 shard_map.169
  (110 shorter events, 35.3 us)
Async XLA Ops:
  7.2 116.3 %all-gather.2.cloned.1.call-start = ((), (), s32[]{:S(2)}) async-start(), calls=%async_computation.8 | async-start | bytes 33816576 | tf_op jit(solution)/shard_map/all_gather | solution.py:385
  9.1 8.9 %copy-start.23 = (s32[128,2,16]{0,2,1:T(8,128)S(1)}, s32[128,2,16]{0,2,1:T(8,128)}, u32[]{:S(2)}) copy-start(s32[128,2,16]{0,2,1:T(8,128)} %param.20) | copy-start | bytes 49156
  9.1 9.1 %copy-start.24 = (s32[128,2,16]{0,2,1:T(8,128)S(1)}, s32[128,2,16]{0,2,1:T(8,128)}, u32[]{:S(2)}) copy-start(s32[128,2,16]{0,2,1:T(8,128)} %param.19) | copy-start | bytes 49156
  9.1 19.1 %copy-start.20 = (bf16[2,512,256]{2,1,0:T(8,128)(2,1)S(1)}, bf16[2,512,256]{2,1,0:T(8,128)(2,1)}, u32[]{:S(2)}) copy-start(bf16[2,512,256]{2,1,0:T(8,128)(2,1)} %param.16) | copy-start | bytes 1572868
  10.7 2.3 collective-permute-start
  13.7 8.6 %all-to-all-start.1 = ((f32[4,2,1024]{2,1,0:T(2,128)}), f32[4,2,1024]{2,1,0:T(2,128)S(1)}, u32[]{:S(2)}, u32[]{:S(2)}) async-start(f32[4,2,1024]{2,1,0:T(2,128)} %broadcast_in_dim.14), calls=%async_computation.1 | async-start | bytes 65536 | tf_op jit(solution)/shard_map/all_to_all | solution.py:355
  23.0 18.9 %all-to-all-start.2 = ((f32[4,2,1024]{2,1,0:T(2,128)}), f32[4,2,1024]{2,1,0:T(2,128)S(1)}, u32[]{:S(2)}, u32[]{:S(2)}) async-start(f32[4,2,1024]{2,1,0:T(2,128)} %broadcast_in_dim.15), calls=%async_computation.2 | async-start | bytes 65536 | tf_op jit(solution)/shard_map/all_to_all | solution.py:355
  30.2 41.8 %copy-start.17 = (f32[1024]{0:T(1024)S(1)}, f32[1024]{0:T(1024)}, u32[]{:S(2)}) copy-start(f32[1024]{0:T(1024)} %param.14) | copy-start | bytes 12292
  30.2 41.8 %copy-start.18 = (f32[1024]{0:T(1024)S(1)}, f32[1024]{0:T(1024)}, u32[]{:S(2)}) copy-start(f32[1024]{0:T(1024)} %param.15) | copy-start | bytes 12292
  41.9 24.8 %copy-start.14 = (s32[256,128]{1,0:T(8,128)}, s32[256,128]{1,0:T(8,128)S(1)}, u32[]{:S(2)}) copy-start(s32[256,128]{1,0:T(8,128)S(1)} %get-tuple-element.33.dense_ref) | copy-start | bytes 393220
  42.6 19.0 %all-to-all-start = ((s32[128,1,128]{2,1,0:T(1,128)}), s32[128,1,128]{2,1,0:T(1,128)S(1)}, u32[]{:S(2)}, u32[]{:S(2)}) async-start(s32[128,1,128]{2,1,0:T(1,128)} %bitcast.4), calls=%async_computation | async-start | bytes 131072 | tf_op jit(solution)/shard_map/all_to_all | solution.py:407
  62.9 8.2 %all-to-all-start.3 = ((f32[4,2,1024]{2,1,0:T(2,128)}), f32[4,2,1024]{2,1,0:T(2,128)}, u32[]{:S(2)}, u32[]{:S(2)}) async-start(f32[4,2,1024]{2,1,0:T(2,128)} %broadcast_in_dim.16), calls=%async_computation.3 | async-start | bytes 65536 | tf_op jit(solution)/shard_map/all_to_all | solution.py:355
  78.5 15.6 %all-to-all-start.4 = ((f32[128,1,128]{2,1,0:T(1,128)}), f32[128,1,128]{2,1,0:T(1,128)S(1)}, u32[]{:S(2)}, u32[]{:S(2)}) async-start(f32[128,1,128]{2,1,0:T(1,128)} %bitcast.116), calls=%async_computation.4 | async-start | bytes 131072 | tf_op jit(solution)/shard_map/all_to_all | solution.py:422
  126.9 41.4 %copy-start.4 = (bf16[2,512,256]{2,1,0:T(8,128)(2,1)S(1)}, bf16[2,512,256]{2,1,0:T(8,128)(2,1)}, u32[]{:S(2)}) copy-start(bf16[2,512,256]{2,1,0:T(8,128)(2,1)} %second_ref.3) | copy-start | bytes 1572868
  126.9 41.4 %copy-start.6 = (f32[128,1024]{1,0:T(8,128)S(1)}, f32[128,1024]{1,0:T(8,128)}, u32[]{:S(2)}) copy-start(f32[128,1024]{1,0:T(8,128)} %copy-done.5) | copy-start | bytes 1572868
  126.9 41.4 %copy-start.11 = (f32[768,128]{1,0:T(8,128)S(1)}, f32[768,128]{1,0:T(8,128)}, u32[]{:S(2)}) copy-start(f32[768,128]{1,0:T(8,128)} %copy-done.10) | copy-start | bytes 1179652
  126.9 41.4 %copy-start.13 = (bf16[128,1024]{1,0:T(8,128)(2,1)S(1)}, bf16[128,1024]{1,0:T(8,128)(2,1)}, u32[]{:S(2)}) copy-start(bf16[128,1024]{1,0:T(8,128)(2,1)} %copy-done.12) | copy-start | bytes 786436
  171.3 3.3 %collective-permute-start.2 = (f32[64,8,512]{2,1,0:T(8,128)S(1)}, f32[64,8,512]{2,1,0:T(8,128)S(1)}, u32[]{:S(2)}, u32[]{:S(2)}) collective-permute-start(f32[64,8,512]{2,1,0:T(8,128)S(1)} %get-tuple-element.40), channel_id=1, source_target_pairs={{0,1},{1,0},{2,3},{3,2},{4,5},{5,4},{6,7},{7,6},{8,9},{9,8},{10,11... | collective-permute-start | bytes 3145736 | tf_op jit(solution)/shard_map/ppermute | solution.py:349
  172.3 2.3 collective-permute-start.1
  176.1 29.5 %all-to-all-start.6 = ((f32[64,8,768]{2,1,0:T(8,128)}), f32[64,8,768]{2,1,0:T(8,128)}, u32[]{:S(2)}, u32[]{:S(2)}) async-start(f32[64,8,768]{2,1,0:T(8,128)} %pad_maximum_fusion), calls=%async_computation.6 | async-start | bytes 3145728 | tf_op jit(solution)/shard_map/all_to_all | solution.py:369
  181.6 24.0 %copy-start.7 = (bf16[128,1024]{1,0:T(8,128)(2,1)S(1)}, bf16[128,1024]{1,0:T(8,128)(2,1)}, u32[]{:S(2)}) copy-start(bf16[128,1024]{1,0:T(8,128)(2,1)} %tokens_ref.1) | copy-start | bytes 786436
  209.2 4.9 %collective-permute-start.3 = (f32[64,8,1024]{2,1,0:T(8,128)S(1)}, f32[64,8,1024]{2,1,0:T(8,128)S(1)}, u32[]{:S(2)}, u32[]{:S(2)}) collective-permute-start(f32[64,8,1024]{2,1,0:T(8,128)S(1)} %get-tuple-element.45), channel_id=1, source_target_pairs={{0,1},{1,0},{2,3},{3,2},{4,5},{5,4},{6,7},{7,6},{8,9},{9,8},{10,11... | collective-permute-start | bytes 6291464 | tf_op jit(solution)/shard_map/ppermute | solution.py:349
  215.9 34.7 %all-to-all-start.7 = ((bf16[64,8,1536]{2,1,0:T(8,128)(2,1)}), bf16[64,8,1536]{2,1,0:T(8,128)(2,1)}, u32[]{:S(2)}, u32[]{:S(2)}) async-start(bf16[64,8,1536]{2,1,0:T(8,128)(2,1)} %pad_maximum_fusion.1), calls=%async_computation.7 | async-start | bytes 3145728 | tf_op jit(solution)/shard_map/all_to_all | solution.py:369
  252.8 2.6 collective-permute-start.4
  (14 other events, 35.4 us)
Sparse Core Ops, SparseCore 0:
  11.6 111.8 all-gather.1
